TPU v7x, 256 devices: a whole 4x4x8 slice. The times are simulated.
256 devices in a mesh: row: 4 (over x_lo, core), col: 8 (over z), depth: 8 (over y, x_hi).
Axes of the slice: x: 4 (x_hi: 2, x_lo: 2; x = x_hi * 2 + x_lo), y: 4, z: 8, core: 2. Of those that a mesh axis runs over, the one named last changes fastest.
Arguments:
- inputs: bfloat16 [4096, 4096], P(('col', 'depth'), 'row'), may hold values from -6 to 6
- w_in: bfloat16 [4096, 16384], P('row', 'col'), may hold values from -0.09375 to 0.09375
- b_in: bfloat16 [16384], P('col'), may hold values from -4 to 4
- w_out: bfloat16 [16384, 4096], P('col', 'row'), may hold values from -0.046875 to 0.046875
- cotangent: bfloat16 [4096, 4096], P(('col', 'depth'), 'row'), may hold values from -6 to 6
Outputs:
- grad_inputs: bfloat16 [4096, 4096], P(('col', 'depth'), 'row')
- grad_w_in: float32 [4096, 16384], P(('row', 'depth'), 'col')
- grad_b_in: float32 [16384], P('col')
- grad_w_out: float32 [16384, 4096], P(('col', 'depth'), 'row')
- grad_b_out: float32 [4096], P('row')
All inputs are finite; a program needn't handle non-finite values.
Results may differ from a plain program's by a relative error of at most 0.007.
Values may be sent and summed in bfloat16 or wider, within the bound.
No kernel may reach another device: no remote copies, remote signals or barrier semaphores. Data moves between devices by JAX's collectives and lax.ppermute only.
A program may use at most 128 MiB of HBM per device.

v0:
```python
import math

import jax
import jax.numpy as jnp
from jax import lax
from jax.sharding import PartitionSpec as P

root_two_pi = 0.7978845608028654
cubic_coef = 0.044715


def gelu_pair(pre):
    inner = root_two_pi * (pre + cubic_coef * pre * pre * pre)
    tangent = jnp.tanh(inner)
    act = 0.5 * pre * (1.0 + tangent)
    slope = 0.5 * (1.0 + tangent) + 0.5 * pre * (1.0 - tangent * tangent) * root_two_pi * (
        1.0 + 3.0 * cubic_coef * pre * pre
    )
    return (act, slope)


def body(inputs, w_in, b_in, w_out, cotangent):
    depth_count = lax.axis_size("depth")
    total_tokens = inputs.shape[0] * lax.axis_size("col") * depth_count
    scale = 1.0 / math.sqrt(total_tokens)
    tok_all, cot_all = (
        lax.all_gather(inputs, "col", axis=0, tiled=True),
        lax.all_gather(cotangent, "col", axis=0, tiled=True),
    )
    pre_part = jnp.dot(tok_all, w_in, preferred_element_type=jnp.float32)
    grad_part = lax.dot_general(
        cot_all, w_out, (((1,), (1,)), ((), ())), preferred_element_type=jnp.float32
    )
    bias_wide = b_in.astype(jnp.float32)
    pre_sum, grad_sum = lax.psum((pre_part, grad_part), "row")
    act_full, slope_full = gelu_pair(pre_sum + bias_wide)
    pre_grad = (slope_full * grad_sum).astype(jnp.bfloat16)
    act_all = act_full.astype(jnp.bfloat16)
    bias_grad = lax.psum(jnp.sum(pre_grad, axis=0, dtype=jnp.float32), "depth")
    grad_inputs = lax.psum_scatter(
        lax.dot_general(
            pre_grad, w_in, (((1,), (1,)), ((), ())), preferred_element_type=jnp.float32
        ),
        "col",
        scatter_dimension=0,
        tiled=True,
    ).astype(jnp.bfloat16)
    grad_w_in = (
        lax.psum_scatter(
            lax.dot_general(
                tok_all, pre_grad, (((0,), (0,)), ((), ())), preferred_element_type=jnp.float32
            ),
            "depth",
            scatter_dimension=0,
            tiled=True,
        )
        * scale
    )
    grad_w_out = (
        lax.psum_scatter(
            lax.dot_general(
                act_all, cot_all, (((0,), (0,)), ((), ())), preferred_element_type=jnp.float32
            ),
            "depth",
            scatter_dimension=0,
            tiled=True,
        )
        * scale
    )
    bias_out = lax.psum(jnp.sum(cotangent, axis=0, dtype=jnp.float32), ("col", "depth"))
    return (grad_inputs, grad_w_in, bias_grad * scale, grad_w_out, bias_out * scale)


def solution(mesh):
    in_specs = (
        P(("col", "depth"), "row"),
        P("row", "col"),
        P("col"),
        P("col", "row"),
        P(("col", "depth"), "row"),
    )
    out_specs = (
        P(("col", "depth"), "row"),
        P(("row", "depth"), "col"),
        P("col"),
        P(("col", "depth"), "row"),
        P("row"),
    )
    return jax.shard_map(body, mesh=mesh, in_specs=in_specs, out_specs=out_specs, check_vma=False)
```

profile of v0, /device:TPU:32, one launch (start us, length us, event | category | flops | bytes accessed | tf_op | source)
XLA Modules:
  0.0 568.2 jit_solution(8674221787728095055)
XLA Ops:
  7.2 0.0 all-gather.3.cloned.1.call-start
  7.2 0.7 all-gather.3.cloned.1.call-update
  7.9 0.0 all-gather.5.cloned.1.call-start
  7.9 0.7 all-gather.5.cloned.1.call-update
  8.6 0.0 all-reduce.3.cloned.1.call-start
  8.7 41.7 %all-gather.3.cloned.1.call-done = bf16[512,1024]{1,0:T(8,128)(2,1)} async-done(((bf16[64,1024]{1,0:T(8,128)(2,1)}), bf16[512,1024]{1,0:T(8,128)(2,1)}) %all-gather.3.cloned.1.call-update) | async-done | bytes 1048592 | tf_op jit(solution)/shard_map/all_gather | solution.py:27
  50.4 6.8 %fusion.18 = f32[512,2048]{1,0:T(8,128)} fusion(bf16[512,1024]{1,0:T(8,128)(2,1)} %all-gather.3.cloned.1.call-done, bf16[1024,2048]{1,0:T(8,128)(2,1)} %param.6), kind=kOutput, calls=%fused_computation.27 | convolution fusion | flops 2147483648 | bytes 9437184 | tf_op jit(solution)/shard_map/dot_general | solution.py:30
  57.2 32.2 %all-gather.5.cloned.1.call-done = bf16[512,1024]{1,0:T(8,128)(2,1)} async-done(((bf16[64,1024]{1,0:T(8,128)(2,1)}), bf16[512,1024]{1,0:T(8,128)(2,1)}) %all-gather.5.cloned.1.call-update) | async-done | bytes 1048592 | tf_op jit(solution)/shard_map/all_gather | solution.py:28
  89.4 6.9 %fusion.19 = f32[512,2048]{1,0:T(8,128)} fusion(bf16[512,1024]{1,0:T(8,128)(2,1)} %all-gather.5.cloned.1.call-done, bf16[2048,1024]{1,0:T(8,128)(2,1)} %param.8), kind=kOutput, calls=%fused_computation.28 | convolution fusion | flops 2147483648 | bytes 9437184 | tf_op jit(solution)/shard_map/dot_general | solution.py:31
  96.3 0.0 copy-start.1
  96.3 0.0 all-reduce.3.cloned.1.call-update
  96.3 0.0 reduce-scatter.4.cloned.1.call-start
  96.4 0.6 copy-done.1
  97.0 163.0 %all-reduce.3.cloned.1.call-done = (f32[512,2048]{1,0:T(8,128)}, f32[512,2048]{1,0:T(8,128)}) async-done(((f32[512,2048]{1,0:T(8,128)}, f32[512,2048]{1,0:T(8,128)}), (f32[512,2048]{1,0:T(8,128)}, f32[512,2048]{1,0:T(8,128)})) %all-reduce.3.cloned.1.call-update) | async-done | bytes 8388624 | tf_op jit(solution)/shard_map/psum | solution.py:35
  260.0 0.0 copy-start.2
  260.0 5.4 convert_reduce_fusion
  265.4 0.0 copy-done.2
  265.4 0.0 copy-start.4
  265.4 3.7 fusion.20
  269.1 0.0 reduce-scatter.4.cloned.1.call-update
  269.1 0.0 reduce-scatter.6.cloned.1.call-start
  269.1 0.0 copy-done.4
  269.2 5.6 convolution_bitcast_fusion
  274.8 0.0 copy-start.3
  274.8 0.0 reduce-scatter.6.cloned.1.call-update
  274.8 0.2 reduce-scatter.8.cloned.1.call-start
  275.0 1.0 copy-done.3
  276.0 8.6 %fusion.7 = f32[2048,1024]{1,0:T(8,128)} fusion(bf16[512,1024]{1,0:T(8,128)(2,1)S(1)} %copy-done.3, f32[512,2048]{1,0:T(8,128)} %get-tuple-element.11, f32[2048]{0:T(1024)S(1)} %convert_element_type.18), kind=kOutput, calls=%fused_computation.12 | convolution fusion | flops 2157969408 | bytes 13639680 | tf_op jit(solution)/shard_map/dot_general | solution.py:61
  284.6 0.0 copy-start
  284.6 0.0 reduce-scatter.8.cloned.1.call-update
  284.6 0.9 copy-done
  285.6 171.0 %psum.31 = f32[1024]{0:T(1024)S(1)} all-reduce(f32[1024]{0:T(1024)S(1)} %convert_reduce_fusion.1), channel_id=1, replica_groups=mesh['row'=4,'col'=8,'depth'=8] {'col','depth'}, use_global_device_ids=true, to_apply=%region_8.0 | all-reduce | flops 1024 | bytes 8192 | tf_op jit(solution)/shard_map/psum | solution.py:70
  456.6 0.6 broadcast_multiply_fusion.3
  457.2 20.0 %psum.30 = f32[2048]{0:T(1024)S(1)} all-reduce(f32[2048]{0:T(1024)S(1)} %get-tuple-element.12), channel_id=1, replica_groups=mesh['row'=4,'col'=8,'depth'=8] {'depth'}, use_global_device_ids=true, to_apply=%region_5.0 | all-reduce | flops 2048 | bytes 16384 | tf_op jit(solution)/shard_map/psum | solution.py:39
  477.2 0.6 broadcast_multiply_fusion.2
  477.8 0.0 reduce-scatter.4.cloned.1.call-done
  477.8 1.6 convert_element_type.20
  479.5 0.0 reduce-scatter.6.cloned.1.call-done
  479.5 1.4 broadcast_multiply_fusion.1
  480.9 1.3 copy.10
  482.2 76.9 %reduce-scatter.8.cloned.1.call-done = f32[256,1024]{1,0:T(8,128)} async-done(((f32[2048,1024]{1,0:T(8,128)}), f32[256,1024]{1,0:T(8,128)}) %reduce-scatter.8.cloned.1.call-update) | async-done | bytes 1048592 | tf_op jit(solution)/shard_map/reduce_scatter | solution.py:60
  559.1 2.3 broadcast_multiply_fusion
  (2 shorter events, 0.0 us)
Async XLA Ops:
  7.2 43.3 %all-gather.3.cloned.1.call-start = ((), (), s32[]{:S(2)}) async-start(), calls=%async_computation.3 | async-start | bytes 1179648 | tf_op jit(solution)/shard_map/all_gather | solution.py:27
  7.9 81.5 %all-gather.5.cloned.1.call-start = ((), (), s32[]{:S(2)}) async-start(), calls=%async_computation.4 | async-start | bytes 1179648 | tf_op jit(solution)/shard_map/all_gather | solution.py:28
  8.6 251.4 %all-reduce.3.cloned.1.call-start = ((), (), s32[]{:S(2)}) async-start(), calls=%async_computation.8 | async-start | bytes 16777216 | tf_op jit(solution)/shard_map/psum | solution.py:35
  96.3 0.7 copy-start.1
  96.3 381.5 %reduce-scatter.4.cloned.1.call-start = ((), (), s32[]{:S(2)}) async-start(), calls=%async_computation.5 | async-start | bytes 2359296 | tf_op jit(solution)/shard_map/reduce_scatter | solution.py:40
  260.0 5.4 copy-start.2
  265.4 3.8 copy-start.4
  269.1 210.4 %reduce-scatter.6.cloned.1.call-start = ((), (), s32[]{:S(2)}) async-start(), calls=%async_computation.6 | async-start | bytes 9437184 | tf_op jit(solution)/shard_map/reduce_scatter | solution.py:49
  274.8 1.2 copy-start.3
  274.8 284.3 %reduce-scatter.8.cloned.1.call-start = ((), (), s32[]{:S(2)}) async-start(), calls=%async_computation.7 | async-start | bytes 9437184 | tf_op jit(solution)/shard_map/reduce_scatter | solution.py:60
  284.6 0.9 copy-start
Sparse Core Ops, SparseCore 0:
  9.8 40.5 all-gather.2
  52.2 37.1 all-gather.4
  96.5 163.5 all-reduce.2
  269.2 42.6 reduce-scatter.3
  315.9 120.8 reduce-scatter.5
  441.2 117.8 reduce-scatter.7
where the time goes:
time: 569 us; the launch traced here: 568 us
  waiting for transfers between devices  315 us (55%)
  blocking collectives  191 us (34%)
  matrix products  31.6 us (6%)
  between operations  14.2 us (2%)
  other arithmetic  11.9 us (2%)
    psum x1, blocking collectives, body(): lax.psum(jnp.sum(cotangent, axis=0, dtype=jnp.float32), ('col', 'depth'))  171 us
    psum x1, waiting for transfers between devices, body(): pre_sum, grad_sum = lax.psum((pre_part, grad_part), 'row')  163 us
    reduce_scatter x1, waiting for transfers between devices, body(): lax.psum_scatter(lax.dot_general(act_all, cot_all, (((0,), (0,)), ((), ()...  76.9 us
    all_gather x1, waiting for transfers between devices, body(): lax.all_gather(inputs, 'col', axis=0, tiled=True)  41.7 us
    all_gather x1, waiting for transfers between devices, body(): lax.all_gather(cotangent, 'col', axis=0, tiled=True)  32.2 us
    psum x1, blocking collectives, body(): bias_grad = lax.psum(jnp.sum(pre_grad, axis=0, dtype=jnp.float32), 'depth')  20 us
  transfers between devices with their start and end apart: 6, of which 4 were waited for; matrix products, arithmetic and copies ran while one was open for 5% of the time, Pallas kernels for 0%

commit v1 on v0

v1 whole, which is shorter than its diff:
```python
import math

import jax
import jax.numpy as jnp
from jax import lax
from jax.experimental import pallas as pl
from jax.experimental.pallas import tpu as pltpu
from jax.sharding import PartitionSpec as P

root_two_pi = 0.7978845608028654
cubic_coef = 0.044715

AXES = ("row", "col", "depth")
ROWS, COLS, DEPTHS = 4, 8, 8
BF, F32 = jnp.bfloat16, jnp.float32

ORDER = ((0, 1, 6, 7, 2, 3, 4, 5), (0, 1, 2, 3, 6, 7, 4, 5))


def gelu_pair(pre):
    inner = root_two_pi * (pre + cubic_coef * pre * pre * pre)
    tangent = jnp.tanh(inner)
    act = 0.5 * pre * (1.0 + tangent)
    slope = 0.5 * (1.0 + tangent) + 0.5 * pre * (1.0 - tangent * tangent) * root_two_pi * (
        1.0 + 3.0 * cubic_coef * pre * pre
    )
    return (act, slope)


def flat(x, y, z, core):
    row = (x % 2) * 2 + core
    depth = y * 2 + x // 2
    return (row * COLS + z) * DEPTHS + depth


def pairs_of(target):
    pairs = []
    for x in range(4):
        for y in range(4):
            for z in range(8):
                for core in range(2):
                    tx, ty, tz, tc = target(x, y, z, core)
                    pairs.append((flat(x, y, z, core), flat(tx % 4, ty % 4, tz % 8, tc % 2)))
    return pairs


CORE = pairs_of(lambda x, y, z, c: (x, y, z, c ^ 1))
SWAP = pairs_of(lambda x, y, z, c: (x if x % 2 else x + 2, y, z, c))
NEAR = {
    "a": pairs_of(lambda x, y, z, c: (x ^ 1, y, z, c)),
    "r": pairs_of(lambda x, y, z, c: (x + 1 if x % 2 else x - 1, y, z, c)),
}
Y_NEXT = pairs_of(lambda x, y, z, c: (x, y ^ 1, z, c))
Y_LAST = pairs_of(lambda x, y, z, c: (x, y ^ 3, z, c))
X_HI = pairs_of(lambda x, y, z, c: (x + 2, y, z, c))
Y_ONE = [pairs_of(lambda x, y, z, c, h=h: (x, y ^ (3 if c ^ h else 1), z, c)) for h in range(2)]
Y_TWO = [pairs_of(lambda x, y, z, c, h=h: (x, y ^ (1 if c ^ h else 3), z, c)) for h in range(2)]


def send(value, pairs):
    return lax.ppermute(value, AXES, pairs)


def dot(a, b):
    return jnp.dot(a, b, preferred_element_type=F32)


def dot_t(a, b):
    return lax.dot_general(a, b, (((1,), (1,)), ((), ())), preferred_element_type=F32)


def dot_tn(a, b):
    return lax.dot_general(a, b, (((0,), (0,)), ((), ())), preferred_element_type=F32)


def plain_of(i, at):
    return (i % 8) * 2 + (at[0] ^ (i // 8))


def order_of(i, core):
    packed = [sum(k << (4 * j) for j, k in enumerate(order)) for order in ORDER]
    return (jnp.where(core == 0, packed[0], packed[1]) >> (4 * i)) & 7


def place_of(i, at):
    h = i // 8
    return (order_of(i % 8, at[0] ^ h) ^ at[1]) * 2 + (at[0] ^ h)


ANY = pl.BlockSpec(memory_space=pl.ANY)
WHOLE = pl.BlockSpec(memory_space=pltpu.VMEM)
SCALARS = pl.BlockSpec(memory_space=pltpu.SMEM)


def permute_kernel(axis, orders, at_ref, a_ref, *refs):
    outs, sems = refs[:-1], refs[-1]
    copies = []
    for o, (order, out) in enumerate(zip(orders, outs)):
        for i in range(16):
            source = pl.ds(pl.multiple_of(order(i, at_ref) * 128, 128), 128)
            target = pl.ds(i * 128, 128)
            if axis == 1:
                source, target = (slice(None), source), (slice(None), target)
            copies.append(
                pltpu.make_async_copy(a_ref.at[source], out.at[target], sems.at[16 * o + i])
            )
    for copy in copies:
        copy.start()
    for copy in copies:
        copy.wait()


def permute(at, w, axis, orders):
    return pl.pallas_call(
        lambda *refs: permute_kernel(axis, orders, *refs),
        in_specs=[SCALARS, ANY],
        out_specs=[WHOLE] * len(orders),
        out_shape=[jax.ShapeDtypeStruct(w.shape, w.dtype)] * len(orders),
        scratch_shapes=[pltpu.SemaphoreType.DMA((16 * len(orders),))],
        cost_estimate=pl.CostEstimate(flops=0, bytes_accessed=1 << 16, transcendentals=0),
        name=f"permute_{axis}",
    )(at, w)


def arrange_kernel(a_ref, tok_out, cot_out):
    n = a_ref.shape[0] // 32
    for z in range(8):
        for g in range(2):
            for i, out in enumerate((tok_out, cot_out)):
                source = (z * 4 + i * 2 + g) * n
                target = (g * 8 + z) * n
                out[target : target + n, :] = a_ref[source : source + n, :]


def arrange(gathered):
    rows, cols = gathered.shape
    return pl.pallas_call(
        arrange_kernel,
        in_specs=[WHOLE],
        out_specs=[WHOLE] * 2,
        out_shape=[jax.ShapeDtypeStruct((rows // 2, cols), BF)] * 2,
        cost_estimate=pl.CostEstimate(flops=0, bytes_accessed=1 << 16, transcendentals=0),
        name="arrange",
    )(gathered)


def gelu_kernel(chip_ref, got_a, got_r, bias_ref, act_out, slope_out):
    half = got_a.shape[0]
    for g, got in enumerate((got_a, got_r)):

        @pl.loop(0, half, step=16)
        def _(i, g=g, got=got):
            i = pl.multiple_of(i, 16)
            rows = pl.ds(pl.multiple_of(g * half + i, 16), 16)
            pre = chip_ref[rows, :].astype(F32) + got[pl.ds(i, 16), :].astype(F32)
            act, slope = gelu_pair(pre + bias_ref[...])
            act_out[rows, :] = act.astype(BF)
            slope_out[rows, :] = slope


def gelu(chip, got, bias):
    return pl.pallas_call(
        gelu_kernel,
        in_specs=[WHOLE] * 4,
        out_specs=[WHOLE] * 2,
        out_shape=[jax.ShapeDtypeStruct(chip.shape, BF), jax.ShapeDtypeStruct(chip.shape, F32)],
        cost_estimate=pl.CostEstimate(flops=0, bytes_accessed=1 << 16, transcendentals=0),
        name="gelu",
    )(chip, *got, bias)


def pre_grad_kernel(at_ref, slope_ref, chip_ref, got_a, got_r, out_ref, sum_ref):
    half = got_a.shape[0]
    for b in range(8):
        here = slice(b * 128, b * 128 + 128)
        at = pl.multiple_of((order_of(b, at_ref[0]) ^ at_ref[1]) * 128, 128)
        there = pl.ds(at, 128)
        for g, got in enumerate((got_a, got_r)):
            rows = slice(g * half, g * half + half)
            grad = chip_ref[rows, here].astype(F32) + got[:, here].astype(F32)
            value = (slope_ref[rows, here] * grad).astype(BF)
            out_ref[rows, there] = value
            sum_ref[g : g + 1, there] = jnp.sum(value.astype(F32), axis=0, keepdims=True)


def pre_grad(at, slope, chip, got):
    return pl.pallas_call(
        pre_grad_kernel,
        in_specs=[SCALARS] + [WHOLE] * 4,
        out_specs=[WHOLE] * 2,
        out_shape=[
            jax.ShapeDtypeStruct(chip.shape, BF),
            jax.ShapeDtypeStruct((2, chip.shape[1]), F32),
        ],
        cost_estimate=pl.CostEstimate(flops=0, bytes_accessed=1 << 16, transcendentals=0),
        name="pre_grad",
    )(at, slope, chip, *got)


def by_depth_kernel(at_ref, a_ref, a_out):
    for i in range(8):
        at = pl.multiple_of((order_of(i, at_ref[0]) ^ at_ref[1]) * 128, 128)
        a_out[:, i * 128 : (i + 1) * 128] = a_ref[:, pl.ds(at, 128)]


def by_depth(at, a):
    return pl.pallas_call(
        by_depth_kernel,
        in_specs=[SCALARS, WHOLE],
        out_specs=WHOLE,
        out_shape=jax.ShapeDtypeStruct(a.shape, a.dtype),
        cost_estimate=pl.CostEstimate(flops=0, bytes_accessed=1 << 16, transcendentals=0),
        name="by_depth",
    )(at, a)


def bias_kernel(at_ref, b_ref, b_out):
    for i in range(8):
        at = pl.multiple_of(place_of(i, at_ref) * 128, 128)
        b_out[:, i * 128 : (i + 1) * 128] = b_ref[:, pl.ds(at, 128)].astype(F32)


def bias_mine(at, b):
    return pl.pallas_call(
        bias_kernel,
        in_specs=[SCALARS, WHOLE],
        out_specs=WHOLE,
        out_shape=jax.ShapeDtypeStruct((1, b.shape[0] // 2), F32),
        cost_estimate=pl.CostEstimate(flops=0, bytes_accessed=1 << 14, transcendentals=0),
        name="bias_mine",
    )(at, b.reshape(1, -1))


def place_kernel(scale, at_ref, keep_ref, got_ref, keep2_ref, got2_ref, out_ref):
    for h, (k, g) in enumerate(((keep_ref, got_ref), (keep2_ref, got2_ref))):
        for i in range(8):
            at = pl.multiple_of((2 * i + (at_ref[0] ^ h)) * 128, 128)
            cols = slice(i * 128, i * 128 + 128)
            out_ref[:, pl.ds(at, 128)] = (k[:, cols] + g[:, cols].astype(F32)) * scale


def place_columns(at, scale, keep, got, keep2, got2):
    rows, cols = keep.shape
    return pl.pallas_call(
        lambda *refs: place_kernel(scale, *refs),
        in_specs=[SCALARS] + [WHOLE] * 4,
        out_specs=WHOLE,
        out_shape=jax.ShapeDtypeStruct((rows, 2 * cols), F32),
        cost_estimate=pl.CostEstimate(flops=0, bytes_accessed=1 << 16, transcendentals=0),
        name="place_columns",
    )(at, keep, got, keep2, got2)


def after(value, *others):
    return lax.optimization_barrier((value, *others))[0]


class DepthSum:
    def __init__(self, left, right, h):
        self.left, self.right, self.h = left, right, h
        self.low = lax.axis_index("depth") % 2 == 0
        self.sent = dot_tn(left[:, 512:], right).astype(BF)
        self.one = send(self.sent, Y_ONE[h])

    def second(self):
        out = dot_tn(self.left[:, 256:512], self.right) + self.one[256:].astype(F32)
        self.two = send(out.astype(BF), Y_TWO[self.h])

    def part(self, first):
        def pick(a, axis):
            low, high = lax.slice_in_dim(a, 0, 128, axis=axis), lax.slice_in_dim(a, 128, 256, axis=axis)
            return jnp.where(first, low, high)

        total = dot_tn(pick(self.left, 1), self.right) + pick(self.one, 0).astype(F32)
        return total + pick(self.two, 0).astype(F32)

    def third(self):
        self.got = send(self.part(~self.low).astype(BF), X_HI)
        self.keep = self.part(self.low)


def body(inputs, w_in, b_in, w_out, cotangent):
    core = lax.axis_index("row") % 2
    z = lax.axis_index("col")
    depth = lax.axis_index("depth")
    near = depth - depth % 2
    total_tokens = inputs.shape[0] * COLS * DEPTHS
    scale = 1.0 / math.sqrt(total_tokens)

    at = jnp.stack([core, near, z]).astype(jnp.int32)

    n = inputs.shape[0] // 2
    width = w_in.shape[1] // 2
    group = 8 * n
    far = send(jnp.concatenate([inputs[n:], cotangent[n:]], axis=0), SWAP)
    gathered = jnp.concatenate([inputs[:n], far[:n], cotangent[:n], far[n:]], axis=0)
    gathered = lax.all_gather(gathered, "col", axis=0, tiled=True)
    bias = bias_mine(at, b_in)
    w_in, w_in_plain = permute(at, w_in, 1, (place_of, plain_of))
    (w_out,) = permute(at, w_out, 0, (place_of,))
    tok, cot = arrange(gathered)

    def row_sum(mine, other):
        got = send(other.astype(BF), CORE)
        chip = (mine + got.astype(F32)).astype(BF)
        return chip, [send(chip[:group], NEAR["a"]), send(chip[group:], NEAR["r"])]

    chip, got = row_sum(dot(tok, w_in[:, :width]), dot(tok, w_in[:, width:]))
    cot_then = after(cot, chip)
    chip_two, got_two = row_sum(dot_t(cot_then, w_out[:width]), dot_t(cot_then, w_out[width:]))
    act, slope = gelu(after(chip, chip_two), got, bias)
    act_away = send(act, CORE)
    outs = [DepthSum(act, cot, 0), DepthSum(act_away, cot, 1)]

    tok_perm = by_depth(at, after(tok, outs[0].sent))
    pg, db = pre_grad(at, slope, chip_two, got_two)
    pg_away = send(pg, CORE)
    ins = [DepthSum(tok_perm, pg, 0), DepthSum(tok_perm, pg_away, 0)]
    for part in outs + ins:
        part.second()
    for part in outs + ins:
        part.third()

    pg_then = after(pg, ins[1].sent)
    gi = dot_t(pg_then, w_in_plain[:, :width]) + dot_t(pg_away, w_in_plain[:, width:])
    gi = jnp.swapaxes(gi.reshape(2, 8, n, -1), 0, 1).reshape(16 * n, -1)
    gi = lax.psum_scatter(gi, "col", scatter_dimension=0, tiled=True).astype(BF)
    grad_inputs = jnp.concatenate([gi[:n], send(gi[n:], SWAP)], axis=0)

    db = after(jnp.concatenate([db, jnp.sum(cot, axis=0, dtype=F32)[None]], axis=0), ins[1].sent)
    db = db.reshape(24, 128)
    for pairs in (Y_NEXT, Y_LAST, X_HI):
        db = db + send(db, pairs)
    db = db * scale
    grad_b_out = db[16:].reshape(-1)
    db = db[:8] + db[8:16]
    db_other = send(db, CORE)
    first = jnp.where(core == 0, db, db_other)
    second = jnp.where(core == 0, db_other, db)
    grad_b_in = jnp.concatenate([first[:, None], second[:, None]], axis=1).reshape(-1)

    one, two = ((part.keep + part.got.astype(F32)) * scale for part in outs)
    grad_w_out = jnp.concatenate(
        [jnp.where(core == 0, one, two), jnp.where(core == 0, two, one)], axis=0
    )
    grad_w_in = place_columns(at, scale, ins[0].keep, ins[0].got, ins[1].keep, ins[1].got)
    return (grad_inputs, grad_w_in, grad_b_in, grad_w_out, grad_b_out)


def solution(mesh):
    in_specs = (
        P(("col", "depth"), "row"),
        P("row", "col"),
        P("col"),
        P("col", "row"),
        P(("col", "depth"), "row"),
    )
    out_specs = (
        P(("col", "depth"), "row"),
        P(("row", "depth"), "col"),
        P("col"),
        P(("col", "depth"), "row"),
        P("row"),
    )
    return jax.shard_map(body, mesh=mesh, in_specs=in_specs, out_specs=out_specs, check_vma=False)
```

time: 569 us -> 224 us (0.39)
  waiting for transfers between devices: 315 us -> 78.6 us
  blocking collectives: 191 us -> 0 us
  starting transfers between devices: 0.42 us -> 39.9 us
  Pallas kernels: 0 us -> 31.1 us
  matrix products: 31.6 us -> 45.9 us
  other arithmetic: 11.9 us -> 5.43 us
    psum x2 -> x0, blocking collectives: 191 us -> none  [the longest x1 171 us: body(): lax.psum(jnp.sum(cotangent, axis=0, dtype=jnp.float32), ('col', 'depth'))]
    psum x1 -> x0, waiting for transfers between devices: 163 us -> none  [body(): pre_sum, grad_sum = lax.psum((pre_part, grad_part), 'row')]
    reduce_scatter x3 -> x1, waiting for transfers between devices: 76.9 us -> 0.01 us  [body(): gi = lax.psum_scatter(gi, 'col', scatter_dimension=0, tiled=True).astype(BF)]
    ppermute x0 -> x26, waiting for transfers between devices: none -> 43.6 us  [send(): return lax.ppermute(value, AXES, pairs)]
    ppermute x0 -> x26, starting transfers between devices: none -> 39.8 us  [send(): return lax.ppermute(value, AXES, pairs)]
    all_gather x2 -> x1, waiting for transfers between devices: 73.9 us -> 35 us  [body(): gathered = lax.all_gather(gathered, 'col', axis=0, tiled=True)]
    pallas_call x0 -> x8, Pallas kernels: none -> 31.1 us  [the longest x2 13.1 us: permute(): pl.pallas_call(lambda *refs: permute_kernel(axis, orders, *refs), in_spec...]
    dot_general x5 -> x22, matrix products: 31.6 us -> 45.9 us  [the longest x16 31.2 us: dot_tn(): lax.dot_general(a, b, (((0,), (0,)), ((), ())), preferred_element_type=F32)]
  transfers between devices with their start and end apart: 6 -> 28, of which waited for: 4 -> 14; matrix products, arithmetic and copies ran while one was open for 5% -> 21% of each run, Pallas kernels for 0% -> 11%
where the time goes in v1:
time: 224 us; the launch traced here: 223 us
  waiting for transfers between devices  78.6 us (35%)
  matrix products  45.9 us (20%)
  starting transfers between devices  39.9 us (18%)
  Pallas kernels  31.1 us (14%)
  between operations  14.4 us (6%)
  local copies, waits for them, and re-layouts  7.32 us (3%)
  other arithmetic  5.43 us (2%)
    ppermute x26, waiting for transfers between devices, send(): return lax.ppermute(value, AXES, pairs)  43.6 us
    ppermute x26, starting transfers between devices, send(): return lax.ppermute(value, AXES, pairs)  39.8 us
    all_gather x1, waiting for transfers between devices, body(): gathered = lax.all_gather(gathered, 'col', axis=0, tiled=True)  35 us
    dot_general x16, matrix products, dot_tn(): lax.dot_general(a, b, (((0,), (0,)), ((), ())), preferred_element_type=F32)  31.2 us
    pallas_call x2, Pallas kernels, permute(): pl.pallas_call(lambda *refs: permute_kernel(axis, orders, *refs), in_spec...  13.1 us
    dot_general x4, matrix products, dot_t(): lax.dot_general(a, b, (((1,), (1,)), ((), ())), preferred_element_type=F32)  7.62 us
    dot_general x2, matrix products, dot(): return jnp.dot(a, b, preferred_element_type=F32)  7.14 us
    pallas_call x1, Pallas kernels, gelu(): pl.pallas_call(gelu_kernel, in_specs=[WHOLE] * 4, out_specs=[WHOLE] * 2,...  5.02 us
  transfers between devices with their start and end apart: 28, of which 14 were waited for; matrix products, arithmetic and copies ran while one was open for 21% of the time, Pallas kernels for 11%

profile of v1, /device:TPU:32, one launch (start us, length us, event | category | flops | bytes accessed | tf_op | source)
XLA Modules:
  0.0 222.6 jit_solution(10280800283450600902)
XLA Ops:
  8.2 4.9 %collective-permute-start = (bf16[64,1024]{1,0:T(8,128)(2,1)S(1)}, bf16[64,1024]{1,0:T(8,128)(2,1)S(1)}, u32[]{:S(2)}, u32[]{:S(2)}) collective-permute-start(bf16[64,1024]{1,0:T(8,128)(2,1)S(1)} %pad_maximum_fusion.2), channel_id=1, source_target_pairs={{0,1},{64,65},{8,9},{72,73},{16,17},{80,81},{24,25},{88,89},{32,33... | collective-permute-start | bytes 393224 | tf_op jit(solution)/shard_map/ppermute | solution.py:61
  13.1 3.7 %collective-permute-done = bf16[64,1024]{1,0:T(8,128)(2,1)S(1)} collective-permute-done((bf16[64,1024]{1,0:T(8,128)(2,1)S(1)}, bf16[64,1024]{1,0:T(8,128)(2,1)S(1)}, u32[]{:S(2)}, u32[]{:S(2)}) %collective-permute-start) | collective-permute-done | bytes 131104 | tf_op jit(solution)/shard_map/ppermute | solution.py:61
  18.3 7.9 %permute_1.1 = (bf16[1024,2048]{1,0:T(8,128)(2,1)}, bf16[1024,2048]{1,0:T(8,128)(2,1)}) custom-call(s32[3]{0:T(128)} %pad_add_fusion.refs_0_.at_ref, bf16[1024,2048]{1,0:T(8,128)(2,1)} %refs_1_.2), custom_call_target="tpu_custom_call" | custom-call | bytes 65536 | tf_op jit(solution)/shard_map/permute_1/pallas_call | solution.py:114
  26.2 35.0 %all-gather.2.cloned.1.call-done.a_ref = bf16[1024,1024]{1,0:T(8,128)(2,1)} async-done(((bf16[128,1024]{1,0:T(8,128)(2,1)}), bf16[1024,1024]{1,0:T(8,128)(2,1)}) %all-gather.2.cloned.1.call-update) | async-done | bytes 2097168 | tf_op jit(solution)/shard_map/all_gather | solution.py:297
  61.1 3.0 %arrange.1 = (bf16[512,1024]{1,0:T(8,128)(2,1)}, bf16[512,1024]{1,0:T(8,128)(2,1)}) custom-call(bf16[1024,1024]{1,0:T(8,128)(2,1)} %all-gather.2.cloned.1.call-done.a_ref), custom_call_target="tpu_custom_call" | custom-call | bytes 65536 | tf_op jit(solution)/shard_map/arrange/pallas_call | solution.py:137
  64.2 4.2 %fusion.15 = bf16[512,1024]{1,0:T(8,128)(2,1)} fusion(bf16[512,1024]{1,0:T(8,128)(2,1)} %get-tuple-element.26.a_ref, bf16[1024,2048]{1,0:T(8,128)(2,1)} %get-tuple-element.19), kind=kOutput, calls=%fused_computation.16 | convolution fusion | flops 1074266112 | bytes 4194304 | tf_op jit(solution)/shard_map/dot_general | solution.py:65
  68.3 5.2 %permute_0.1 = bf16[2048,1024]{1,0:T(8,128)(2,1)} custom-call(s32[3]{0:T(128)} %pad_add_fusion.refs_0_.at_ref, bf16[2048,1024]{1,0:T(8,128)(2,1)} %refs_1_.3), custom_call_target="tpu_custom_call" | custom-call | bytes 65536 | tf_op jit(solution)/shard_map/permute_0/pallas_call | solution.py:114
  73.5 3.0 %add_convert_fusion.1.chip_ref = bf16[512,1024]{1,0:T(8,128)(2,1)S(1)} fusion(bf16[512,1024]{1,0:T(8,128)(2,1)S(1)} %collective-permute-done.1, bf16[512,1024]{1,0:T(8,128)(2,1)S(1)} %copy-done.5, bf16[1024,2048]{1,0:T(8,128)(2,1)} %get-tuple-element.19), kind=kOutput, calls=%fused_computation.10 | convolution fusion | flops 1075314688 | bytes 5242880 | tf_op jit(solution)/shard_map/dot_general | solution.py:65
  79.4 1.5 collective-permute-start.3
  80.9 2.1 collective-permute-start.4
  88.6 5.9 %collective-permute-done.3.got_a = bf16[256,1024]{1,0:T(8,128)(2,1)} collective-permute-done((bf16[256,1024]{1,0:T(8,128)(2,1)}, bf16[256,1024]{1,0:T(8,128)(2,1)}, u32[]{:S(2)}, u32[]{:S(2)}) %collective-permute-start.3) | collective-permute-done | bytes 524320 | tf_op jit(solution)/shard_map/ppermute | solution.py:61
  94.5 2.7 %collective-permute-done.4.got_r = bf16[256,1024]{1,0:T(8,128)(2,1)} collective-permute-done((bf16[256,1024]{1,0:T(8,128)(2,1)}, bf16[256,1024]{1,0:T(8,128)(2,1)}, u32[]{:S(2)}, u32[]{:S(2)}) %collective-permute-start.4) | collective-permute-done | bytes 524320 | tf_op jit(solution)/shard_map/ppermute | solution.py:61
  97.2 5.0 %gelu.1 = (bf16[512,1024]{1,0:T(8,128)(2,1)}, f32[512,1024]{1,0:T(8,128)}) custom-call(bf16[512,1024]{1,0:T(8,128)(2,1)} %copy-done.2, bf16[256,1024]{1,0:T(8,128)(2,1)} %collective-permute-done.3.got_a, bf16[256,1024]{1,0:T(8,128)(2,1)} %collective-permute-done.4.got_r, f32[1,1024]{1,0:T(1,128)} %bias_mine.1.bias_ref), custom_call_target="tpu_custom_call" | custom-call | bytes 65536 | tf_op jit(solution)/shard_map/gelu/pallas_call | solution.py:162
  102.2 2.6 %collective-permute-done.5.got_a = bf16[256,1024]{1,0:T(8,128)(2,1)S(1)} collective-permute-done((bf16[256,1024]{1,0:T(8,128)(2,1)}, bf16[256,1024]{1,0:T(8,128)(2,1)S(1)}, u32[]{:S(2)}, u32[]{:S(2)}) %collective-permute-start.5) | collective-permute-done | bytes 524320 | tf_op jit(solution)/shard_map/ppermute | solution.py:61
  104.8 2.4 %collective-permute-done.6.got_r = bf16[256,1024]{1,0:T(8,128)(2,1)S(1)} collective-permute-done((bf16[256,1024]{1,0:T(8,128)(2,1)}, bf16[256,1024]{1,0:T(8,128)(2,1)S(1)}, u32[]{:S(2)}, u32[]{:S(2)}) %collective-permute-start.6) | collective-permute-done | bytes 524320 | tf_op jit(solution)/shard_map/ppermute | solution.py:61
  108.0 3.7 %pre_grad.1 = (bf16[512,1024]{1,0:T(8,128)(2,1)}, f32[2,1024]{1,0:T(2,128)}) custom-call(s32[3]{0:T(128)} %pad_add_fusion.refs_0_.at_ref, f32[512,1024]{1,0:T(8,128)} %get-tuple-element.23.slope_ref, bf16[512,1024]{1,0:T(8,128)(2,1)} %copy-done, bf16[256,1024]{1,0:T(8,128)(2,1)} %copy-done.6, bf16[256,1024]{1,0:T(8,128)(2,1)} %copy-done.7), custom_call_target="tpu_custom_call" | custom-call | bytes 65536 | tf_op jit(solution)/shard_map/pre_grad/pallas_call | solution.py:187
  112.5 2.7 %convolution_convert_fusion.3 = bf16[512,1024]{1,0:T(8,128)(2,1)} fusion(bf16[512,1024]{1,0:T(8,128)(2,1)S(1)} %copy-done.3, bf16[512,1024]{1,0:T(8,128)(2,1)} %get-tuple-element.25), kind=kOutput, calls=%fused_computation.21 | convolution fusion | flops 537395200 | bytes 2621440 | tf_op jit(solution)/shard_map/dot_general | solution.py:73
  115.2 1.5 collective-permute-start.19
  116.7 2.5 %by_depth.1 = bf16[512,1024]{1,0:T(8,128)(2,1)} custom-call(s32[3]{0:T(128)} %pad_add_fusion.refs_0_.at_ref, bf16[512,1024]{1,0:T(8,128)(2,1)} %get-tuple-element.26.a_ref), custom_call_target="tpu_custom_call" | custom-call | bytes 65536 | tf_op jit(solution)/shard_map/by_depth/pallas_call | solution.py:207
  119.2 3.2 %convolution_convert_fusion.1 = bf16[512,1024]{1,0:T(8,128)(2,1)} fusion(bf16[512,1024]{1,0:T(8,128)(2,1)} %get-tuple-element.27, bf16[512,1024]{1,0:T(8,128)(2,1)} %by_depth.1), kind=kOutput, calls=%fused_computation.19 | convolution fusion | flops 537395200 | bytes 2621440 | tf_op jit(solution)/shard_map/dot_general | solution.py:73
  123.0 2.9 %convolution_convert_fusion.2 = bf16[512,1024]{1,0:T(8,128)(2,1)} fusion(bf16[512,1024]{1,0:T(8,128)(2,1)} %collective-permute-done.7, bf16[512,1024]{1,0:T(8,128)(2,1)S(1)} %copy-done.4), kind=kOutput, calls=%fused_computation.20 | convolution fusion | flops 537395200 | bytes 2621440 | tf_op jit(solution)/shard_map/dot_general | solution.py:73
  125.9 2.5 %fusion.6 = f32[512,1024]{1,0:T(8,128)S(1)} fusion(bf16[512,1024]{1,0:T(8,128)(2,1)} %get-tuple-element.27, bf16[1024,2048]{1,0:T(8,128)(2,1)S(1)} %copy-done.12), kind=kOutput, calls=%fused_computation.7 | convolution fusion | flops 1073741824 | bytes 5242880 | tf_op jit(solution)/shard_map/dot_general | solution.py:69
  128.4 2.5 %fusion.12 = f32[512,1024]{1,0:T(8,128)S(1)} fusion(f32[512,1024]{1,0:T(8,128)S(1)} %fusion.6, bf16[512,1024]{1,0:T(8,128)(2,1)} %collective-permute-done.7, bf16[1024,2048]{1,0:T(8,128)(2,1)S(1)} %copy-done.12), kind=kOutput, calls=%fused_computation.15 | convolution fusion | flops 1074266112 | bytes 7340032 | tf_op jit(solution)/shard_map/dot_general | solution.py:69
  131.0 1.5 copy.11
  132.5 1.6 collective-permute-start.15
  134.1 1.8 convolution_convert_fusion
  135.8 2.2 collective-permute-start.23
  138.0 7.5 %collective-permute-done.15 = f32[24,128]{1,0:T(8,128)S(1)} collective-permute-done((f32[24,128]{1,0:T(8,128)S(1)}, f32[24,128]{1,0:T(8,128)S(1)}, u32[]{:S(2)}, u32[]{:S(2)}) %collective-permute-start.15) | collective-permute-done | bytes 12320 | tf_op jit(solution)/shard_map/ppermute | solution.py:61
  145.5 2.7 %collective-permute-start.16 = (f32[24,128]{1,0:T(8,128)S(1)}, f32[24,128]{1,0:T(8,128)S(1)}, u32[]{:S(2)}, u32[]{:S(2)}) collective-permute-start(f32[24,128]{1,0:T(8,128)S(1)} %add.115), channel_id=1, source_target_pairs={{0,6},{64,70},{8,14},{72,78},{16,22},{80,86},{24,30},{88,94},{32,3... | collective-permute-start | bytes 36872 | tf_op jit(solution)/shard_map/ppermute | solution.py:61
  150.5 11.5 %collective-permute-done.16 = f32[24,128]{1,0:T(8,128)S(1)} collective-permute-done((f32[24,128]{1,0:T(8,128)S(1)}, f32[24,128]{1,0:T(8,128)S(1)}, u32[]{:S(2)}, u32[]{:S(2)}) %collective-permute-start.16) | collective-permute-done | bytes 12320 | tf_op jit(solution)/shard_map/ppermute | solution.py:61
  161.9 1.5 collective-permute-start.17
  163.4 1.5 fusion.23
  164.9 3.8 %collective-permute-start.10 = (bf16[256,1024]{1,0:T(8,128)(2,1)S(1)}, bf16[256,1024]{1,0:T(8,128)(2,1)S(1)}, u32[]{:S(2)}, u32[]{:S(2)}) collective-permute-start(bf16[256,1024]{1,0:T(8,128)(2,1)S(1)} %fusion.23), channel_id=1, source_target_pairs={{0,6},{64,66},{8,14},{72,74},{16,22},{80,82},{24,30},{88,90},{32,3... | collective-permute-start | bytes 1572872 | tf_op jit(solution)/shard_map/ppermute | solution.py:61
  171.4 1.6 collective-permute-start.21
  175.9 2.1 fusion.42
  178.0 2.1 collective-permute-start.11
  180.0 2.2 fusion.27.refs_1_
  182.2 2.1 collective-permute-done.24
  185.6 2.1 collective-permute-start.25
  187.7 2.1 fusion.24
  189.8 2.8 %collective-permute-start.13 = (bf16[256,1024]{1,0:T(8,128)(2,1)S(1)}, bf16[256,1024]{1,0:T(8,128)(2,1)S(1)}, u32[]{:S(2)}, u32[]{:S(2)}) collective-permute-start(bf16[256,1024]{1,0:T(8,128)(2,1)S(1)} %fusion.24), channel_id=1, source_target_pairs={{0,6},{64,66},{8,14},{72,74},{16,22},{80,82},{24,30},{88,90},{32,3... | collective-permute-start | bytes 1572872 | tf_op jit(solution)/shard_map/ppermute | solution.py:61
  192.7 3.1 %collective-permute-done.25 = bf16[128,1024]{1,0:T(8,128)(2,1)S(1)} collective-permute-done((bf16[128,1024]{1,0:T(8,128)(2,1)S(1)}, bf16[128,1024]{1,0:T(8,128)(2,1)S(1)}, u32[]{:S(2)}, u32[]{:S(2)}) %collective-permute-start.25) | collective-permute-done | bytes 262176 | tf_op jit(solution)/shard_map/ppermute | solution.py:61
  197.2 1.4 broadcast_select_fusion.1
  200.3 1.8 fusion.41
  202.1 1.6 collective-permute-start.14
  204.7 3.9 %collective-permute-start.8 = (bf16[32,1024]{1,0:T(8,128)(2,1)S(1)}, bf16[32,1024]{1,0:T(8,128)(2,1)S(1)}, u32[]{:S(2)}, u32[]{:S(2)}) collective-permute-start(bf16[32,1024]{1,0:T(8,128)(2,1)S(1)} %get-tuple-element.38), channel_id=1, source_target_pairs={{0,1},{64,65},{8,9},{72,73},{16,17},{80,81},{24,25},{88,89},{32,33... | collective-permute-start | bytes 196616 | tf_op jit(solution)/shard_map/ppermute | solution.py:61
  208.6 2.7 %fusion.29.refs_3_ = f32[128,1024]{1,0:T(8,128)} fusion(bf16[512,1024]{1,0:T(8,128)(2,1)} %collective-permute-done.7, pred[]{:T(512)S(6)} %eq.19, bf16[256,1024]{1,0:T(8,128)(2,1)} %copy-done.16, bf16[512,1024]{1,0:T(8,128)(2,1)} %copy-done.14, bf16[512,1024]{1,0:T(8,128)(2,1)S(1)} %copy-done.4), kind=kOutput, calls=%fused_computation.40 | convolution fusion | flops 135069696 | bytes 2884608 | tf_op jit(solution)/shard_map/dot_general | solution.py:73
  212.7 2.5 %place_columns.1 = f32[128,2048]{1,0:T(8,128)} custom-call(s32[3]{0:T(128)} %pad_add_fusion.refs_0_.at_ref, f32[128,1024]{1,0:T(8,128)} %fusion.27.refs_1_, bf16[128,1024]{1,0:T(8,128)(2,1)} %copy-done.8, f32[128,1024]{1,0:T(8,128)} %fusion.29.refs_3_, bf16[128,1024]{1,0:T(8,128)(2,1)} %copy-done.9), custom_call_target="tpu_custom_call" | custom-call | bytes 65536 | tf_op jit(solution)/shard_map/place_columns/pallas_call | solution.py:244
  (96 shorter events, 28.3 us)
Async XLA Ops:
  7.2 54.0 %all-gather.2.cloned.1.call-start = ((), (), s32[]{:S(2)}) async-start(), calls=%async_computation.1 | async-start | bytes 2359296 | tf_op jit(solution)/shard_map/all_gather | solution.py:297
  8.2 8.6 %collective-permute-start = (bf16[64,1024]{1,0:T(8,128)(2,1)S(1)}, bf16[64,1024]{1,0:T(8,128)(2,1)S(1)}, u32[]{:S(2)}, u32[]{:S(2)}) collective-permute-start(bf16[64,1024]{1,0:T(8,128)(2,1)S(1)} %pad_maximum_fusion.2), channel_id=1, source_target_pairs={{0,1},{64,65},{8,9},{72,73},{16,17},{80,81},{24,25},{88,89},{32,33... | collective-permute-start | bytes 393224 | tf_op jit(solution)/shard_map/ppermute | solution.py:61
  17.6 186.1 %reduce-scatter.2.cloned.1.call-start = ((), (), s32[]{:S(2)}) async-start(), calls=%async_computation.2 | async-start | bytes 2359296 | tf_op jit(solution)/shard_map/reduce_scatter | solution.py:327
  68.3 5.2 %copy-start.5 = (bf16[512,1024]{1,0:T(8,128)(2,1)S(1)}, bf16[512,1024]{1,0:T(8,128)(2,1)}, u32[]{:S(2)}) copy-start(bf16[512,1024]{1,0:T(8,128)(2,1)} %get-tuple-element.26.a_ref) | copy-start | bytes 3145732
  68.3 5.2 %collective-permute-start.1 = (bf16[512,1024]{1,0:T(8,128)(2,1)}, bf16[512,1024]{1,0:T(8,128)(2,1)S(1)}, u32[]{:S(2)}, u32[]{:S(2)}) collective-permute-start(bf16[512,1024]{1,0:T(8,128)(2,1)} %fusion.15), channel_id=1, source_target_pairs={{0,64},{64,0},{8,72},{72,8},{16,80},{80,16},{24,88},{88,24},{32,96... | collective-permute-start | bytes 3145736 | tf_op jit(solution)/shard_map/ppermute | solution.py:61
  73.5 3.1 %copy-start.1 = (bf16[2048,1024]{1,0:T(8,128)(2,1)S(1)}, bf16[2048,1024]{1,0:T(8,128)(2,1)}, u32[]{:S(2)}) copy-start(bf16[2048,1024]{1,0:T(8,128)(2,1)} %permute_0.1) | copy-start | bytes 12582916
  73.5 3.1 %copy-start.3 = (bf16[512,1024]{1,0:T(8,128)(2,1)S(1)}, bf16[512,1024]{1,0:T(8,128)(2,1)}, u32[]{:S(2)}) copy-start(bf16[512,1024]{1,0:T(8,128)(2,1)} %get-tuple-element.21) | copy-start | bytes 3145732
  76.5 1.8 copy-start.2
  77.9 5.0 %collective-permute-start.2 = (bf16[512,1024]{1,0:T(8,128)(2,1)S(1)}, bf16[512,1024]{1,0:T(8,128)(2,1)S(1)}, u32[]{:S(2)}, u32[]{:S(2)}) collective-permute-start(bf16[512,1024]{1,0:T(8,128)(2,1)S(1)} %fusion.18), channel_id=1, source_target_pairs={{0,64},{64,0},{8,72},{72,8},{16,80},{80,16},{24,88},{88,24},{32,96... | collective-permute-start | bytes 3145736 | tf_op jit(solution)/shard_map/ppermute | solution.py:61
  79.4 15.1 %collective-permute-start.3 = (bf16[256,1024]{1,0:T(8,128)(2,1)}, bf16[256,1024]{1,0:T(8,128)(2,1)}, u32[]{:S(2)}, u32[]{:S(2)}) collective-permute-start(bf16[256,1024]{1,0:T(8,128)(2,1)} %get-tuple-element.36), channel_id=1, source_target_pairs={{0,128},{64,192},{8,136},{72,200},{16,144},{80,208},{24,152},{88,2... | collective-permute-start | bytes 1572872 | tf_op jit(solution)/shard_map/ppermute | solution.py:61
  80.9 16.3 %collective-permute-start.4 = (bf16[256,1024]{1,0:T(8,128)(2,1)}, bf16[256,1024]{1,0:T(8,128)(2,1)}, u32[]{:S(2)}, u32[]{:S(2)}) collective-permute-start(bf16[256,1024]{1,0:T(8,128)(2,1)} %get-tuple-element.35), channel_id=1, source_target_pairs={{0,129},{64,193},{8,137},{72,201},{16,145},{80,209},{24,153},{88,2... | collective-permute-start | bytes 1572872 | tf_op jit(solution)/shard_map/ppermute | solution.py:61
  84.2 18.0 %copy-start = (bf16[512,1024]{1,0:T(8,128)(2,1)}, bf16[512,1024]{1,0:T(8,128)(2,1)S(1)}, u32[]{:S(2)}) copy-start(bf16[512,1024]{1,0:T(8,128)(2,1)S(1)} %add_convert_fusion.chip_ref) | copy-start | bytes 3145732
  84.3 2.4 %copy-start.11 = (bf16[2048]{0:T(1024)(128)(2,1)S(1)}, bf16[2048]{0:T(1024)(128)(2,1)}, u32[]{:S(2)}) copy-start(bf16[2048]{0:T(1024)(128)(2,1)} %param.7) | copy-start | bytes 12292
  85.4 19.4 %collective-permute-start.5 = (bf16[256,1024]{1,0:T(8,128)(2,1)}, bf16[256,1024]{1,0:T(8,128)(2,1)S(1)}, u32[]{:S(2)}, u32[]{:S(2)}) collective-permute-start(bf16[256,1024]{1,0:T(8,128)(2,1)} %get-tuple-element.34), channel_id=1, source_target_pairs={{0,128},{64,192},{8,136},{72,200},{16,144},{80,208},{24,152},{88,2... | collective-permute-start | bytes 1572872 | tf_op jit(solution)/shard_map/ppermute | solution.py:61
  86.0 21.2 %collective-permute-start.6 = (bf16[256,1024]{1,0:T(8,128)(2,1)}, bf16[256,1024]{1,0:T(8,128)(2,1)S(1)}, u32[]{:S(2)}, u32[]{:S(2)}) collective-permute-start(bf16[256,1024]{1,0:T(8,128)(2,1)} %get-tuple-element.33), channel_id=1, source_target_pairs={{0,129},{64,193},{8,137},{72,201},{16,145},{80,209},{24,153},{88,2... | collective-permute-start | bytes 1572872 | tf_op jit(solution)/shard_map/ppermute | solution.py:61
  104.8 2.4 %copy-start.6 = (bf16[256,1024]{1,0:T(8,128)(2,1)}, bf16[256,1024]{1,0:T(8,128)(2,1)S(1)}, u32[]{:S(2)}) copy-start(bf16[256,1024]{1,0:T(8,128)(2,1)S(1)} %collective-permute-done.5.got_a) | copy-start | bytes 1572868
  107.2 0.8 copy-start.7
  111.7 11.3 %collective-permute-start.7 = (bf16[512,1024]{1,0:T(8,128)(2,1)}, bf16[512,1024]{1,0:T(8,128)(2,1)}, u32[]{:S(2)}, u32[]{:S(2)}) collective-permute-start(bf16[512,1024]{1,0:T(8,128)(2,1)} %get-tuple-element.27), channel_id=1, source_target_pairs={{0,64},{64,0},{8,72},{72,8},{16,80},{80,16},{24,88},{88,24},{32,96... | collective-permute-start | bytes 3145736 | tf_op jit(solution)/shard_map/ppermute | solution.py:61
  111.9 22.2 %collective-permute-start.22 = (bf16[512,1024]{1,0:T(8,128)(2,1)}, bf16[512,1024]{1,0:T(8,128)(2,1)}, u32[]{:S(2)}, u32[]{:S(2)}) collective-permute-start(bf16[512,1024]{1,0:T(8,128)(2,1)} %get-tuple-element.25), channel_id=1, source_target_pairs={{0,64},{64,0},{8,72},{72,8},{16,80},{80,16},{24,88},{88,24},{32,96... | collective-permute-start | bytes 3145736 | tf_op jit(solution)/shard_map/ppermute | solution.py:61
  115.2 7.7 %copy-start.10 = (f32[2,1024]{1,0:T(2,128)S(1)}, f32[2,1024]{1,0:T(2,128)}, u32[]{:S(2)}) copy-start(f32[2,1024]{1,0:T(2,128)} %get-tuple-element.29) | copy-start | bytes 24580
  115.2 33.1 %collective-permute-start.19 = (bf16[512,1024]{1,0:T(8,128)(2,1)}, bf16[512,1024]{1,0:T(8,128)(2,1)S(1)}, u32[]{:S(2)}, u32[]{:S(2)}) collective-permute-start(bf16[512,1024]{1,0:T(8,128)(2,1)} %convolution_convert_fusion.3), channel_id=1, source_target_pairs={{0,2},{64,70},{8,10},{72,78},{16,18},{80,86},{24,26},{88,94},{32,3... | collective-permute-start | bytes 3145736 | tf_op jit(solution)/shard_map/ppermute | solution.py:61
  119.2 3.8 %copy-start.4 = (bf16[512,1024]{1,0:T(8,128)(2,1)S(1)}, bf16[512,1024]{1,0:T(8,128)(2,1)}, u32[]{:S(2)}) copy-start(bf16[512,1024]{1,0:T(8,128)(2,1)} %by_depth.1) | copy-start | bytes 3145732
  119.2 6.7 %copy-start.12 = (bf16[1024,2048]{1,0:T(8,128)(2,1)S(1)}, bf16[1024,2048]{1,0:T(8,128)(2,1)}, u32[]{:S(2)}) copy-start(bf16[1024,2048]{1,0:T(8,128)(2,1)} %get-tuple-element.28) | copy-start | bytes 12582916
  122.4 41.0 %collective-permute-start.9 = (bf16[512,1024]{1,0:T(8,128)(2,1)}, bf16[512,1024]{1,0:T(8,128)(2,1)}, u32[]{:S(2)}, u32[]{:S(2)}) collective-permute-start(bf16[512,1024]{1,0:T(8,128)(2,1)} %convolution_convert_fusion.1), channel_id=1, source_target_pairs={{0,2},{64,70},{8,10},{72,78},{16,18},{80,86},{24,26},{88,94},{32,3... | collective-permute-start | bytes 3145736 | tf_op jit(solution)/shard_map/ppermute | solution.py:61
  132.5 17.8 %copy-start.15 = (bf16[512,1024]{1,0:T(8,128)(2,1)S(1)}, bf16[512,1024]{1,0:T(8,128)(2,1)}, u32[]{:S(2)}) copy-start(bf16[512,1024]{1,0:T(8,128)(2,1)} %convolution_convert_fusion.2) | copy-start | bytes 3145732
  132.5 30.9 %copy-start.13 = (bf16[512,1024]{1,0:T(8,128)(2,1)S(1)}, bf16[512,1024]{1,0:T(8,128)(2,1)}, u32[]{:S(2)}) copy-start(bf16[512,1024]{1,0:T(8,128)(2,1)} %get-tuple-element.27) | copy-start | bytes 3145732
  132.5 13.0 %collective-permute-start.15 = (f32[24,128]{1,0:T(8,128)S(1)}, f32[24,128]{1,0:T(8,128)S(1)}, u32[]{:S(2)}, u32[]{:S(2)}) collective-permute-start(f32[24,128]{1,0:T(8,128)S(1)} %reshape.31), channel_id=1, source_target_pairs={{0,2},{64,66},{8,10},{72,74},{16,18},{80,82},{24,26},{88,90},{32,3... | collective-permute-start | bytes 36872 | tf_op jit(solution)/shard_map/ppermute | solution.py:61
  135.8 37.7 %collective-permute-start.23 = (bf16[512,1024]{1,0:T(8,128)(2,1)S(1)}, bf16[512,1024]{1,0:T(8,128)(2,1)S(1)}, u32[]{:S(2)}, u32[]{:S(2)}) collective-permute-start(bf16[512,1024]{1,0:T(8,128)(2,1)S(1)} %convolution_convert_fusion), channel_id=1, source_target_pairs={{0,6},{64,66},{8,14},{72,74},{16,22},{80,82},{24,30},{88,90},{32,3... | collective-permute-start | bytes 3145736 | tf_op jit(solution)/shard_map/ppermute | solution.py:61
  145.5 16.4 %collective-permute-start.16 = (f32[24,128]{1,0:T(8,128)S(1)}, f32[24,128]{1,0:T(8,128)S(1)}, u32[]{:S(2)}, u32[]{:S(2)}) collective-permute-start(f32[24,128]{1,0:T(8,128)S(1)} %add.115), channel_id=1, source_target_pairs={{0,6},{64,70},{8,14},{72,78},{16,22},{80,86},{24,30},{88,94},{32,3... | collective-permute-start | bytes 36872 | tf_op jit(solution)/shard_map/ppermute | solution.py:61
  149.7 20.4 %collective-permute-start.20 = (bf16[256,1024]{1,0:T(8,128)(2,1)S(1)}, bf16[256,1024]{1,0:T(8,128)(2,1)S(1)}, u32[]{:S(2)}, u32[]{:S(2)}) collective-permute-start(bf16[256,1024]{1,0:T(8,128)(2,1)S(1)} %fusion.25), channel_id=1, source_target_pairs={{0,6},{64,66},{8,14},{72,74},{16,22},{80,82},{24,30},{88,90},{32,3... | collective-permute-start | bytes 1572872 | tf_op jit(solution)/shard_map/ppermute | solution.py:61
  150.3 37.5 %collective-permute-start.12 = (bf16[512,1024]{1,0:T(8,128)(2,1)S(1)}, bf16[512,1024]{1,0:T(8,128)(2,1)S(1)}, u32[]{:S(2)}, u32[]{:S(2)}) collective-permute-start(bf16[512,1024]{1,0:T(8,128)(2,1)S(1)} %copy-done.15), channel_id=1, source_target_pairs={{0,2},{64,70},{8,10},{72,78},{16,18},{80,86},{24,26},{88,94},{32,3... | collective-permute-start | bytes 3145736 | tf_op jit(solution)/shard_map/ppermute | solution.py:61
  161.9 6.8 %collective-permute-start.17 = (f32[24,128]{1,0:T(8,128)S(1)}, f32[24,128]{1,0:T(8,128)S(1)}, u32[]{:S(2)}, u32[]{:S(2)}) collective-permute-start(f32[24,128]{1,0:T(8,128)S(1)} %add.116), channel_id=1, source_target_pairs={{0,1},{64,65},{8,9},{72,73},{16,17},{80,81},{24,25},{88,89},{32,33... | collective-permute-start | bytes 36872 | tf_op jit(solution)/shard_map/ppermute | solution.py:61
  164.9 10.9 %collective-permute-start.10 = (bf16[256,1024]{1,0:T(8,128)(2,1)S(1)}, bf16[256,1024]{1,0:T(8,128)(2,1)S(1)}, u32[]{:S(2)}, u32[]{:S(2)}) collective-permute-start(bf16[256,1024]{1,0:T(8,128)(2,1)S(1)} %fusion.23), channel_id=1, source_target_pairs={{0,6},{64,66},{8,14},{72,74},{16,22},{80,82},{24,30},{88,90},{32,3... | collective-permute-start | bytes 1572872 | tf_op jit(solution)/shard_map/ppermute | solution.py:61
  169.3 3.7 %collective-permute-start.18 = (f32[8,128]{1,0:T(8,128)S(1)}, f32[8,128]{1,0:T(8,128)S(1)}, u32[]{:S(2)}, u32[]{:S(2)}) collective-permute-start(f32[8,128]{1,0:T(8,128)S(1)} %get-tuple-element.46), channel_id=1, source_target_pairs={{0,64},{64,0},{8,72},{72,8},{16,80},{80,16},{24,88},{88,24},{32,96... | collective-permute-start | bytes 12296 | tf_op jit(solution)/shard_map/ppermute | solution.py:61
  171.4 25.8 %collective-permute-start.21 = (bf16[128,1024]{1,0:T(8,128)(2,1)S(1)}, bf16[128,1024]{1,0:T(8,128)(2,1)S(1)}, u32[]{:S(2)}, u32[]{:S(2)}) collective-permute-start(bf16[128,1024]{1,0:T(8,128)(2,1)S(1)} %fusion.40), channel_id=1, source_target_pairs={{0,1},{64,65},{8,9},{72,73},{16,17},{80,81},{24,25},{88,89},{32,33... | collective-permute-start | bytes 786440 | tf_op jit(solution)/shard_map/ppermute | solution.py:61
  175.0 9.3 %collective-permute-start.24 = (bf16[256,1024]{1,0:T(8,128)(2,1)S(1)}, bf16[256,1024]{1,0:T(8,128)(2,1)S(1)}, u32[]{:S(2)}, u32[]{:S(2)}) collective-permute-start(bf16[256,1024]{1,0:T(8,128)(2,1)S(1)} %fusion.26), channel_id=1, source_target_pairs={{0,2},{64,70},{8,10},{72,78},{16,18},{80,86},{24,26},{88,94},{32,3... | collective-permute-start | bytes 1572872 | tf_op jit(solution)/shard_map/ppermute | solution.py:61
  178.0 33.3 %collective-permute-start.11 = (bf16[128,1024]{1,0:T(8,128)(2,1)}, bf16[128,1024]{1,0:T(8,128)(2,1)S(1)}, u32[]{:S(2)}, u32[]{:S(2)}) collective-permute-start(bf16[128,1024]{1,0:T(8,128)(2,1)} %fusion.42), channel_id=1, source_target_pairs={{0,1},{64,65},{8,9},{72,73},{16,17},{80,81},{24,25},{88,89},{32,33... | collective-permute-start | bytes 786440 | tf_op jit(solution)/shard_map/ppermute | solution.py:61
  185.6 10.2 %collective-permute-start.25 = (bf16[128,1024]{1,0:T(8,128)(2,1)S(1)}, bf16[128,1024]{1,0:T(8,128)(2,1)S(1)}, u32[]{:S(2)}, u32[]{:S(2)}) collective-permute-start(bf16[128,1024]{1,0:T(8,128)(2,1)S(1)} %fusion.39), channel_id=1, source_target_pairs={{0,1},{64,65},{8,9},{72,73},{16,17},{80,81},{24,25},{88,89},{32,33... | collective-permute-start | bytes 786440 | tf_op jit(solution)/shard_map/ppermute | solution.py:61
  187.7 12.6 %copy-start.14 = (bf16[512,1024]{1,0:T(8,128)(2,1)}, bf16[512,1024]{1,0:T(8,128)(2,1)S(1)}, u32[]{:S(2)}) copy-start(bf16[512,1024]{1,0:T(8,128)(2,1)S(1)} %collective-permute-done.12) | copy-start | bytes 3145732
  189.8 10.5 %collective-permute-start.13 = (bf16[256,1024]{1,0:T(8,128)(2,1)S(1)}, bf16[256,1024]{1,0:T(8,128)(2,1)S(1)}, u32[]{:S(2)}, u32[]{:S(2)}) collective-permute-start(bf16[256,1024]{1,0:T(8,128)(2,1)S(1)} %fusion.24), channel_id=1, source_target_pairs={{0,6},{64,66},{8,14},{72,74},{16,22},{80,82},{24,30},{88,90},{32,3... | collective-permute-start | bytes 1572872 | tf_op jit(solution)/shard_map/ppermute | solution.py:61
  200.3 1.8 copy-start.16
  202.1 9.4 %collective-permute-start.14 = (bf16[128,1024]{1,0:T(8,128)(2,1)S(1)}, bf16[128,1024]{1,0:T(8,128)(2,1)S(1)}, u32[]{:S(2)}, u32[]{:S(2)}) collective-permute-start(bf16[128,1024]{1,0:T(8,128)(2,1)S(1)} %fusion.41), channel_id=1, source_target_pairs={{0,1},{64,65},{8,9},{72,73},{16,17},{80,81},{24,25},{88,89},{32,33... | collective-permute-start | bytes 786440 | tf_op jit(solution)/shard_map/ppermute | solution.py:61
  204.7 10.5 %collective-permute-start.8 = (bf16[32,1024]{1,0:T(8,128)(2,1)S(1)}, bf16[32,1024]{1,0:T(8,128)(2,1)S(1)}, u32[]{:S(2)}, u32[]{:S(2)}) collective-permute-start(bf16[32,1024]{1,0:T(8,128)(2,1)S(1)} %get-tuple-element.38), channel_id=1, source_target_pairs={{0,1},{64,65},{8,9},{72,73},{16,17},{80,81},{24,25},{88,89},{32,33... | collective-permute-start | bytes 196616 | tf_op jit(solution)/shard_map/ppermute | solution.py:61
  211.3 0.7 copy-start.8
  212.0 0.7 copy-start.9
Sparse Core Ops, SparseCore 0:
  17.7 43.3 all-gather.1
  132.6 39.5 reduce-scatter.1

commit v2 on v0

v2 whole, which is shorter than its diff:
```python
import functools
import math

import jax
import jax.numpy as jnp
from jax import lax
from jax.experimental import pallas as pl
from jax.experimental.pallas import tpu as pltpu
from jax.sharding import PartitionSpec as P

root_two_pi = 0.7978845608028654
cubic_coef = 0.044715

AXES = ("row", "col", "depth")
COLS, DEPTHS = 8, 8
BF, F32 = jnp.bfloat16, jnp.float32

Y_FIRST = ((0, 1, 6, 7, 2, 3, 4, 5), (0, 1, 2, 3, 6, 7, 4, 5))
X_FIRST = ((0, 6, 2, 4, 1, 7, 3, 5), (0, 2, 6, 4, 1, 3, 7, 5))


def gelu_pair(pre):
    inner = root_two_pi * (pre + cubic_coef * pre * pre * pre)
    tangent = jnp.tanh(inner)
    act = 0.5 * pre * (1.0 + tangent)
    slope = 0.5 * (1.0 + tangent) + 0.5 * pre * (1.0 - tangent * tangent) * root_two_pi * (
        1.0 + 3.0 * cubic_coef * pre * pre
    )
    return (act, slope)


def flat(x, y, z, core):
    row = (x % 2) * 2 + core
    depth = y * 2 + x // 2
    return (row * COLS + z) * DEPTHS + depth


def pairs_of(target):
    pairs = []
    for x in range(4):
        for y in range(4):
            for z in range(8):
                for core in range(2):
                    tx, ty, tz, tc = target(x, y, z, core)
                    pairs.append((flat(x, y, z, core), flat(tx % 4, ty % 4, tz % 8, tc % 2)))
    return pairs


CORE = pairs_of(lambda x, y, z, c: (x, y, z, c ^ 1))
NEAR = pairs_of(lambda x, y, z, c: (x ^ 1, y, z, c))
X_HI = pairs_of(lambda x, y, z, c: (x + 2, y, z, c))
Y_ONE = pairs_of(lambda x, y, z, c: (x, y ^ (3 if c else 1), z, c))
Y_TWO = pairs_of(lambda x, y, z, c: (x, y ^ (1 if c else 3), z, c))
Z = {k: pairs_of(lambda x, y, z, c, k=k: (x, y, z + k, c)) for k in (-2, -1, 1, 2)}
Z_XOR = {k: pairs_of(lambda x, y, z, c, k=k: (x, y, z ^ k, c)) for k in (1, 2, 4)}


def send(value, pairs):
    return lax.ppermute(value, AXES, pairs)


def together(*values):
    return lax.optimization_barrier(values)


def after(value, *others):
    return together(value, *others)[0]


def dot(a, b):
    return jnp.dot(a, b, preferred_element_type=F32)


def dot_t(a, b):
    return lax.dot_general(a, b, (((1,), (1,)), ((), ())), preferred_element_type=F32)


def dot_tn(a, b):
    return lax.dot_general(a, b, (((0,), (0,)), ((), ())), preferred_element_type=F32)


ANY = pl.BlockSpec(memory_space=pl.ANY)
WHOLE = pl.BlockSpec(memory_space=pltpu.VMEM)
SCALARS = pl.BlockSpec(memory_space=pltpu.SMEM)
STEP = 256


def tiles(n):
    return [slice(i, i + STEP) for i in range(0, n, STEP)]


def local(kernel, name, outs, at, *arrays):
    single = not isinstance(outs, list)
    shapes = [jax.ShapeDtypeStruct(*out) for out in ([outs] if single else outs)]
    return pl.pallas_call(
        kernel,
        in_specs=[SCALARS] + [WHOLE] * len(arrays),
        out_specs=WHOLE if single else [WHOLE] * len(shapes),
        out_shape=shapes[0] if single else shapes,
        cost_estimate=pl.CostEstimate(flops=0, bytes_accessed=1 << 12, transcendentals=0),
        compiler_params=pltpu.CompilerParams(vmem_limit_bytes=16 << 20),
        name=name,
    )(at, *arrays)


def order_of(i, at, order=Y_FIRST):
    packed = [sum(k << (4 * j) for j, k in enumerate(ks)) for ks in order]
    return ((jnp.where(at[0] == 0, packed[0], packed[1]) >> (4 * i)) & 7) ^ at[1]


def place_of(i, at):
    h = i // 8
    return order_of(i % 8, (at[0] ^ h, at[1])) * 2 + (at[0] ^ h)


def plain_of(i, at):
    return (i % 8) * 2 + (at[0] ^ (i // 8))


def permute_kernel(axis, orders, at_ref, a_ref, *refs):
    outs, sems = refs[:-1], refs[-1]
    copies = []
    for o, (order, out) in enumerate(zip(orders, outs)):
        for i in range(16):
            source = pl.ds(pl.multiple_of(order(i, at_ref) * 128, 128), 128)
            target = pl.ds(i * 128, 128)
            if axis == 1:
                source, target = (slice(None), source), (slice(None), target)
            copies.append(
                pltpu.make_async_copy(a_ref.at[source], out.at[target], sems.at[16 * o + i])
            )
    for copy in copies:
        copy.start()
    for copy in copies:
        copy.wait()


def permute(at, w, axis, orders):
    return pl.pallas_call(
        functools.partial(permute_kernel, axis, orders),
        in_specs=[SCALARS, ANY],
        out_specs=[WHOLE] * len(orders),
        out_shape=[jax.ShapeDtypeStruct(w.shape, w.dtype)] * len(orders),
        scratch_shapes=[pltpu.SemaphoreType.DMA((16 * len(orders),))],
        compiler_params=pltpu.CompilerParams(vmem_limit_bytes=16 << 20),
        cost_estimate=pl.CostEstimate(flops=0, bytes_accessed=1 << 12, transcendentals=0),
        name=f"permute_{axis}",
    )(at, w)


def bias_kernel(at_ref, b_ref, b_out):
    for i in range(8):
        at = pl.multiple_of(place_of(i, at_ref) * 128, 128)
        b_out[:, i * 128 : (i + 1) * 128] = b_ref[:, pl.ds(at, 128)].astype(F32)


def bias_mine(at, b):
    return local(bias_kernel, "bias_mine", ((1, b.shape[0] // 2), F32), at, b.reshape(1, -1))


def pack_kernel(a_ref, b_ref, out_ref, sems):
    rows = a_ref.shape[0]
    copies = [
        pltpu.make_async_copy(ref, out_ref.at[pl.ds(i * rows, rows)], sems.at[i])
        for i, ref in enumerate((a_ref, b_ref))
    ]
    for copy in copies:
        copy.start()
    for copy in copies:
        copy.wait()


def pack(a, b):
    return pl.pallas_call(
        pack_kernel,
        in_specs=[ANY] * 2,
        out_specs=WHOLE,
        out_shape=jax.ShapeDtypeStruct((2 * a.shape[0], a.shape[1]), a.dtype),
        scratch_shapes=[pltpu.SemaphoreType.DMA((2,))],
        cost_estimate=pl.CostEstimate(flops=0, bytes_accessed=1 << 12, transcendentals=0),
        name="pack",
    )(a, b)


AWAY_Z = (0, 1, 2, -2, -1, 3, -3, 4)
NEAR_BLOCKS = 5


def gather_near(block, *meanwhile):
    near = [send(block, Z[-k]) for k in AWAY_Z[1:NEAR_BLOCKS]]
    return [block, *together(*near, *meanwhile)[:4]]


def gather_far(near):
    half = near[0].shape[0] // 2
    up, down = near[2], near[3]
    last = send(up[:half], Z[-2]), send(down[half:], Z[2])
    return [send(up, Z[-1]), send(down, Z[1]), *last]


def arrange_near_kernel(at_ref, *refs):
    blocks, w_ref, tok_out, out_ref = refs[:NEAR_BLOCKS], *refs[NEAR_BLOCKS:]
    n = blocks[0].shape[0] // 2
    for i, block in enumerate(blocks):
        tok_out[i * n : (i + 1) * n, :] = block[:n, :]
    width = out_ref.shape[1]
    for cols in tiles(width):
        other = slice(width + cols.start, width + cols.stop)
        out_ref[:, cols] = dot(tok_out[...], w_ref[:, other]).astype(BF)


def arrange_near(at, blocks, w_in):
    rows, cols = blocks[0].shape
    rows = rows // 2 * NEAR_BLOCKS
    outs = [((rows, cols), BF), ((rows, w_in.shape[1] // 2), BF)]
    return local(arrange_near_kernel, "arrange_near", outs, at, *blocks, w_in)


def arrange_far_kernel(at_ref, tok_ref, *refs):
    blocks, w_ref, tok_out, cot_out, out_ref, sums, sum_out = refs[:9], *refs[9:]
    n = blocks[0].shape[0] // 2
    first = tok_ref.shape[0]
    tok_out[:first, :] = tok_ref[...]
    for i, block in enumerate(blocks[:7]):
        rows = slice(i * n, (i + 1) * n)
        if i >= NEAR_BLOCKS:
            tok_out[rows, :] = block[:n, :]
        cot_out[rows, :] = block[n:, :]
    tok_out[7 * n :, :] = blocks[7][...]
    cot_out[7 * n :, :] = blocks[8][...]
    width = out_ref.shape[1]
    for cols in tiles(width):
        other = slice(width + cols.start, width + cols.stop)
        out_ref[:, cols] = dot(tok_out[first:, :], w_ref[:, other]).astype(BF)
    for i, k in enumerate(AWAY_Z):
        value = jnp.sum(cot_out[i * n : (i + 1) * n, :].astype(F32), axis=0, keepdims=True)
        sums[pl.ds((at_ref[2] + k) & 7, 1), :] = value
    sum_out[...] = jnp.sum(sums[...], axis=0, keepdims=True)


def arrange_far(at, tok, blocks, w_in):
    rows, cols = blocks[0].shape
    rows, width = 4 * rows, w_in.shape[1] // 2
    outs = [((rows, cols), BF)] * 2 + [((rows - tok.shape[0], width), BF), ((8, cols), F32), ((1, cols), F32)]
    tok, cot, terms, _, cot_sum = local(arrange_far_kernel, "arrange_far", outs, at, tok, *blocks, w_in)
    return tok, cot, terms, cot_sum


def grad_other_kernel(at_ref, cot_ref, w_ref, out_ref):
    width = out_ref.shape[1]
    for cols in tiles(width):
        other = slice(width + cols.start, width + cols.stop)
        out_ref[:, cols] = dot_t(cot_ref[...], w_ref[other, :]).astype(BF)


def grad_other(at, cot, w_out):
    out = ((cot.shape[0], w_out.shape[0] // 2), BF)
    return local(grad_other_kernel, "grad_other", out, at, cot, w_out)


def chip_kernel(transposed, at_ref, a_ref, w_ref, got_ref, out_ref):
    rows = slice(a_ref.shape[0] - out_ref.shape[0], a_ref.shape[0])
    for cols in tiles(out_ref.shape[1]):
        if transposed:
            value = dot_t(a_ref[rows, :], w_ref[cols, :])
        else:
            value = dot(a_ref[rows, :], w_ref[:, cols])
        out_ref[:, cols] = (value + got_ref[:, cols].astype(F32)).astype(BF)


def chip_sum(at, a, w, got, transposed):
    kernel = functools.partial(chip_kernel, transposed)
    return local(kernel, "chip_sum", (got.shape, BF), at, a, w, got)


def gelu_kernel(slope, at_ref, *refs):
    halves, bias_ref, out_ref = (refs[:2], refs[2:4]), refs[4], refs[5]
    base = 0
    for chip_ref, got_ref in halves:

        @pl.loop(0, chip_ref.shape[0], step=16)
        def _(i, base=base, chip_ref=chip_ref, got_ref=got_ref):
            i = pl.multiple_of(i, 16)
            rows = pl.ds(i, 16)
            pre = chip_ref[rows, :].astype(F32) + got_ref[rows, :].astype(F32)
            value = gelu_pair(pre + bias_ref[...])[slope]
            out_ref[pl.ds(pl.multiple_of(base + i, 16), 16), :] = value.astype(out_ref.dtype)

        base += chip_ref.shape[0]


def gelu(at, near, far, bias, slope):
    rows = near[0].shape[0] + far[0].shape[0]
    out, name = ((rows, bias.shape[1]), F32 if slope else BF), "slope" if slope else "act"
    return local(functools.partial(gelu_kernel, slope), name, out, at, *near, *far, bias)


def pre_grad_kernel(at_ref, slope_ref, chip_ref, got_ref, out_ref, sum_ref):
    for b in range(8):
        here = slice(b * 128, b * 128 + 128)
        there = pl.ds(pl.multiple_of(order_of(b, at_ref) * 128, 128), 128)
        grad = chip_ref[:, here].astype(F32) + got_ref[:, here].astype(F32)
        value = (slope_ref[:, here] * grad).astype(BF)
        out_ref[:, there] = value
        sum_ref[:, there] = jnp.sum(value.astype(F32), axis=0, keepdims=True)


def pre_grad(at, slope, chip, got):
    outs = [(slope.shape, BF), ((1, slope.shape[1]), F32)]
    return local(pre_grad_kernel, "pre_grad", outs, at, slope, chip, got)


def by_depth_kernel(at_ref, a_ref, *outs):
    for order, out in zip((Y_FIRST, X_FIRST), outs):
        for i in range(8):
            at = pl.multiple_of(order_of(i, at_ref, order) * 128, 128)
            out[:, i * 128 : (i + 1) * 128] = a_ref[:, pl.ds(at, 128)]


def by_depth(at, a):
    return local(by_depth_kernel, "by_depth", [(a.shape, a.dtype)] * 2, at, a)


OWN = (((512, 1024),), ((256, 512),), ((128, 256),), ((0, 128),))
AWAY = (((256, 512), (768, 1024)), ((512, 768),), ((128, 256),), ((0, 128),))


def split(value):
    high = value.astype(BF).astype(F32)
    return jnp.concatenate([high, value - high], axis=0).astype(BF)


def joined(ref, start):
    return ref[start : start + 8, :].astype(F32) + ref[start + 8 : start + 16, :].astype(F32)


SIZES = (512, 256, 128, 128)


def depth_kernel(level, sides, at_ref, *refs):
    count = min(level, 2)
    lefts, right_ref, refs = refs[: len(sides)], refs[len(sides)], refs[len(sides) + 1 :]
    got_refs, refs, out_ref = refs[:count], refs[count:-1], refs[-1]
    size = SIZES[level]
    skip = 0 if level == 3 else size
    for s, (side, left_ref) in enumerate(zip(sides, lefts)):
        done = 0
        for start, stop in side[level]:
            rows = slice(s * size + done, s * size + done + stop - start)
            for cols in tiles(out_ref.shape[1]):
                value = dot_tn(left_ref[:, start:stop], right_ref[:, cols])
                for i, got_ref in enumerate(got_refs):
                    base = s * SIZES[i] + skip + done
                    value = value + got_ref[base : base + stop - start, cols].astype(F32)
                out_ref[rows, cols] = value.astype(out_ref.dtype)
            done += stop - start
    if refs and level == 0:
        own, away, cot_sum = refs
        row = lax.broadcasted_iota(jnp.int32, (8, out_ref.shape[1]), 0)
        value = jnp.where(row == 2, cot_sum[...], 0.0)
        value = jnp.where(row == at_ref[0], own[...], value)
        value = jnp.where(row == 1 - at_ref[0], away[...], value)
        out_ref[512:528, :] = split(value)
    elif refs and level == 1:
        out_ref[256:272, :] = split(joined(refs[0], 512) + joined(got_refs[0], 512))
    elif refs and level == 2:
        out_ref[128:144, :] = refs[0][256:272, :]
        out_ref[144:160, :] = got_refs[1][256:272, :]


class DepthSum:
    def __init__(self, at, sides, lefts, right, pairs, riders=()):
        self.at, self.sides, self.lefts, self.right, self.pairs = at, sides, lefts, right, pairs
        self.riders, self.got, self.sent = riders, [], []

    def rows(self, level, dtype, riders):
        size = SIZES[level] * len(self.sides) + (0, 16, 32)[bool(riders) + (bool(riders) and level == 2)]
        kernel = functools.partial(depth_kernel, level, self.sides)
        out = ((size, self.right.shape[1]), dtype)
        got = self.got[: min(level, 2)]
        return local(
            kernel, f"depth_{level}", out, self.at, *self.lefts, self.right, *got, *riders
        )

    def exchange(self):
        level = len(self.got)
        riders = self.riders if level == 0 else self.sent[-1:] if self.riders else ()
        self.sent.append(self.rows(level, BF, riders))
        self.got.append(send(self.sent[-1], self.pairs[level]))

    def kept_rows(self, *earlier):
        self.right = after(self.right, *earlier)
        return self.rows(3, F32, ())


def inputs_grad_kernel(at_ref, own_ref, away_ref, w_ref, out_ref, sent_ref):
    n = out_ref.shape[0] // 8
    width = own_ref.shape[1]
    for cols in tiles(out_ref.shape[1]):
        value = dot_t(own_ref[...], w_ref[cols, :width]) + dot_t(away_ref[...], w_ref[cols, width:])
        for i, away in enumerate(AWAY_Z):
            k = at_ref[2] ^ ((at_ref[2] + away) & 7)
            place = ((k & 1) << 2) | (k & 2) | (k >> 2)
            out_ref[pl.ds(pl.multiple_of(place * n, n), n), cols] = value[i * n : (i + 1) * n]
    sent_ref[...] = out_ref[4 * n :, :].astype(BF)


def inputs_grad(at, own, away, w_in):
    rows, cols = own.shape[0], w_in.shape[0]
    outs = [((rows, cols), F32), ((rows // 2, cols), BF)]
    return local(inputs_grad_kernel, "inputs_grad", outs, at, own, away, w_in)


def rows_kernel(scale, at_ref, keep_ref, got_ref, out_ref):
    for h in range(2):
        here = slice(h * 128, h * 128 + 128)
        there = pl.ds(pl.multiple_of((at_ref[0] ^ h) * 128, 128), 128)
        out_ref[there, :] = (keep_ref[here, :] + got_ref[here, :].astype(F32)) * scale


def place_rows(at, scale, keep, got):
    kernel = functools.partial(rows_kernel, scale)
    return local(kernel, "place_rows", (keep.shape, F32), at, keep, got)


def columns_kernel(scale, at_ref, keep_ref, got_ref, keep2_ref, got2_ref, sent_ref, out_ref, bias_ref):
    for h, (k, g) in enumerate(((keep_ref, got_ref), (keep2_ref, got2_ref))):
        for i in range(8):
            at = pl.multiple_of((2 * i + (at_ref[0] ^ h)) * 128, 128)
            cols = slice(i * 128, i * 128 + 128)
            out_ref[:, pl.ds(at, 128)] = (k[:, cols] + g[:128, cols].astype(F32)) * scale
    v = [joined(ref, start) for ref in (sent_ref, got2_ref) for start in (128, 144)]
    zero = at_ref[0] == 0
    first = v[0] + jnp.where(zero, v[1], v[2])
    second = jnp.where(zero, v[2], v[1]) + v[3]
    total = (first + second) * scale
    for i in range(8):
        cols = slice(i * 128, i * 128 + 128)
        for row in range(2):
            bias_ref[2 * i + row : 2 * i + row + 1, :] = total[row : row + 1, cols]
        bias_ref[16 + i : 17 + i, :] = total[2:3, cols]


def place_columns(at, scale, keep, got, keep2, got2, sent2):
    rows, cols = keep.shape
    kernel = functools.partial(columns_kernel, scale)
    outs = [((rows, 2 * cols), F32), ((24, 128), F32)]
    return local(kernel, "place_columns", outs, at, keep, got, keep2, got2, sent2)


def body(inputs, w_in, b_in, w_out, cotangent):
    core = lax.axis_index("row") % 2
    total_tokens = inputs.shape[0] * COLS * DEPTHS
    scale = 1.0 / math.sqrt(total_tokens)
    at = jnp.stack([core, lax.axis_index("depth"), lax.axis_index("col")]).astype(jnp.int32)
    n = inputs.shape[0]

    bias = bias_mine(at, b_in)
    w_in, w_in_plain = permute(at, w_in, 1, (place_of, plain_of))
    (w_out,) = permute(at, w_out, 0, (place_of,))
    near = gather_near(pack(inputs, cotangent), bias, w_in_plain, w_out)
    far = gather_far(near)

    tok_near, terms = arrange_near(at, near, w_in)
    chip_near = chip_sum(at, tok_near, w_in, send(terms, CORE), False)
    got_near = send(chip_near, NEAR)
    tok, cot, terms, cot_sum = arrange_far(at, tok_near, near + far, w_in)
    terms, got_near = together(send(terms, CORE), got_near)
    chip_far = chip_sum(at, tok, w_in, terms, False)
    got_far = send(chip_far, NEAR)
    terms = grad_other(at, after(cot, chip_far), w_out)
    chip_two = chip_sum(at, cot, w_out, send(terms, CORE), True)
    got_two = send(chip_two, NEAR)
    got_far = after(got_far, chip_two)
    act = gelu(at, (chip_near, got_near), (chip_far, got_far), bias, 0)
    act_away = send(act, CORE)

    out = DepthSum(at, (OWN, AWAY), (act, act_away), cot, (Y_ONE, Y_TWO, X_HI))
    out.exchange()
    bias = after(bias, act_away)
    slope = gelu(at, (chip_near, got_near), (chip_far, got_far), bias, 1)
    tok_one, tok_two = by_depth(at, after(tok, slope))
    pg, db = pre_grad(at, after(slope, tok_one), chip_two, got_two)
    pg_away = send(pg, CORE)
    db_away = send(db, CORE)

    out.got[0], tok_one, tok_two = together(out.got[0], tok_one, tok_two, pg)[:3]
    out.exchange()
    one = DepthSum(at, (OWN,), (after(tok_one, out.sent[1]),), pg, (Y_ONE, Y_TWO, X_HI))
    one.exchange()
    riders = db, db_away, cot_sum
    two = DepthSum(at, (OWN,), (tok_two,), pg_away, (X_HI, Y_ONE, Y_TWO), riders)
    two.exchange()
    gi, gi_sent = inputs_grad(at, after(pg, one.sent[0], two.sent[0]), pg_away, w_in_plain)
    gi_got = [send(gi_sent, Z_XOR[1])]

    one.got[0], two.got[0], out.got[1], gi_got[0] = together(
        one.got[0], two.got[0], out.got[1], gi_got[0]
    )
    one.exchange()
    two.exchange()
    out.exchange()
    gi_sent = (gi[2 * n : 4 * n] + gi_got[0][2 * n :].astype(F32)).astype(BF)
    gi_got.append(send(gi_sent, Z_XOR[2]))
    out_kept = out.kept_rows(one.sent[1], two.sent[1], out.sent[2], gi_sent)

    one.got[1], two.got[1], out.got[2], gi_got[1] = together(
        one.got[1], two.got[1], out.got[2], gi_got[1]
    )
    one.exchange()
    two.exchange()
    gi_sent = gi[n : 2 * n] + gi_got[0][n : 2 * n].astype(F32) + gi_got[1][n:].astype(F32)
    gi_sent = gi_sent.astype(BF)
    gi_got.append(send(gi_sent, Z_XOR[4]))
    sent = one.sent[2], two.sent[2], gi_sent
    one_kept, two_kept = one.kept_rows(*sent), two.kept_rows(*sent)
    grad_w_out = place_rows(at, scale, after(out_kept, one_kept, two_kept), out.got[2])
    gi = gi[:n] + sum(got[:n].astype(F32) for got in gi_got)
    grad_inputs = gi.astype(BF)
    grad_w_in, db = place_columns(
        at, scale, one_kept, one.got[2], two_kept, two.got[2], two.sent[2]
    )
    grad_b_in, grad_b_out = db[:16].reshape(-1), db[16:].reshape(-1)
    return (grad_inputs, grad_w_in, grad_b_in, grad_w_out, grad_b_out)


def solution(mesh):
    in_specs = (
        P(("col", "depth"), "row"),
        P("row", "col"),
        P("col"),
        P("col", "row"),
        P(("col", "depth"), "row"),
    )
    out_specs = (
        P(("col", "depth"), "row"),
        P(("row", "depth"), "col"),
        P("col"),
        P(("col", "depth"), "row"),
        P("row"),
    )
    return jax.shard_map(body, mesh=mesh, in_specs=in_specs, out_specs=out_specs, check_vma=False)
```

time: 569 us -> 176 us (0.31)
  waiting for transfers between devices: 315 us -> 85.7 us
  blocking collectives: 191 us -> 0 us
  Pallas kernels: 0 us -> 42.7 us
  starting transfers between devices: 0.42 us -> 40 us
  matrix products: 31.6 us -> 0 us
  between operations: 14.2 us -> 0.92 us
  other arithmetic: 11.9 us -> 0.92 us
    psum x2 -> x0, blocking collectives: 191 us -> none  [the longest x1 171 us: body(): lax.psum(jnp.sum(cotangent, axis=0, dtype=jnp.float32), ('col', 'depth'))]
    psum x1 -> x0, waiting for transfers between devices: 163 us -> none  [body(): pre_sum, grad_sum = lax.psum((pre_part, grad_part), 'row')]
    ppermute x0 -> x29, waiting for transfers between devices: none -> 85.7 us  [send(): return lax.ppermute(value, AXES, pairs)]
    reduce_scatter x3 -> x0, waiting for transfers between devices: 76.9 us -> none  [the longest x1 76.9 us: body(): lax.psum_scatter(lax.dot_general(act_all, cot_all, (((0,), (0,)), ((), ()...]
    all_gather x2 -> x0, waiting for transfers between devices: 73.9 us -> none  [the longest x1 41.7 us: body(): lax.all_gather(inputs, 'col', axis=0, tiled=True)]
    pallas_call x0 -> x29, Pallas kernels: none -> 42.7 us  [the longest x26 36.5 us: local(): pl.pallas_call(kernel, in_specs=[SCALARS] + [WHOLE] * len(arrays), out_sp...]
    ppermute x0 -> x29, starting transfers between devices: none -> 40 us  [send(): return lax.ppermute(value, AXES, pairs)]
    dot_general x5 -> x0, matrix products: 31.6 us -> none  [the longest x1 8.63 us: body(): lax.dot_general(act_all, cot_all, (((0,), (0,)), ((), ())), preferred_ele...]
  transfers between devices with their start and end apart: 6 -> 29, of which waited for: 4 -> 16; matrix products, arithmetic and copies ran while one was open for 5% -> 1% of each run, Pallas kernels for 0% -> 17%
where the time goes in v2:
time: 176 us; the launch traced here: 175 us
  waiting for transfers between devices  85.7 us (49%)
  Pallas kernels  42.7 us (24%)
  starting transfers between devices  40 us (23%)
  local copies, waits for them, and re-layouts  5.2 us (3%)
    ppermute x29, waiting for transfers between devices, send(): return lax.ppermute(value, AXES, pairs)  85.7 us
    ppermute x29, starting transfers between devices, send(): return lax.ppermute(value, AXES, pairs)  40 us
    pallas_call x26, Pallas kernels, local(): pl.pallas_call(kernel, in_specs=[SCALARS] + [WHOLE] * len(arrays), out_sp...  36.5 us
    pallas_call x2, Pallas kernels, permute(): pl.pallas_call(functools.partial(permute_kernel, axis, orders), in_specs=...  4.46 us
  transfers between devices with their start and end apart: 29, of which 16 were waited for; matrix products, arithmetic and copies ran while one was open for 1% of the time, Pallas kernels for 17%

profile of v2, /device:TPU:32, one launch (start us, length us, event | category | flops | bytes accessed | tf_op | source)
XLA Modules:
  0.0 175.4 jit_solution(4735748952248610260)
XLA Ops:
  0.6 1.7 pack.1.refs_0_
  2.3 2.0 %collective-permute-start.3 = (bf16[128,1024]{1,0:T(8,128)(2,1)}, bf16[128,1024]{1,0:T(8,128)(2,1)S(1)}, u32[]{:S(2)}, u32[]{:S(2)}) collective-permute-start(bf16[128,1024]{1,0:T(8,128)(2,1)} %pack.1.refs_0_), channel_id=1, source_target_pairs={{0,8},{64,72},{8,16},{72,80},{16,24},{80,88},{24,32},{88,96},{32,4... | collective-permute-start | bytes 786440 | tf_op jit(solution)/shard_map/ppermute | solution.py:59
  4.3 4.5 %collective-permute-start.2 = (bf16[128,1024]{1,0:T(8,128)(2,1)}, bf16[128,1024]{1,0:T(8,128)(2,1)S(1)}, u32[]{:S(2)}, u32[]{:S(2)}) collective-permute-start(bf16[128,1024]{1,0:T(8,128)(2,1)} %pack.1.refs_0_), channel_id=1, source_target_pairs={{0,16},{64,80},{8,24},{72,88},{16,32},{80,96},{24,40},{88,104},{32... | collective-permute-start | bytes 786440 | tf_op jit(solution)/shard_map/ppermute | solution.py:59
  11.2 2.2 %copy-done = bf16[2048,1024]{1,0:T(8,128)(2,1)S(1)} copy-done((bf16[2048,1024]{1,0:T(8,128)(2,1)S(1)}, bf16[2048,1024]{1,0:T(8,128)(2,1)}, u32[]{:S(2)}) %copy-start) | copy-done | bytes 4194328
  14.4 1.1 copy-done.1
  15.6 3.4 %permute_1.1 = (bf16[1024,2048]{1,0:T(8,128)(2,1)S(1)}, bf16[1024,2048]{1,0:T(8,128)(2,1)S(1)}) custom-call(s32[3]{0:T(128)S(1)} %pad_add_fusion.at_ref, bf16[1024,2048]{1,0:T(8,128)(2,1)S(1)} %copy-done.1), custom_call_target="tpu_custom_call" | custom-call | bytes 4096 | tf_op jit(solution)/shard_map/permute_1/pallas_call | solution.py:139
  19.0 6.6 %collective-permute-done.2.refs_3_ = bf16[128,1024]{1,0:T(8,128)(2,1)S(1)} collective-permute-done((bf16[128,1024]{1,0:T(8,128)(2,1)}, bf16[128,1024]{1,0:T(8,128)(2,1)S(1)}, u32[]{:S(2)}, u32[]{:S(2)}) %collective-permute-start.2) | collective-permute-done | bytes 262176 | tf_op jit(solution)/shard_map/ppermute | solution.py:59
  25.6 1.5 collective-permute-done.refs_1_
  27.1 1.4 arrange_near.1
  28.6 1.1 collective-permute-start.5
  29.7 1.2 collective-permute-start.6
  30.9 1.4 chip_sum.3.refs_0_
  32.3 1.6 collective-permute-start.10
  33.9 4.8 %collective-permute-start.8 = (bf16[64,1024]{1,0:T(8,128)(2,1)S(1)}, bf16[64,1024]{1,0:T(8,128)(2,1)S(1)}, u32[]{:S(2)}, u32[]{:S(2)}) collective-permute-start(bf16[64,1024]{1,0:T(8,128)(2,1)S(1)} %slice.37), channel_id=1, source_target_pairs={{0,16},{64,80},{8,24},{72,88},{16,32},{80,96},{24,40},{88,104},{32... | collective-permute-start | bytes 393224 | tf_op jit(solution)/shard_map/ppermute | solution.py:59
  38.8 7.7 %collective-permute-done.8.refs_8_ = bf16[64,1024]{1,0:T(8,128)(2,1)S(1)} collective-permute-done((bf16[64,1024]{1,0:T(8,128)(2,1)S(1)}, bf16[64,1024]{1,0:T(8,128)(2,1)S(1)}, u32[]{:S(2)}, u32[]{:S(2)}) %collective-permute-start.8) | collective-permute-done | bytes 131104 | tf_op jit(solution)/shard_map/ppermute | solution.py:59
  46.5 1.9 %arrange_far.1 = (bf16[512,1024]{1,0:T(8,128)(2,1)S(1)}, bf16[512,1024]{1,0:T(8,128)(2,1)S(1)}, bf16[192,1024]{1,0:T(8,128)(2,1)S(1)}, f32[8,1024]{1,0:T(8,128)}, f32[1,1024]{1,0:T(1,128)S(1)}) custom-call(s32[3]{0:T(128)S(1)} %pad_add_fusion.at_ref, bf16[320,1024]{1,0:T(8,128)(2,1)S(1)} %get-tuple-element.55.a_ref.tok_ref, bf16[128,1024]{1,0:T(8,128)(2,1)S(1)} %copy-done.2, ...), custom_call_target="tpu_custom_call" | custom-call | bytes 4096 | tf_op jit(solution)/shard_map/arrange_far/pallas_call | solution.py:95
  48.4 1.7 collective-permute-done.9.got_ref
  50.2 1.1 chip_sum.4.refs_2_
  51.3 1.8 %grad_other.1 = bf16[512,1024]{1,0:T(8,128)(2,1)S(1)} custom-call(s32[3]{0:T(128)S(1)} %pad_add_fusion.at_ref, bf16[512,1024]{1,0:T(8,128)(2,1)S(1)} %get-tuple-element.90.cot_ref.a_ref.refs_2_, bf16[2048,1024]{1,0:T(8,128)(2,1)S(1)} %permute_0.1.w_ref), custom_call_target="tpu_custom_call" | custom-call | bytes 4096 | tf_op jit(solution)/shard_map/grad_other/pallas_call | solution.py:95
  53.3 1.5 collective-permute-start.11
  55.9 1.8 %chip_sum.5.chip_ref = bf16[512,1024]{1,0:T(8,128)(2,1)S(1)} custom-call(s32[3]{0:T(128)S(1)} %pad_add_fusion.at_ref, bf16[512,1024]{1,0:T(8,128)(2,1)S(1)} %get-tuple-element.90.cot_ref.a_ref.refs_2_, bf16[2048,1024]{1,0:T(8,128)(2,1)S(1)} %permute_0.1.w_ref, bf16[512,1024]{1,0:T(8,128)(2,1)S(1)} %collective-permute-done.12.got_ref), custom_call_target="tpu_custom_call" | custom-call | bytes 4096 | tf_op jit(solution)/shard_map/chip_sum/pallas_call | solution.py:95
  57.7 7.0 %collective-permute-done.11.refs_3_ = bf16[192,1024]{1,0:T(8,128)(2,1)S(1)} collective-permute-done((bf16[192,1024]{1,0:T(8,128)(2,1)S(1)}, bf16[192,1024]{1,0:T(8,128)(2,1)S(1)}, u32[]{:S(2)}, u32[]{:S(2)}) %collective-permute-start.11) | collective-permute-done | bytes 393248 | tf_op jit(solution)/shard_map/ppermute | solution.py:59
  64.7 1.9 %act.1.refs_0_ = bf16[512,1024]{1,0:T(8,128)(2,1)S(1)} custom-call(s32[3]{0:T(128)S(1)} %pad_add_fusion.at_ref, bf16[320,1024]{1,0:T(8,128)(2,1)S(1)} %chip_sum.3.refs_0_, bf16[320,1024]{1,0:T(8,128)(2,1)S(1)} %collective-permute-done.10.refs_1_, bf16[192,1024]{1,0:T(8,128)(2,1)S(1)} %chip_sum.4.refs_2_, ...), custom_call_target="tpu_custom_call" | custom-call | bytes 4096 | tf_op jit(solution)/shard_map/act/pallas_call | solution.py:95
  66.7 2.6 %collective-permute-done.13.refs_1_ = bf16[512,1024]{1,0:T(8,128)(2,1)S(1)} collective-permute-done((bf16[512,1024]{1,0:T(8,128)(2,1)S(1)}, bf16[512,1024]{1,0:T(8,128)(2,1)S(1)}, u32[]{:S(2)}, u32[]{:S(2)}) %collective-permute-start.13) | collective-permute-done | bytes 1048608 | tf_op jit(solution)/shard_map/ppermute | solution.py:59
  69.4 1.8 %depth_0.3 = bf16[1024,1024]{1,0:T(8,128)(2,1)S(1)} custom-call(s32[3]{0:T(128)S(1)} %pad_add_fusion.at_ref, bf16[512,1024]{1,0:T(8,128)(2,1)S(1)} %act.1.refs_0_, bf16[512,1024]{1,0:T(8,128)(2,1)S(1)} %collective-permute-done.13.refs_1_, bf16[512,1024]{1,0:T(8,128)(2,1)S(1)} %get-tuple-element.90.cot_ref.a_ref.refs_2_), custom_call_target="tpu_custom_call" | custom-call | bytes 4096 | tf_op jit(solution)/shard_map/depth_0/pallas_call | solution.py:95
  71.2 1.7 collective-permute-start.15
  72.9 1.4 collective-permute-start.14
  74.3 2.4 %slope.1.slope_ref = f32[512,1024]{1,0:T(8,128)S(1)} custom-call(s32[3]{0:T(128)S(1)} %pad_add_fusion.at_ref, bf16[320,1024]{1,0:T(8,128)(2,1)S(1)} %chip_sum.3.refs_0_, bf16[320,1024]{1,0:T(8,128)(2,1)S(1)} %collective-permute-done.10.refs_1_, bf16[192,1024]{1,0:T(8,128)(2,1)S(1)} %chip_sum.4.refs_2_, ...), custom_call_target="tpu_custom_call" | custom-call | bytes 4096 | tf_op jit(solution)/shard_map/slope/pallas_call | solution.py:95
  76.7 1.1 by_depth.1
  77.9 20.7 %collective-permute-done.14.got_ref = bf16[512,1024]{1,0:T(8,128)(2,1)S(1)} collective-permute-done((bf16[512,1024]{1,0:T(8,128)(2,1)S(1)}, bf16[512,1024]{1,0:T(8,128)(2,1)S(1)}, u32[]{:S(2)}, u32[]{:S(2)}) %collective-permute-start.14) | collective-permute-done | bytes 1048608 | tf_op jit(solution)/shard_map/ppermute | solution.py:59
  98.6 1.3 pre_grad.1
  100.5 2.2 %collective-permute-done.17.refs_3_ = f32[1,1024]{1,0:T(1,128)S(1)} collective-permute-done((f32[1,1024]{1,0:T(1,128)S(1)}, f32[1,1024]{1,0:T(1,128)S(1)}, u32[]{:S(2)}, u32[]{:S(2)}) %collective-permute-start.17) | collective-permute-done | bytes 4128 | tf_op jit(solution)/shard_map/ppermute | solution.py:59
  102.6 1.3 depth_0.5.refs_3_
  103.9 3.3 %collective-permute-start.19 = (bf16[528,1024]{1,0:T(8,128)(2,1)S(1)}, bf16[528,1024]{1,0:T(8,128)(2,1)S(1)}, u32[]{:S(2)}, u32[]{:S(2)}) collective-permute-start(bf16[528,1024]{1,0:T(8,128)(2,1)S(1)} %depth_0.5.refs_3_), channel_id=1, source_target_pairs={{0,1},{64,65},{8,9},{72,73},{16,17},{80,81},{24,25},{88,89},{32,33... | collective-permute-start | bytes 3244040 | tf_op jit(solution)/shard_map/ppermute | solution.py:59
  107.2 1.3 depth_1.3
  108.5 1.3 depth_0.4
  111.8 3.0 %inputs_grad.1 = (f32[512,1024]{1,0:T(8,128)S(1)}, bf16[256,1024]{1,0:T(8,128)(2,1)S(1)}) custom-call(s32[3]{0:T(128)S(1)} %pad_add_fusion.at_ref, bf16[512,1024]{1,0:T(8,128)(2,1)S(1)} %get-tuple-element.86.refs_1_.own_ref, bf16[512,1024]{1,0:T(8,128)(2,1)S(1)} %collective-permute-done.16.refs_1_.away_ref, bf16[1024,2048]{1,0:T(8,128)(2,1)S(1)} %get-tuple-element.49.w_ref), custom_call_target="tpu_custom_call" | custom-call | bytes 4096 | tf_op jit(solution)/shard_map/inputs_grad/pallas_call | solution.py:95
  114.9 12.6 %collective-permute-done.21 = bf16[256,1024]{1,0:T(8,128)(2,1)S(1)} collective-permute-done((bf16[256,1024]{1,0:T(8,128)(2,1)S(1)}, bf16[256,1024]{1,0:T(8,128)(2,1)S(1)}, u32[]{:S(2)}, u32[]{:S(2)}) %collective-permute-start.21) | collective-permute-done | bytes 524320 | tf_op jit(solution)/shard_map/ppermute | solution.py:59
  127.5 8.1 %collective-permute-done.18.refs_2_ = bf16[512,1024]{1,0:T(8,128)(2,1)S(1)} collective-permute-done((bf16[512,1024]{1,0:T(8,128)(2,1)S(1)}, bf16[512,1024]{1,0:T(8,128)(2,1)S(1)}, u32[]{:S(2)}, u32[]{:S(2)}) %collective-permute-start.18) | collective-permute-done | bytes 1048608 | tf_op jit(solution)/shard_map/ppermute | solution.py:59
  138.2 1.5 collective-permute-start.22
  139.8 1.1 depth_2.3
  141.6 3.6 %collective-permute-start.25 = (bf16[128,1024]{1,0:T(8,128)(2,1)S(1)}, bf16[128,1024]{1,0:T(8,128)(2,1)S(1)}, u32[]{:S(2)}, u32[]{:S(2)}) collective-permute-start(bf16[128,1024]{1,0:T(8,128)(2,1)S(1)} %add_convert_fusion), channel_id=1, source_target_pairs={{0,16},{64,80},{8,24},{72,88},{16,0},{80,64},{24,8},{88,72},{32,48... | collective-permute-start | bytes 786440 | tf_op jit(solution)/shard_map/ppermute | solution.py:59
  145.2 10.0 %collective-permute-done.25 = bf16[128,1024]{1,0:T(8,128)(2,1)S(1)} collective-permute-done((bf16[128,1024]{1,0:T(8,128)(2,1)S(1)}, bf16[128,1024]{1,0:T(8,128)(2,1)S(1)}, u32[]{:S(2)}, u32[]{:S(2)}) %collective-permute-start.25) | collective-permute-done | bytes 262176 | tf_op jit(solution)/shard_map/ppermute | solution.py:59
  155.7 4.8 %collective-permute-start.26 = (bf16[64,1024]{1,0:T(8,128)(2,1)S(1)}, bf16[64,1024]{1,0:T(8,128)(2,1)S(1)}, u32[]{:S(2)}, u32[]{:S(2)}) collective-permute-start(bf16[64,1024]{1,0:T(8,128)(2,1)S(1)} %add_convert_fusion.2), channel_id=1, source_target_pairs={{0,32},{64,96},{8,40},{72,104},{16,48},{80,112},{24,56},{88,120},{... | collective-permute-start | bytes 393224 | tf_op jit(solution)/shard_map/ppermute | solution.py:59
  161.4 1.6 collective-permute-start.28
  167.4 1.6 place_rows.1
  169.7 2.9 %collective-permute-done.27.got_ref = bf16[128,1024]{1,0:T(8,128)(2,1)S(1)} collective-permute-done((bf16[128,1024]{1,0:T(8,128)(2,1)S(1)}, bf16[128,1024]{1,0:T(8,128)(2,1)S(1)}, u32[]{:S(2)}, u32[]{:S(2)}) %collective-permute-start.27) | collective-permute-done | bytes 262176 | tf_op jit(solution)/shard_map/ppermute | solution.py:59
  172.6 1.7 place_columns.1
  (54 shorter events, 18.7 us)
Async XLA Ops:
  2.3 16.6 %collective-permute-start.3 = (bf16[128,1024]{1,0:T(8,128)(2,1)}, bf16[128,1024]{1,0:T(8,128)(2,1)S(1)}, u32[]{:S(2)}, u32[]{:S(2)}) collective-permute-start(bf16[128,1024]{1,0:T(8,128)(2,1)} %pack.1.refs_0_), channel_id=1, source_target_pairs={{0,8},{64,72},{8,16},{72,80},{16,24},{80,88},{24,32},{88,96},{32,4... | collective-permute-start | bytes 786440 | tf_op jit(solution)/shard_map/ppermute | solution.py:59
  4.3 21.2 %collective-permute-start.2 = (bf16[128,1024]{1,0:T(8,128)(2,1)}, bf16[128,1024]{1,0:T(8,128)(2,1)S(1)}, u32[]{:S(2)}, u32[]{:S(2)}) collective-permute-start(bf16[128,1024]{1,0:T(8,128)(2,1)} %pack.1.refs_0_), channel_id=1, source_target_pairs={{0,16},{64,80},{8,24},{72,88},{16,32},{80,96},{24,40},{88,104},{32... | collective-permute-start | bytes 786440 | tf_op jit(solution)/shard_map/ppermute | solution.py:59
  8.8 16.8 %collective-permute-start.1 = (bf16[128,1024]{1,0:T(8,128)(2,1)}, bf16[128,1024]{1,0:T(8,128)(2,1)S(1)}, u32[]{:S(2)}, u32[]{:S(2)}) collective-permute-start(bf16[128,1024]{1,0:T(8,128)(2,1)} %pack.1.refs_0_), channel_id=1, source_target_pairs={{0,48},{64,112},{8,56},{72,120},{16,0},{80,64},{24,8},{88,72},{32,... | collective-permute-start | bytes 786440 | tf_op jit(solution)/shard_map/ppermute | solution.py:59
  8.8 18.3 %collective-permute-start = (bf16[128,1024]{1,0:T(8,128)(2,1)}, bf16[128,1024]{1,0:T(8,128)(2,1)S(1)}, u32[]{:S(2)}, u32[]{:S(2)}) collective-permute-start(bf16[128,1024]{1,0:T(8,128)(2,1)} %pack.1.refs_0_), channel_id=1, source_target_pairs={{0,56},{64,120},{8,0},{72,64},{16,8},{80,72},{24,16},{88,80},{32,2... | collective-permute-start | bytes 786440 | tf_op jit(solution)/shard_map/ppermute | solution.py:59
  11.2 2.2 %copy-start = (bf16[2048,1024]{1,0:T(8,128)(2,1)S(1)}, bf16[2048,1024]{1,0:T(8,128)(2,1)}, u32[]{:S(2)}) copy-start(bf16[2048,1024]{1,0:T(8,128)(2,1)} %a_ref.5) | copy-start | bytes 12582916
  13.4 2.2 %copy-start.1 = (bf16[1024,2048]{1,0:T(8,128)(2,1)S(1)}, bf16[1024,2048]{1,0:T(8,128)(2,1)}, u32[]{:S(2)}) copy-start(bf16[1024,2048]{1,0:T(8,128)(2,1)} %a_ref.4) | copy-start | bytes 12582916
  15.6 11.5 %copy-start.2 = (bf16[128,1024]{1,0:T(8,128)(2,1)S(1)}, bf16[128,1024]{1,0:T(8,128)(2,1)}, u32[]{:S(2)}) copy-start(bf16[128,1024]{1,0:T(8,128)(2,1)} %pack.1.refs_0_) | copy-start | bytes 786436
  28.5 2.4 %collective-permute-start.4 = (bf16[320,1024]{1,0:T(8,128)(2,1)S(1)}, bf16[320,1024]{1,0:T(8,128)(2,1)S(1)}, u32[]{:S(2)}, u32[]{:S(2)}) collective-permute-start(bf16[320,1024]{1,0:T(8,128)(2,1)S(1)} %get-tuple-element.56), channel_id=1, source_target_pairs={{0,64},{64,0},{8,72},{72,8},{16,80},{80,16},{24,88},{88,24},{32,96... | collective-permute-start | bytes 1966088 | tf_op jit(solution)/shard_map/ppermute | solution.py:59
  28.6 17.9 %collective-permute-start.5 = (bf16[128,1024]{1,0:T(8,128)(2,1)S(1)}, bf16[128,1024]{1,0:T(8,128)(2,1)S(1)}, u32[]{:S(2)}, u32[]{:S(2)}) collective-permute-start(bf16[128,1024]{1,0:T(8,128)(2,1)S(1)} %collective-permute-done.1.refs_2_), channel_id=1, source_target_pairs={{0,56},{64,120},{8,0},{72,64},{16,8},{80,72},{24,16},{88,80},{32,2... | collective-permute-start | bytes 786440 | tf_op jit(solution)/shard_map/ppermute | solution.py:59
  29.7 16.8 %collective-permute-start.6 = (bf16[128,1024]{1,0:T(8,128)(2,1)S(1)}, bf16[128,1024]{1,0:T(8,128)(2,1)S(1)}, u32[]{:S(2)}, u32[]{:S(2)}) collective-permute-start(bf16[128,1024]{1,0:T(8,128)(2,1)S(1)} %collective-permute-done.2.refs_3_), channel_id=1, source_target_pairs={{0,8},{64,72},{8,16},{72,80},{16,24},{80,88},{24,32},{88,96},{32,4... | collective-permute-start | bytes 786440 | tf_op jit(solution)/shard_map/ppermute | solution.py:59
  32.3 17.8 %collective-permute-start.10 = (bf16[320,1024]{1,0:T(8,128)(2,1)S(1)}, bf16[320,1024]{1,0:T(8,128)(2,1)S(1)}, u32[]{:S(2)}, u32[]{:S(2)}) collective-permute-start(bf16[320,1024]{1,0:T(8,128)(2,1)S(1)} %chip_sum.3.refs_0_), channel_id=1, source_target_pairs={{0,128},{64,192},{8,136},{72,200},{16,144},{80,208},{24,152},{88,2... | collective-permute-start | bytes 1966088 | tf_op jit(solution)/shard_map/ppermute | solution.py:59
  33.9 12.5 %collective-permute-start.8 = (bf16[64,1024]{1,0:T(8,128)(2,1)S(1)}, bf16[64,1024]{1,0:T(8,128)(2,1)S(1)}, u32[]{:S(2)}, u32[]{:S(2)}) collective-permute-start(bf16[64,1024]{1,0:T(8,128)(2,1)S(1)} %slice.37), channel_id=1, source_target_pairs={{0,16},{64,80},{8,24},{72,88},{16,32},{80,96},{24,40},{88,104},{32... | collective-permute-start | bytes 393224 | tf_op jit(solution)/shard_map/ppermute | solution.py:59
  38.7 7.8 %collective-permute-start.7 = (bf16[64,1024]{1,0:T(8,128)(2,1)S(1)}, bf16[64,1024]{1,0:T(8,128)(2,1)S(1)}, u32[]{:S(2)}, u32[]{:S(2)}) collective-permute-start(bf16[64,1024]{1,0:T(8,128)(2,1)S(1)} %slice.36), channel_id=1, source_target_pairs={{0,48},{64,112},{8,56},{72,120},{16,0},{80,64},{24,8},{88,72},{32,... | collective-permute-start | bytes 393224 | tf_op jit(solution)/shard_map/ppermute | solution.py:59
  48.4 1.7 collective-permute-start.9
  53.1 2.7 %collective-permute-start.12 = (bf16[512,1024]{1,0:T(8,128)(2,1)S(1)}, bf16[512,1024]{1,0:T(8,128)(2,1)S(1)}, u32[]{:S(2)}, u32[]{:S(2)}) collective-permute-start(bf16[512,1024]{1,0:T(8,128)(2,1)S(1)} %grad_other.1), channel_id=1, source_target_pairs={{0,64},{64,0},{8,72},{72,8},{16,80},{80,16},{24,88},{88,24},{32,96... | collective-permute-start | bytes 3145736 | tf_op jit(solution)/shard_map/ppermute | solution.py:59
  53.3 11.4 %collective-permute-start.11 = (bf16[192,1024]{1,0:T(8,128)(2,1)S(1)}, bf16[192,1024]{1,0:T(8,128)(2,1)S(1)}, u32[]{:S(2)}, u32[]{:S(2)}) collective-permute-start(bf16[192,1024]{1,0:T(8,128)(2,1)S(1)} %chip_sum.4.refs_2_), channel_id=1, source_target_pairs={{0,128},{64,192},{8,136},{72,200},{16,144},{80,208},{24,152},{88,2... | collective-permute-start | bytes 1179656 | tf_op jit(solution)/shard_map/ppermute | solution.py:59
  66.6 2.7 %collective-permute-start.13 = (bf16[512,1024]{1,0:T(8,128)(2,1)S(1)}, bf16[512,1024]{1,0:T(8,128)(2,1)S(1)}, u32[]{:S(2)}, u32[]{:S(2)}) collective-permute-start(bf16[512,1024]{1,0:T(8,128)(2,1)S(1)} %act.1.refs_0_), channel_id=1, source_target_pairs={{0,64},{64,0},{8,72},{72,8},{16,80},{80,16},{24,88},{88,24},{32,96... | collective-permute-start | bytes 3145736 | tf_op jit(solution)/shard_map/ppermute | solution.py:59
  71.2 29.3 %collective-permute-start.15 = (bf16[1024,1024]{1,0:T(8,128)(2,1)S(1)}, bf16[1024,1024]{1,0:T(8,128)(2,1)S(1)}, u32[]{:S(2)}, u32[]{:S(2)}) collective-permute-start(bf16[1024,1024]{1,0:T(8,128)(2,1)S(1)} %depth_0.3), channel_id=1, source_target_pairs={{0,2},{64,70},{8,10},{72,78},{16,18},{80,86},{24,26},{88,94},{32,3... | collective-permute-start | bytes 6291464 | tf_op jit(solution)/shard_map/ppermute | solution.py:59
  72.9 25.7 %collective-permute-start.14 = (bf16[512,1024]{1,0:T(8,128)(2,1)S(1)}, bf16[512,1024]{1,0:T(8,128)(2,1)S(1)}, u32[]{:S(2)}, u32[]{:S(2)}) collective-permute-start(bf16[512,1024]{1,0:T(8,128)(2,1)S(1)} %chip_sum.5.chip_ref), channel_id=1, source_target_pairs={{0,128},{64,192},{8,136},{72,200},{16,144},{80,208},{24,152},{88,2... | collective-permute-start | bytes 3145736 | tf_op jit(solution)/shard_map/ppermute | solution.py:59
  99.9 2.8 %collective-permute-start.16 = (bf16[512,1024]{1,0:T(8,128)(2,1)S(1)}, bf16[512,1024]{1,0:T(8,128)(2,1)S(1)}, u32[]{:S(2)}, u32[]{:S(2)}) collective-permute-start(bf16[512,1024]{1,0:T(8,128)(2,1)S(1)} %get-tuple-element.86.refs_1_.own_ref), channel_id=1, source_target_pairs={{0,64},{64,0},{8,72},{72,8},{16,80},{80,16},{24,88},{88,24},{32,96... | collective-permute-start | bytes 3145736 | tf_op jit(solution)/shard_map/ppermute | solution.py:59
  100.1 2.5 %collective-permute-start.17 = (f32[1,1024]{1,0:T(1,128)S(1)}, f32[1,1024]{1,0:T(1,128)S(1)}, u32[]{:S(2)}, u32[]{:S(2)}) collective-permute-start(f32[1,1024]{1,0:T(1,128)S(1)} %get-tuple-element.74.refs_2_), channel_id=1, source_target_pairs={{0,64},{64,0},{8,72},{72,8},{16,80},{80,16},{24,88},{88,24},{32,96... | collective-permute-start | bytes 12296 | tf_op jit(solution)/shard_map/ppermute | solution.py:59
  103.9 32.1 %collective-permute-start.19 = (bf16[528,1024]{1,0:T(8,128)(2,1)S(1)}, bf16[528,1024]{1,0:T(8,128)(2,1)S(1)}, u32[]{:S(2)}, u32[]{:S(2)}) collective-permute-start(bf16[528,1024]{1,0:T(8,128)(2,1)S(1)} %depth_0.5.refs_3_), channel_id=1, source_target_pairs={{0,1},{64,65},{8,9},{72,73},{16,17},{80,81},{24,25},{88,89},{32,33... | collective-permute-start | bytes 3244040 | tf_op jit(solution)/shard_map/ppermute | solution.py:59
  109.8 25.7 %collective-permute-start.18 = (bf16[512,1024]{1,0:T(8,128)(2,1)S(1)}, bf16[512,1024]{1,0:T(8,128)(2,1)S(1)}, u32[]{:S(2)}, u32[]{:S(2)}) collective-permute-start(bf16[512,1024]{1,0:T(8,128)(2,1)S(1)} %depth_0.4), channel_id=1, source_target_pairs={{0,2},{64,70},{8,10},{72,78},{16,18},{80,86},{24,26},{88,94},{32,3... | collective-permute-start | bytes 3145736 | tf_op jit(solution)/shard_map/ppermute | solution.py:59
  110.7 25.4 %collective-permute-start.20 = (bf16[512,1024]{1,0:T(8,128)(2,1)S(1)}, bf16[512,1024]{1,0:T(8,128)(2,1)S(1)}, u32[]{:S(2)}, u32[]{:S(2)}) collective-permute-start(bf16[512,1024]{1,0:T(8,128)(2,1)S(1)} %depth_1.3), channel_id=1, source_target_pairs={{0,6},{64,66},{8,14},{72,74},{16,22},{80,82},{24,30},{88,90},{32,3... | collective-permute-start | bytes 3145736 | tf_op jit(solution)/shard_map/ppermute | solution.py:59
  114.8 12.7 %collective-permute-start.21 = (bf16[256,1024]{1,0:T(8,128)(2,1)S(1)}, bf16[256,1024]{1,0:T(8,128)(2,1)S(1)}, u32[]{:S(2)}, u32[]{:S(2)}) collective-permute-start(bf16[256,1024]{1,0:T(8,128)(2,1)S(1)} %get-tuple-element.78), channel_id=1, source_target_pairs={{0,8},{64,72},{8,0},{72,64},{16,24},{80,88},{24,16},{88,80},{32,40... | collective-permute-start | bytes 1572872 | tf_op jit(solution)/shard_map/ppermute | solution.py:59
  137.1 18.5 %collective-permute-start.23 = (bf16[272,1024]{1,0:T(8,128)(2,1)S(1)}, bf16[272,1024]{1,0:T(8,128)(2,1)S(1)}, u32[]{:S(2)}, u32[]{:S(2)}) collective-permute-start(bf16[272,1024]{1,0:T(8,128)(2,1)S(1)} %depth_1.5.refs_4_), channel_id=1, source_target_pairs={{0,2},{64,70},{8,10},{72,78},{16,18},{80,86},{24,26},{88,94},{32,3... | collective-permute-start | bytes 1671176 | tf_op jit(solution)/shard_map/ppermute | solution.py:59
  138.2 16.9 %collective-permute-start.22 = (bf16[256,1024]{1,0:T(8,128)(2,1)S(1)}, bf16[256,1024]{1,0:T(8,128)(2,1)S(1)}, u32[]{:S(2)}, u32[]{:S(2)}) collective-permute-start(bf16[256,1024]{1,0:T(8,128)(2,1)S(1)} %depth_1.4), channel_id=1, source_target_pairs={{0,6},{64,66},{8,14},{72,74},{16,22},{80,82},{24,30},{88,90},{32,3... | collective-permute-start | bytes 1572872 | tf_op jit(solution)/shard_map/ppermute | solution.py:59
  140.9 14.7 %collective-permute-start.24 = (bf16[256,1024]{1,0:T(8,128)(2,1)S(1)}, bf16[256,1024]{1,0:T(8,128)(2,1)S(1)}, u32[]{:S(2)}, u32[]{:S(2)}) collective-permute-start(bf16[256,1024]{1,0:T(8,128)(2,1)S(1)} %depth_2.3), channel_id=1, source_target_pairs={{0,1},{64,65},{8,9},{72,73},{16,17},{80,81},{24,25},{88,89},{32,33... | collective-permute-start | bytes 1572872 | tf_op jit(solution)/shard_map/ppermute | solution.py:59
  141.6 13.5 %collective-permute-start.25 = (bf16[128,1024]{1,0:T(8,128)(2,1)S(1)}, bf16[128,1024]{1,0:T(8,128)(2,1)S(1)}, u32[]{:S(2)}, u32[]{:S(2)}) collective-permute-start(bf16[128,1024]{1,0:T(8,128)(2,1)S(1)} %add_convert_fusion), channel_id=1, source_target_pairs={{0,16},{64,80},{8,24},{72,88},{16,0},{80,64},{24,8},{88,72},{32,48... | collective-permute-start | bytes 786440 | tf_op jit(solution)/shard_map/ppermute | solution.py:59
  155.7 13.3 %collective-permute-start.26 = (bf16[64,1024]{1,0:T(8,128)(2,1)S(1)}, bf16[64,1024]{1,0:T(8,128)(2,1)S(1)}, u32[]{:S(2)}, u32[]{:S(2)}) collective-permute-start(bf16[64,1024]{1,0:T(8,128)(2,1)S(1)} %add_convert_fusion.2), channel_id=1, source_target_pairs={{0,32},{64,96},{8,40},{72,104},{16,48},{80,112},{24,56},{88,120},{... | collective-permute-start | bytes 393224 | tf_op jit(solution)/shard_map/ppermute | solution.py:59
  161.4 11.2 %collective-permute-start.28 = (bf16[160,1024]{1,0:T(8,128)(2,1)S(1)}, bf16[160,1024]{1,0:T(8,128)(2,1)S(1)}, u32[]{:S(2)}, u32[]{:S(2)}) collective-permute-start(bf16[160,1024]{1,0:T(8,128)(2,1)S(1)} %depth_2.5.sent_ref), channel_id=1, source_target_pairs={{0,6},{64,66},{8,14},{72,74},{16,22},{80,82},{24,30},{88,90},{32,3... | collective-permute-start | bytes 983048 | tf_op jit(solution)/shard_map/ppermute | solution.py:59
  163.9 8.7 %collective-permute-start.27 = (bf16[128,1024]{1,0:T(8,128)(2,1)S(1)}, bf16[128,1024]{1,0:T(8,128)(2,1)S(1)}, u32[]{:S(2)}, u32[]{:S(2)}) collective-permute-start(bf16[128,1024]{1,0:T(8,128)(2,1)S(1)} %depth_2.4), channel_id=1, source_target_pairs={{0,1},{64,65},{8,9},{72,73},{16,17},{80,81},{24,25},{88,89},{32,33... | collective-permute-start | bytes 786440 | tf_op jit(solution)/shard_map/ppermute | solution.py:59

commit v3 on v2

--- a/solution.py
+++ b/solution.py
@@ -52,7 +52,10 @@
 Y_ONE = pairs_of(lambda x, y, z, c: (x, y ^ (3 if c else 1), z, c))
 Y_TWO = pairs_of(lambda x, y, z, c: (x, y ^ (1 if c else 3), z, c))
 Z = {k: pairs_of(lambda x, y, z, c, k=k: (x, y, z + k, c)) for k in (-2, -1, 1, 2)}
-Z_XOR = {k: pairs_of(lambda x, y, z, c, k=k: (x, y, z ^ k, c)) for k in (1, 2, 4)}
+Z_STEPS = [
+    pairs_of(lambda x, y, z, c, k=k: (x, y, z + (k if (z + c) % 2 == 0 else -k), c)) for k in (1, -1, 3)
+]
+Z_ORDER = (0, 3, 7, 4, 1, 6, 2, 5)
 
 
 def send(value, pairs):
@@ -295,23 +298,35 @@
     return local(functools.partial(gelu_kernel, slope), name, out, at, *near, *far, bias)
 
 
-def pre_grad_kernel(at_ref, slope_ref, chip_ref, got_ref, out_ref, sum_ref):
+def split(value):
+    high = value.astype(BF).astype(F32)
+    return jnp.concatenate([high, value - high], axis=0).astype(BF)
+
+
+def joined(ref, start):
+    return ref[start : start + 8, :].astype(F32) + ref[start + 8 : start + 16, :].astype(F32)
+
+
+def pre_grad_kernel(at_ref, slope_ref, chip_ref, got_ref, out_ref):
+    tokens = chip_ref.shape[0]
+    row = lax.broadcasted_iota(jnp.int32, (8, 128), 0)
     for b in range(8):
         here = slice(b * 128, b * 128 + 128)
         there = pl.ds(pl.multiple_of(order_of(b, at_ref) * 128, 128), 128)
         grad = chip_ref[:, here].astype(F32) + got_ref[:, here].astype(F32)
         value = (slope_ref[:, here] * grad).astype(BF)
-        out_ref[:, there] = value
-        sum_ref[:, there] = jnp.sum(value.astype(F32), axis=0, keepdims=True)
+        out_ref[:tokens, there] = value
+        total = jnp.sum(value.astype(F32), axis=0, keepdims=True)
+        out_ref[tokens:, there] = split(jnp.where(row == 0, total, 0.0))
 
 
 def pre_grad(at, slope, chip, got):
-    outs = [(slope.shape, BF), ((1, slope.shape[1]), F32)]
-    return local(pre_grad_kernel, "pre_grad", outs, at, slope, chip, got)
+    rows, cols = slope.shape
+    return local(pre_grad_kernel, "pre_grad", ((rows + 16, cols), BF), at, slope, chip, got)
 
 
 def by_depth_kernel(at_ref, a_ref, *outs):
-    for order, out in zip((Y_FIRST, X_FIRST), outs):
+    for order, out in zip((Y_FIRST[::-1], X_FIRST), outs):
         for i in range(8):
             at = pl.multiple_of(order_of(i, at_ref, order) * 128, 128)
             out[:, i * 128 : (i + 1) * 128] = a_ref[:, pl.ds(at, 128)]
@@ -325,88 +340,108 @@
 AWAY = (((256, 512), (768, 1024)), ((512, 768),), ((128, 256),), ((0, 128),))
 
 
-def split(value):
-    high = value.astype(BF).astype(F32)
-    return jnp.concatenate([high, value - high], axis=0).astype(BF)
-
-
-def joined(ref, start):
-    return ref[start : start + 8, :].astype(F32) + ref[start + 8 : start + 16, :].astype(F32)
-
-
 SIZES = (512, 256, 128, 128)
 
 
-def depth_kernel(level, sides, at_ref, *refs):
-    count = min(level, 2)
-    lefts, right_ref, refs = refs[: len(sides)], refs[len(sides)], refs[len(sides) + 1 :]
-    got_refs, refs, out_ref = refs[:count], refs[count:-1], refs[-1]
-    size = SIZES[level]
+def depth_part(plan, at_ref, refs, out_ref):
+    sides, level = plan["sides"], plan["level"]
+    lefts = [next(refs) for _ in sides]
+    right_ref = next(refs)
+    got_refs = [(next(refs), offset) for offset in plan["got"]]
+    size, base = SIZES[level], plan["base"]
     skip = 0 if level == 3 else size
     for s, (side, left_ref) in enumerate(zip(sides, lefts)):
         done = 0
         for start, stop in side[level]:
-            rows = slice(s * size + done, s * size + done + stop - start)
+            rows = slice(base + s * size + done, base + s * size + done + stop - start)
             for cols in tiles(out_ref.shape[1]):
-                value = dot_tn(left_ref[:, start:stop], right_ref[:, cols])
-                for i, got_ref in enumerate(got_refs):
-                    base = s * SIZES[i] + skip + done
-                    value = value + got_ref[base : base + stop - start, cols].astype(F32)
+                value = dot_tn(left_ref[:, start:stop], right_ref[: left_ref.shape[0], cols])
+                for i, (got_ref, offset) in enumerate(got_refs):
+                    at = offset + s * SIZES[i] + skip + done
+                    value = value + got_ref[at : at + stop - start, cols].astype(F32)
                 out_ref[rows, cols] = value.astype(out_ref.dtype)
             done += stop - start
-    if refs and level == 0:
-        own, away, cot_sum = refs
+    base += size * len(sides)
+    if plan["riders"] == "first":
+        own, away, cot_sum = next(refs), next(refs), next(refs)
         row = lax.broadcasted_iota(jnp.int32, (8, out_ref.shape[1]), 0)
         value = jnp.where(row == 2, cot_sum[...], 0.0)
-        value = jnp.where(row == at_ref[0], own[...], value)
-        value = jnp.where(row == 1 - at_ref[0], away[...], value)
-        out_ref[512:528, :] = split(value)
-    elif refs and level == 1:
-        out_ref[256:272, :] = split(joined(refs[0], 512) + joined(got_refs[0], 512))
-    elif refs and level == 2:
-        out_ref[128:144, :] = refs[0][256:272, :]
-        out_ref[144:160, :] = got_refs[1][256:272, :]
+        value = jnp.where(row == at_ref[0], joined(own, own.shape[0] - 16)[:1], value)
+        value = jnp.where(row == 1 - at_ref[0], joined(away, away.shape[0] - 16)[:1], value)
+        out_ref[base : base + 16, :] = split(value)
+    elif plan["riders"] is not None:
+        sent, got = next(refs), got_refs[-1]
+        here, there = plan["riders"] + SIZES[level - 1], got[1] + SIZES[level - 1]
+        if level == 1:
+            out_ref[base : base + 16, :] = split(joined(sent, here) + joined(got[0], there))
+        else:
+            out_ref[base : base + 16, :] = sent[here : here + 16, :]
+            out_ref[base + 16 : base + 32, :] = got[0][there : there + 16, :]
+
+
+def depth_kernel(plans, at_ref, *refs):
+    given = iter(refs[:-1])
+    for plan in plans:
+        depth_part(plan, at_ref, given, refs[-1])
 
 
 class DepthSum:
-    def __init__(self, at, sides, lefts, right, pairs, riders=()):
-        self.at, self.sides, self.lefts, self.right, self.pairs = at, sides, lefts, right, pairs
-        self.riders, self.got, self.sent = riders, [], []
-
-    def rows(self, level, dtype, riders):
-        size = SIZES[level] * len(self.sides) + (0, 16, 32)[bool(riders) + (bool(riders) and level == 2)]
-        kernel = functools.partial(depth_kernel, level, self.sides)
-        out = ((size, self.right.shape[1]), dtype)
-        got = self.got[: min(level, 2)]
-        return local(
-            kernel, f"depth_{level}", out, self.at, *self.lefts, self.right, *got, *riders
-        )
-
-    def exchange(self):
-        level = len(self.got)
-        riders = self.riders if level == 0 else self.sent[-1:] if self.riders else ()
-        self.sent.append(self.rows(level, BF, riders))
-        self.got.append(send(self.sent[-1], self.pairs[level]))
-
-    def kept_rows(self, *earlier):
+    def __init__(self, sides, lefts, right, riders=()):
+        self.sides, self.lefts, self.right, self.riders = sides, lefts, right, riders
+        self.sent, self.got = [], []
+
+    def plan(self, level, base):
+        got, riders, size = self.got[: min(level, 2)], None, SIZES[level] * len(self.sides)
+        given = [*self.lefts, self.right, *(message for message, _ in got)]
+        if self.riders and level < 3:
+            riders = self.sent[-1][1] if level else "first"
+            given += [self.sent[-1][0]] if level else self.riders
+            size += 32 if level == 2 else 16
+        offsets = [offset for _, offset in got]
+        return dict(sides=self.sides, level=level, got=offsets, riders=riders, base=base), given, size
+
+    def kept_rows(self, at, *earlier):
         self.right = after(self.right, *earlier)
-        return self.rows(3, F32, ())
+        plan, given, size = self.plan(3, 0)
+        out = ((size, self.right.shape[1]), F32)
+        return local(functools.partial(depth_kernel, [plan]), "depth_kept", out, at, *given)
+
+
+def exchange(at, parts, pairs):
+    plans, operands, base = [], [], 0
+    for part in parts:
+        plan, given, size = part.plan(len(part.got), base)
+        plans.append(plan)
+        operands += given
+        base += size
+    out = ((base, parts[0].right.shape[1]), BF)
+    message = local(functools.partial(depth_kernel, plans), "depth", out, at, *operands)
+    got = send(message, pairs)
+    for part, plan in zip(parts, plans):
+        part.sent.append((message, plan["base"]))
+        part.got.append((got, plan["base"]))
+    return message, got
+
+
+def arrived(parts, got):
+    for part in parts:
+        part.got[-1] = got, part.got[-1][1]
 
 
 def inputs_grad_kernel(at_ref, own_ref, away_ref, w_ref, out_ref, sent_ref):
-    n = out_ref.shape[0] // 8
-    width = own_ref.shape[1]
+    tokens, width = out_ref.shape[0], own_ref.shape[1]
+    n = tokens // 8
     for cols in tiles(out_ref.shape[1]):
-        value = dot_t(own_ref[...], w_ref[cols, :width]) + dot_t(away_ref[...], w_ref[cols, width:])
+        value = dot_t(own_ref[:tokens, :], w_ref[cols, :width])
+        value = value + dot_t(away_ref[:tokens, :], w_ref[cols, width:])
         for i, away in enumerate(AWAY_Z):
-            k = at_ref[2] ^ ((at_ref[2] + away) & 7)
-            place = ((k & 1) << 2) | (k & 2) | (k >> 2)
+            place = jnp.where((at_ref[2] + at_ref[0]) % 2 == 0, Z_ORDER.index(away % 8), Z_ORDER.index(-away % 8))
             out_ref[pl.ds(pl.multiple_of(place * n, n), n), cols] = value[i * n : (i + 1) * n]
     sent_ref[...] = out_ref[4 * n :, :].astype(BF)
 
 
 def inputs_grad(at, own, away, w_in):
-    rows, cols = own.shape[0], w_in.shape[0]
+    rows, cols = own.shape[0] - 16, w_in.shape[0]
     outs = [((rows, cols), F32), ((rows // 2, cols), BF)]
     return local(inputs_grad_kernel, "inputs_grad", outs, at, own, away, w_in)
 
@@ -423,7 +458,7 @@
     return local(kernel, "place_rows", (keep.shape, F32), at, keep, got)
 
 
-def columns_kernel(scale, at_ref, keep_ref, got_ref, keep2_ref, got2_ref, sent_ref, out_ref, bias_ref):
+def columns_kernel(scale, at_ref, keep_ref, got_ref, keep2_ref, got2_ref, sent_ref, out_ref, in_ref, bias_ref):
     for h, (k, g) in enumerate(((keep_ref, got_ref), (keep2_ref, got2_ref))):
         for i in range(8):
             at = pl.multiple_of((2 * i + (at_ref[0] ^ h)) * 128, 128)
@@ -437,14 +472,14 @@
     for i in range(8):
         cols = slice(i * 128, i * 128 + 128)
         for row in range(2):
-            bias_ref[2 * i + row : 2 * i + row + 1, :] = total[row : row + 1, cols]
-        bias_ref[16 + i : 17 + i, :] = total[2:3, cols]
+            in_ref[2 * i + row : 2 * i + row + 1, :] = total[row : row + 1, cols]
+        bias_ref[i : i + 1, :] = total[2:3, cols]
 
 
 def place_columns(at, scale, keep, got, keep2, got2, sent2):
     rows, cols = keep.shape
     kernel = functools.partial(columns_kernel, scale)
-    outs = [((rows, 2 * cols), F32), ((24, 128), F32)]
+    outs = [((rows, 2 * cols), F32), ((16, 128), F32), ((8, 128), F32)]
     return local(kernel, "place_columns", outs, at, keep, got, keep2, got2, sent2)
 
 
@@ -468,59 +503,55 @@
     terms, got_near = together(send(terms, CORE), got_near)
     chip_far = chip_sum(at, tok, w_in, terms, False)
     got_far = send(chip_far, NEAR)
-    terms = grad_other(at, after(cot, chip_far), w_out)
+    terms = grad_other(at, after(cot, got_far), w_out)
     chip_two = chip_sum(at, cot, w_out, send(terms, CORE), True)
     got_two = send(chip_two, NEAR)
-    got_far = after(got_far, chip_two)
     act = gelu(at, (chip_near, got_near), (chip_far, got_far), bias, 0)
     act_away = send(act, CORE)
 
-    out = DepthSum(at, (OWN, AWAY), (act, act_away), cot, (Y_ONE, Y_TWO, X_HI))
-    out.exchange()
+    out = DepthSum((OWN, AWAY), (act, act_away), cot)
+    _, got = exchange(at, [out], Y_ONE)
     bias = after(bias, act_away)
     slope = gelu(at, (chip_near, got_near), (chip_far, got_far), bias, 1)
     tok_one, tok_two = by_depth(at, after(tok, slope))
-    pg, db = pre_grad(at, after(slope, tok_one), chip_two, got_two)
+    pg = pre_grad(at, after(slope, tok_one), chip_two, got_two)
     pg_away = send(pg, CORE)
-    db_away = send(db, CORE)
-
-    out.got[0], tok_one, tok_two = together(out.got[0], tok_one, tok_two, pg)[:3]
-    out.exchange()
-    one = DepthSum(at, (OWN,), (after(tok_one, out.sent[1]),), pg, (Y_ONE, Y_TWO, X_HI))
-    one.exchange()
-    riders = db, db_away, cot_sum
-    two = DepthSum(at, (OWN,), (tok_two,), pg_away, (X_HI, Y_ONE, Y_TWO), riders)
-    two.exchange()
-    gi, gi_sent = inputs_grad(at, after(pg, one.sent[0], two.sent[0]), pg_away, w_in_plain)
-    gi_got = [send(gi_sent, Z_XOR[1])]
-
-    one.got[0], two.got[0], out.got[1], gi_got[0] = together(
-        one.got[0], two.got[0], out.got[1], gi_got[0]
-    )
-    one.exchange()
-    two.exchange()
-    out.exchange()
+
+    got, tok_one, tok_two, _ = together(got, tok_one, tok_two, pg)
+    arrived([out], got)
+    one = DepthSum((OWN,), (tok_one,), pg)
+    sent_one, got_one = exchange(at, [out, one], Y_TWO)
+    two = DepthSum((OWN,), (after(tok_two, sent_one),), pg_away, (pg, pg_away, cot_sum))
+    sent_two, got_two = exchange(at, [two], X_HI)
+    gi, gi_sent = inputs_grad(at, after(pg, sent_two), pg_away, w_in_plain)
+    gi_got = [send(gi_sent, Z_STEPS[0])]
     gi_sent = (gi[2 * n : 4 * n] + gi_got[0][2 * n :].astype(F32)).astype(BF)
-    gi_got.append(send(gi_sent, Z_XOR[2]))
-    out_kept = out.kept_rows(one.sent[1], two.sent[1], out.sent[2], gi_sent)
-
-    one.got[1], two.got[1], out.got[2], gi_got[1] = together(
-        one.got[1], two.got[1], out.got[2], gi_got[1]
-    )
-    one.exchange()
-    two.exchange()
+    gi_got.append(send(gi_sent, Z_STEPS[1]))
+
+    got_one, got_two, gi_got[1] = together(got_one, got_two, gi_got[1])
+    arrived([out, one], got_one)
+    arrived([two], got_two)
+    sent_one, got_one = exchange(at, [one, two], Y_ONE)
+    sent_two, got_two = exchange(at, [out], X_HI)
     gi_sent = gi[n : 2 * n] + gi_got[0][n : 2 * n].astype(F32) + gi_got[1][n:].astype(F32)
     gi_sent = gi_sent.astype(BF)
-    gi_got.append(send(gi_sent, Z_XOR[4]))
-    sent = one.sent[2], two.sent[2], gi_sent
-    one_kept, two_kept = one.kept_rows(*sent), two.kept_rows(*sent)
-    grad_w_out = place_rows(at, scale, after(out_kept, one_kept, two_kept), out.got[2])
+    gi_got.append(send(gi_sent, Z_STEPS[2]))
+    out_kept = out.kept_rows(at, sent_one, sent_two, gi_sent)
+
+    got_one, got_two, gi_got[2], out_kept = together(got_one, got_two, gi_got[2], out_kept)
+    arrived([one, two], got_one)
+    arrived([out], got_two)
+    sent_one, got_one = exchange(at, [one], X_HI)
+    sent_two, got_two = exchange(at, [two], Y_TWO)
+    sent = sent_one, sent_two
+    one_kept, two_kept = one.kept_rows(at, *sent), two.kept_rows(at, *sent)
+    grad_w_out = place_rows(at, scale, after(out_kept, one_kept, two_kept), out.got[2][0])
     gi = gi[:n] + sum(got[:n].astype(F32) for got in gi_got)
     grad_inputs = gi.astype(BF)
-    grad_w_in, db = place_columns(
-        at, scale, one_kept, one.got[2], two_kept, two.got[2], two.sent[2]
+    grad_w_in, db_in, db_out = place_columns(
+        at, scale, one_kept, got_one, two_kept, got_two, sent_two
     )
-    grad_b_in, grad_b_out = db[:16].reshape(-1), db[16:].reshape(-1)
+    grad_b_in, grad_b_out = db_in.reshape(-1), db_out.reshape(-1)
     return (grad_inputs, grad_w_in, grad_b_in, grad_w_out, grad_b_out)
 
 

time: 176 us -> 164 us (0.932)
  waiting for transfers between devices: 85.7 us -> 76.2 us
    ppermute x29 -> x26, waiting for transfers between devices: 85.7 us -> 76.2 us  [send(): return lax.ppermute(value, AXES, pairs)]
    pallas_call x26 -> x24, Pallas kernels: 36.5 us -> 35.6 us  [local(): pl.pallas_call(kernel, in_specs=[SCALARS] + [WHOLE] * len(arrays), out_sp...]
    ppermute x29 -> x26, starting transfers between devices: 40 us -> 39.5 us  [send(): return lax.ppermute(value, AXES, pairs)]
  transfers between devices with their start and end apart: 29 -> 26, of which waited for: 16 -> 14; matrix products, arithmetic and copies ran while one was open for 1% -> 1% of each run, Pallas kernels for 17% -> 19%
where the time goes in v3:
time: 164 us; the launch traced here: 163 us
  waiting for transfers between devices  76.2 us (46%)
  Pallas kernels  41.7 us (25%)
  starting transfers between devices  39.5 us (24%)
  local copies, waits for them, and re-layouts  4.01 us (2%)
    ppermute x26, waiting for transfers between devices, send(): return lax.ppermute(value, AXES, pairs)  76.2 us
    ppermute x26, starting transfers between devices, send(): return lax.ppermute(value, AXES, pairs)  39.5 us
    pallas_call x24, Pallas kernels, local(): pl.pallas_call(kernel, in_specs=[SCALARS] + [WHOLE] * len(arrays), out_sp...  35.6 us
    pallas_call x2, Pallas kernels, permute(): pl.pallas_call(functools.partial(permute_kernel, axis, orders), in_specs=...  4.46 us
    unnamed x6, local copies, waits for them, and re-layouts  3.3 us
  transfers between devices with their start and end apart: 26, of which 14 were waited for; matrix products, arithmetic and copies ran while one was open for 1% of the time, Pallas kernels for 19%

profile of v3, /device:TPU:32, one launch (start us, length us, event | category | flops | bytes accessed | tf_op | source)
XLA Modules:
  0.0 163.2 jit_solution(1961567155008025904)
XLA Ops:
  0.6 1.7 %pack.1.refs_0_ = bf16[128,1024]{1,0:T(8,128)(2,1)} custom-call(bf16[64,1024]{1,0:T(8,128)(2,1)} %a_ref.3, bf16[64,1024]{1,0:T(8,128)(2,1)} %b_ref.1), custom_call_target="tpu_custom_call" | custom-call | bytes 4096 | tf_op jit(solution)/shard_map/pack/pallas_call | solution.py:177
  2.3 2.0 %collective-permute-start.3 = (bf16[128,1024]{1,0:T(8,128)(2,1)}, bf16[128,1024]{1,0:T(8,128)(2,1)S(1)}, u32[]{:S(2)}, u32[]{:S(2)}) collective-permute-start(bf16[128,1024]{1,0:T(8,128)(2,1)} %pack.1.refs_0_), channel_id=1, source_target_pairs={{0,8},{64,72},{8,16},{72,80},{16,24},{80,88},{24,32},{88,96},{32,4... | collective-permute-start | bytes 786440 | tf_op jit(solution)/shard_map/ppermute | solution.py:62
  4.3 4.5 %collective-permute-start.2 = (bf16[128,1024]{1,0:T(8,128)(2,1)}, bf16[128,1024]{1,0:T(8,128)(2,1)S(1)}, u32[]{:S(2)}, u32[]{:S(2)}) collective-permute-start(bf16[128,1024]{1,0:T(8,128)(2,1)} %pack.1.refs_0_), channel_id=1, source_target_pairs={{0,16},{64,80},{8,24},{72,88},{16,32},{80,96},{24,40},{88,104},{32... | collective-permute-start | bytes 786440 | tf_op jit(solution)/shard_map/ppermute | solution.py:62
  11.2 2.2 %copy-done = bf16[2048,1024]{1,0:T(8,128)(2,1)S(1)} copy-done((bf16[2048,1024]{1,0:T(8,128)(2,1)S(1)}, bf16[2048,1024]{1,0:T(8,128)(2,1)}, u32[]{:S(2)}) %copy-start) | copy-done | bytes 4194328
  14.4 1.1 copy-done.1
  15.6 3.4 %permute_1.1 = (bf16[1024,2048]{1,0:T(8,128)(2,1)S(1)}, bf16[1024,2048]{1,0:T(8,128)(2,1)S(1)}) custom-call(s32[3]{0:T(128)S(1)} %pad_add_fusion.at_ref, bf16[1024,2048]{1,0:T(8,128)(2,1)S(1)} %copy-done.1), custom_call_target="tpu_custom_call" | custom-call | bytes 4096 | tf_op jit(solution)/shard_map/permute_1/pallas_call | solution.py:142
  19.0 6.6 %collective-permute-done.2.refs_3_ = bf16[128,1024]{1,0:T(8,128)(2,1)S(1)} collective-permute-done((bf16[128,1024]{1,0:T(8,128)(2,1)}, bf16[128,1024]{1,0:T(8,128)(2,1)S(1)}, u32[]{:S(2)}, u32[]{:S(2)}) %collective-permute-start.2) | collective-permute-done | bytes 262176 | tf_op jit(solution)/shard_map/ppermute | solution.py:62
  25.6 1.5 collective-permute-done.refs_1_
  27.1 1.4 arrange_near.1
  28.6 1.1 collective-permute-start.5
  29.7 1.2 collective-permute-start.6
  30.9 1.4 chip_sum.3.refs_0_
  32.3 1.6 collective-permute-start.10
  33.9 4.8 %collective-permute-start.8 = (bf16[64,1024]{1,0:T(8,128)(2,1)S(1)}, bf16[64,1024]{1,0:T(8,128)(2,1)S(1)}, u32[]{:S(2)}, u32[]{:S(2)}) collective-permute-start(bf16[64,1024]{1,0:T(8,128)(2,1)S(1)} %slice.31), channel_id=1, source_target_pairs={{0,16},{64,80},{8,24},{72,88},{16,32},{80,96},{24,40},{88,104},{32... | collective-permute-start | bytes 393224 | tf_op jit(solution)/shard_map/ppermute | solution.py:62
  38.8 7.7 %collective-permute-done.8.refs_8_ = bf16[64,1024]{1,0:T(8,128)(2,1)S(1)} collective-permute-done((bf16[64,1024]{1,0:T(8,128)(2,1)S(1)}, bf16[64,1024]{1,0:T(8,128)(2,1)S(1)}, u32[]{:S(2)}, u32[]{:S(2)}) %collective-permute-start.8) | collective-permute-done | bytes 131104 | tf_op jit(solution)/shard_map/ppermute | solution.py:62
  46.5 1.9 %arrange_far.1 = (bf16[512,1024]{1,0:T(8,128)(2,1)S(1)}, bf16[512,1024]{1,0:T(8,128)(2,1)S(1)}, bf16[192,1024]{1,0:T(8,128)(2,1)S(1)}, f32[8,1024]{1,0:T(8,128)}, f32[1,1024]{1,0:T(1,128)S(1)}) custom-call(s32[3]{0:T(128)S(1)} %pad_add_fusion.at_ref, bf16[320,1024]{1,0:T(8,128)(2,1)S(1)} %get-tuple-element.52.a_ref.tok_ref, bf16[128,1024]{1,0:T(8,128)(2,1)S(1)} %copy-done.2, ...), custom_call_target="tpu_custom_call" | custom-call | bytes 4096 | tf_op jit(solution)/shard_map/arrange_far/pallas_call | solution.py:98
  48.4 1.7 %collective-permute-done.9.got_ref = bf16[192,1024]{1,0:T(8,128)(2,1)S(1)} collective-permute-done((bf16[192,1024]{1,0:T(8,128)(2,1)S(1)}, bf16[192,1024]{1,0:T(8,128)(2,1)S(1)}, u32[]{:S(2)}, u32[]{:S(2)}) %collective-permute-start.9) | collective-permute-done | bytes 393248 | tf_op jit(solution)/shard_map/ppermute | solution.py:62
  50.2 1.1 chip_sum.4.refs_2_
  51.3 1.5 collective-permute-start.11
  52.8 9.7 %collective-permute-done.11.refs_3_ = bf16[192,1024]{1,0:T(8,128)(2,1)S(1)} collective-permute-done((bf16[192,1024]{1,0:T(8,128)(2,1)S(1)}, bf16[192,1024]{1,0:T(8,128)(2,1)S(1)}, u32[]{:S(2)}, u32[]{:S(2)}) %collective-permute-start.11) | collective-permute-done | bytes 393248 | tf_op jit(solution)/shard_map/ppermute | solution.py:62
  62.5 1.8 %act.1.refs_0_ = bf16[512,1024]{1,0:T(8,128)(2,1)S(1)} custom-call(s32[3]{0:T(128)S(1)} %pad_add_fusion.at_ref, bf16[320,1024]{1,0:T(8,128)(2,1)S(1)} %chip_sum.3.refs_0_, bf16[320,1024]{1,0:T(8,128)(2,1)S(1)} %collective-permute-done.10.refs_1_, bf16[192,1024]{1,0:T(8,128)(2,1)S(1)} %chip_sum.4.refs_2_, ...), custom_call_target="tpu_custom_call" | custom-call | bytes 4096 | tf_op jit(solution)/shard_map/act/pallas_call | solution.py:98
  64.5 1.8 %grad_other.1 = bf16[512,1024]{1,0:T(8,128)(2,1)S(1)} custom-call(s32[3]{0:T(128)S(1)} %pad_add_fusion.at_ref, bf16[512,1024]{1,0:T(8,128)(2,1)S(1)} %get-tuple-element.76.cot_ref.a_ref.refs_2_, bf16[2048,1024]{1,0:T(8,128)(2,1)S(1)} %permute_0.1.w_ref), custom_call_target="tpu_custom_call" | custom-call | bytes 4096 | tf_op jit(solution)/shard_map/grad_other/pallas_call | solution.py:98
  67.1 1.8 %depth.7 = bf16[1024,1024]{1,0:T(8,128)(2,1)S(1)} custom-call(s32[3]{0:T(128)S(1)} %pad_add_fusion.at_ref, bf16[512,1024]{1,0:T(8,128)(2,1)S(1)} %act.1.refs_0_, bf16[512,1024]{1,0:T(8,128)(2,1)S(1)} %collective-permute-done.12.refs_1_, bf16[512,1024]{1,0:T(8,128)(2,1)S(1)} %get-tuple-element.76.cot_ref.a_ref.refs_2_), custom_call_target="tpu_custom_call" | custom-call | bytes 4096 | tf_op jit(solution)/shard_map/depth/pallas_call | solution.py:98
  69.0 1.7 %collective-permute-start.15 = (bf16[1024,1024]{1,0:T(8,128)(2,1)S(1)}, bf16[1024,1024]{1,0:T(8,128)(2,1)S(1)}, u32[]{:S(2)}, u32[]{:S(2)}) collective-permute-start(bf16[1024,1024]{1,0:T(8,128)(2,1)S(1)} %depth.7), channel_id=1, source_target_pairs={{0,2},{64,70},{8,10},{72,78},{16,18},{80,86},{24,26},{88,94},{32,3... | collective-permute-start | bytes 6291464 | tf_op jit(solution)/shard_map/ppermute | solution.py:62
  70.7 1.8 %chip_sum.5.chip_ref = bf16[512,1024]{1,0:T(8,128)(2,1)S(1)} custom-call(s32[3]{0:T(128)S(1)} %pad_add_fusion.at_ref, bf16[512,1024]{1,0:T(8,128)(2,1)S(1)} %get-tuple-element.76.cot_ref.a_ref.refs_2_, bf16[2048,1024]{1,0:T(8,128)(2,1)S(1)} %permute_0.1.w_ref, bf16[512,1024]{1,0:T(8,128)(2,1)S(1)} %collective-permute-done.13.got_ref), custom_call_target="tpu_custom_call" | custom-call | bytes 4096 | tf_op jit(solution)/shard_map/chip_sum/pallas_call | solution.py:98
  72.5 1.5 collective-permute-start.14
  74.0 2.4 %slope.1.slope_ref = f32[512,1024]{1,0:T(8,128)S(1)} custom-call(s32[3]{0:T(128)S(1)} %pad_add_fusion.at_ref, bf16[320,1024]{1,0:T(8,128)(2,1)S(1)} %chip_sum.3.refs_0_, bf16[320,1024]{1,0:T(8,128)(2,1)S(1)} %collective-permute-done.10.refs_1_, bf16[192,1024]{1,0:T(8,128)(2,1)S(1)} %chip_sum.4.refs_2_, ...), custom_call_target="tpu_custom_call" | custom-call | bytes 4096 | tf_op jit(solution)/shard_map/slope/pallas_call | solution.py:98
  76.5 1.1 by_depth.1
  77.6 20.7 %collective-permute-done.14.got_ref = bf16[512,1024]{1,0:T(8,128)(2,1)S(1)} collective-permute-done((bf16[512,1024]{1,0:T(8,128)(2,1)S(1)}, bf16[512,1024]{1,0:T(8,128)(2,1)S(1)}, u32[]{:S(2)}, u32[]{:S(2)}) %collective-permute-start.14) | collective-permute-done | bytes 1048608 | tf_op jit(solution)/shard_map/ppermute | solution.py:62
  98.3 1.8 %pre_grad.1.refs_5_.refs_2_.own_ref.refs_1_ = bf16[528,1024]{1,0:T(8,128)(2,1)S(1)} custom-call(s32[3]{0:T(128)S(1)} %pad_add_fusion.at_ref, f32[512,1024]{1,0:T(8,128)S(1)} %slope.1.slope_ref, bf16[512,1024]{1,0:T(8,128)(2,1)S(1)} %chip_sum.5.chip_ref, bf16[512,1024]{1,0:T(8,128)(2,1)S(1)} %collective-permute-done.14.got_ref), custom_call_target="tpu_custom_call" | custom-call | bytes 4096 | tf_op jit(solution)/shard_map/pre_grad/pallas_call | solution.py:98
  100.4 1.9 %depth.8 = bf16[1024,1024]{1,0:T(8,128)(2,1)S(1)} custom-call(s32[3]{0:T(128)S(1)} %pad_add_fusion.at_ref, bf16[512,1024]{1,0:T(8,128)(2,1)S(1)} %act.1.refs_0_, bf16[512,1024]{1,0:T(8,128)(2,1)S(1)} %collective-permute-done.12.refs_1_, bf16[512,1024]{1,0:T(8,128)(2,1)S(1)} %get-tuple-element.76.cot_ref.a_ref.refs_2_, ...), custom_call_target="tpu_custom_call" | custom-call | bytes 4096 | tf_op jit(solution)/shard_map/depth/pallas_call | solution.py:98
  102.2 1.5 collective-permute-start.18
  103.7 1.3 depth.9.refs_6_
  105.0 3.1 %collective-permute-start.19 = (bf16[528,1024]{1,0:T(8,128)(2,1)S(1)}, bf16[528,1024]{1,0:T(8,128)(2,1)S(1)}, u32[]{:S(2)}, u32[]{:S(2)}) collective-permute-start(bf16[528,1024]{1,0:T(8,128)(2,1)S(1)} %depth.9.refs_6_), channel_id=1, source_target_pairs={{0,1},{64,65},{8,9},{72,73},{16,17},{80,81},{24,25},{88,89},{32,33... | collective-permute-start | bytes 3244040 | tf_op jit(solution)/shard_map/ppermute | solution.py:62
  108.0 3.0 %inputs_grad.1 = (f32[512,1024]{1,0:T(8,128)S(1)}, bf16[256,1024]{1,0:T(8,128)(2,1)S(1)}) custom-call(s32[3]{0:T(128)S(1)} %pad_add_fusion.at_ref, bf16[528,1024]{1,0:T(8,128)(2,1)S(1)} %pre_grad.1.refs_5_.refs_2_.own_ref.refs_1_, bf16[528,1024]{1,0:T(8,128)(2,1)S(1)} %collective-permute-done.16.refs_1_.refs_3_.away_ref.refs_4_, ...), custom_call_target="tpu_custom_call" | custom-call | bytes 4096 | tf_op jit(solution)/shard_map/inputs_grad/pallas_call | solution.py:98
  111.2 9.2 %collective-permute-done.17 = bf16[256,1024]{1,0:T(8,128)(2,1)S(1)} collective-permute-done((bf16[256,1024]{1,0:T(8,128)(2,1)S(1)}, bf16[256,1024]{1,0:T(8,128)(2,1)S(1)}, u32[]{:S(2)}, u32[]{:S(2)}) %collective-permute-start.17) | collective-permute-done | bytes 524320 | tf_op jit(solution)/shard_map/ppermute | solution.py:62
  120.4 2.0 %collective-permute-start.20 = (bf16[128,1024]{1,0:T(8,128)(2,1)S(1)}, bf16[128,1024]{1,0:T(8,128)(2,1)S(1)}, u32[]{:S(2)}, u32[]{:S(2)}) collective-permute-start(bf16[128,1024]{1,0:T(8,128)(2,1)S(1)} %add_convert_fusion), channel_id=1, source_target_pairs={{0,56},{64,72},{8,16},{72,64},{16,8},{80,88},{24,32},{88,80},{32,2... | collective-permute-start | bytes 786440 | tf_op jit(solution)/shard_map/ppermute | solution.py:62
  122.4 4.5 %collective-permute-done.20 = bf16[128,1024]{1,0:T(8,128)(2,1)S(1)} collective-permute-done((bf16[128,1024]{1,0:T(8,128)(2,1)S(1)}, bf16[128,1024]{1,0:T(8,128)(2,1)S(1)}, u32[]{:S(2)}, u32[]{:S(2)}) %collective-permute-start.20) | collective-permute-done | bytes 262176 | tf_op jit(solution)/shard_map/ppermute | solution.py:62
  126.9 5.1 %collective-permute-done.19.refs_5_.refs_2_ = bf16[528,1024]{1,0:T(8,128)(2,1)S(1)} collective-permute-done((bf16[528,1024]{1,0:T(8,128)(2,1)S(1)}, bf16[528,1024]{1,0:T(8,128)(2,1)S(1)}, u32[]{:S(2)}, u32[]{:S(2)}) %collective-permute-start.19) | collective-permute-done | bytes 1081376 | tf_op jit(solution)/shard_map/ppermute | solution.py:62
  132.0 1.3 depth.10.refs_4_
  133.3 1.4 collective-permute-start.21
  134.7 1.1 depth.11
  135.8 3.1 %collective-permute-start.22 = (bf16[256,1024]{1,0:T(8,128)(2,1)S(1)}, bf16[256,1024]{1,0:T(8,128)(2,1)S(1)}, u32[]{:S(2)}, u32[]{:S(2)}) collective-permute-start(bf16[256,1024]{1,0:T(8,128)(2,1)S(1)} %depth.11), channel_id=1, source_target_pairs={{0,1},{64,65},{8,9},{72,73},{16,17},{80,81},{24,25},{88,89},{32,33... | collective-permute-start | bytes 1572872 | tf_op jit(solution)/shard_map/ppermute | solution.py:62
  140.5 7.8 %collective-permute-done.23 = bf16[64,1024]{1,0:T(8,128)(2,1)S(1)} collective-permute-done((bf16[64,1024]{1,0:T(8,128)(2,1)S(1)}, bf16[64,1024]{1,0:T(8,128)(2,1)S(1)}, u32[]{:S(2)}, u32[]{:S(2)}) %collective-permute-start.23) | collective-permute-done | bytes 131104 | tf_op jit(solution)/shard_map/ppermute | solution.py:62
  149.8 2.8 %collective-permute-start.25 = (bf16[160,1024]{1,0:T(8,128)(2,1)S(1)}, bf16[160,1024]{1,0:T(8,128)(2,1)S(1)}, u32[]{:S(2)}, u32[]{:S(2)}) collective-permute-start(bf16[160,1024]{1,0:T(8,128)(2,1)S(1)} %depth.13.sent_ref), channel_id=1, source_target_pairs={{0,6},{64,66},{8,14},{72,74},{16,22},{80,82},{24,30},{88,90},{32,3... | collective-permute-start | bytes 983048 | tf_op jit(solution)/shard_map/ppermute | solution.py:62
  153.5 3.2 %collective-permute-start.24 = (bf16[128,1024]{1,0:T(8,128)(2,1)S(1)}, bf16[128,1024]{1,0:T(8,128)(2,1)S(1)}, u32[]{:S(2)}, u32[]{:S(2)}) collective-permute-start(bf16[128,1024]{1,0:T(8,128)(2,1)S(1)} %depth.12), channel_id=1, source_target_pairs={{0,1},{64,65},{8,9},{72,73},{16,17},{80,81},{24,25},{88,89},{32,33... | collective-permute-start | bytes 786440 | tf_op jit(solution)/shard_map/ppermute | solution.py:62
  158.5 1.6 place_rows.1
  161.5 1.7 %place_columns.1 = (f32[128,2048]{1,0:T(8,128)}, f32[16,128]{1,0:T(8,128)}, f32[8,128]{1,0:T(8,128)}) custom-call(s32[3]{0:T(128)S(1)} %pad_add_fusion.at_ref, f32[128,1024]{1,0:T(8,128)S(1)} %depth_kept.4.keep_ref, bf16[128,1024]{1,0:T(8,128)(2,1)S(1)} %collective-permute-done.24.got_ref, f32[128,1024]{1,0:T(8,128)S(1)} %depth_kept.5.keep2_ref, ...), custom_call_target="tpu_custom_call" | custom-call | bytes 4096 | tf_op jit(solution)/shard_map/place_columns/pallas_call | solution.py:98
  (44 shorter events, 12.1 us)
Async XLA Ops:
  2.3 16.6 %collective-permute-start.3 = (bf16[128,1024]{1,0:T(8,128)(2,1)}, bf16[128,1024]{1,0:T(8,128)(2,1)S(1)}, u32[]{:S(2)}, u32[]{:S(2)}) collective-permute-start(bf16[128,1024]{1,0:T(8,128)(2,1)} %pack.1.refs_0_), channel_id=1, source_target_pairs={{0,8},{64,72},{8,16},{72,80},{16,24},{80,88},{24,32},{88,96},{32,4... | collective-permute-start | bytes 786440 | tf_op jit(solution)/shard_map/ppermute | solution.py:62
  4.3 21.2 %collective-permute-start.2 = (bf16[128,1024]{1,0:T(8,128)(2,1)}, bf16[128,1024]{1,0:T(8,128)(2,1)S(1)}, u32[]{:S(2)}, u32[]{:S(2)}) collective-permute-start(bf16[128,1024]{1,0:T(8,128)(2,1)} %pack.1.refs_0_), channel_id=1, source_target_pairs={{0,16},{64,80},{8,24},{72,88},{16,32},{80,96},{24,40},{88,104},{32... | collective-permute-start | bytes 786440 | tf_op jit(solution)/shard_map/ppermute | solution.py:62
  8.8 16.8 %collective-permute-start.1 = (bf16[128,1024]{1,0:T(8,128)(2,1)}, bf16[128,1024]{1,0:T(8,128)(2,1)S(1)}, u32[]{:S(2)}, u32[]{:S(2)}) collective-permute-start(bf16[128,1024]{1,0:T(8,128)(2,1)} %pack.1.refs_0_), channel_id=1, source_target_pairs={{0,48},{64,112},{8,56},{72,120},{16,0},{80,64},{24,8},{88,72},{32,... | collective-permute-start | bytes 786440 | tf_op jit(solution)/shard_map/ppermute | solution.py:62
  8.8 18.3 %collective-permute-start = (bf16[128,1024]{1,0:T(8,128)(2,1)}, bf16[128,1024]{1,0:T(8,128)(2,1)S(1)}, u32[]{:S(2)}, u32[]{:S(2)}) collective-permute-start(bf16[128,1024]{1,0:T(8,128)(2,1)} %pack.1.refs_0_), channel_id=1, source_target_pairs={{0,56},{64,120},{8,0},{72,64},{16,8},{80,72},{24,16},{88,80},{32,2... | collective-permute-start | bytes 786440 | tf_op jit(solution)/shard_map/ppermute | solution.py:62
  11.2 2.2 %copy-start = (bf16[2048,1024]{1,0:T(8,128)(2,1)S(1)}, bf16[2048,1024]{1,0:T(8,128)(2,1)}, u32[]{:S(2)}) copy-start(bf16[2048,1024]{1,0:T(8,128)(2,1)} %a_ref.5) | copy-start | bytes 12582916
  13.4 2.2 %copy-start.1 = (bf16[1024,2048]{1,0:T(8,128)(2,1)S(1)}, bf16[1024,2048]{1,0:T(8,128)(2,1)}, u32[]{:S(2)}) copy-start(bf16[1024,2048]{1,0:T(8,128)(2,1)} %a_ref.4) | copy-start | bytes 12582916
  15.6 11.5 %copy-start.2 = (bf16[128,1024]{1,0:T(8,128)(2,1)S(1)}, bf16[128,1024]{1,0:T(8,128)(2,1)}, u32[]{:S(2)}) copy-start(bf16[128,1024]{1,0:T(8,128)(2,1)} %pack.1.refs_0_) | copy-start | bytes 786436
  28.5 2.4 %collective-permute-start.4 = (bf16[320,1024]{1,0:T(8,128)(2,1)S(1)}, bf16[320,1024]{1,0:T(8,128)(2,1)S(1)}, u32[]{:S(2)}, u32[]{:S(2)}) collective-permute-start(bf16[320,1024]{1,0:T(8,128)(2,1)S(1)} %get-tuple-element.53), channel_id=1, source_target_pairs={{0,64},{64,0},{8,72},{72,8},{16,80},{80,16},{24,88},{88,24},{32,96... | collective-permute-start | bytes 1966088 | tf_op jit(solution)/shard_map/ppermute | solution.py:62
  28.6 17.9 %collective-permute-start.5 = (bf16[128,1024]{1,0:T(8,128)(2,1)S(1)}, bf16[128,1024]{1,0:T(8,128)(2,1)S(1)}, u32[]{:S(2)}, u32[]{:S(2)}) collective-permute-start(bf16[128,1024]{1,0:T(8,128)(2,1)S(1)} %collective-permute-done.1.refs_2_), channel_id=1, source_target_pairs={{0,56},{64,120},{8,0},{72,64},{16,8},{80,72},{24,16},{88,80},{32,2... | collective-permute-start | bytes 786440 | tf_op jit(solution)/shard_map/ppermute | solution.py:62
  29.7 16.8 %collective-permute-start.6 = (bf16[128,1024]{1,0:T(8,128)(2,1)S(1)}, bf16[128,1024]{1,0:T(8,128)(2,1)S(1)}, u32[]{:S(2)}, u32[]{:S(2)}) collective-permute-start(bf16[128,1024]{1,0:T(8,128)(2,1)S(1)} %collective-permute-done.2.refs_3_), channel_id=1, source_target_pairs={{0,8},{64,72},{8,16},{72,80},{16,24},{80,88},{24,32},{88,96},{32,4... | collective-permute-start | bytes 786440 | tf_op jit(solution)/shard_map/ppermute | solution.py:62
  32.3 17.8 %collective-permute-start.10 = (bf16[320,1024]{1,0:T(8,128)(2,1)S(1)}, bf16[320,1024]{1,0:T(8,128)(2,1)S(1)}, u32[]{:S(2)}, u32[]{:S(2)}) collective-permute-start(bf16[320,1024]{1,0:T(8,128)(2,1)S(1)} %chip_sum.3.refs_0_), channel_id=1, source_target_pairs={{0,128},{64,192},{8,136},{72,200},{16,144},{80,208},{24,152},{88,2... | collective-permute-start | bytes 1966088 | tf_op jit(solution)/shard_map/ppermute | solution.py:62
  33.9 12.5 %collective-permute-start.8 = (bf16[64,1024]{1,0:T(8,128)(2,1)S(1)}, bf16[64,1024]{1,0:T(8,128)(2,1)S(1)}, u32[]{:S(2)}, u32[]{:S(2)}) collective-permute-start(bf16[64,1024]{1,0:T(8,128)(2,1)S(1)} %slice.31), channel_id=1, source_target_pairs={{0,16},{64,80},{8,24},{72,88},{16,32},{80,96},{24,40},{88,104},{32... | collective-permute-start | bytes 393224 | tf_op jit(solution)/shard_map/ppermute | solution.py:62
  38.7 7.8 %collective-permute-start.7 = (bf16[64,1024]{1,0:T(8,128)(2,1)S(1)}, bf16[64,1024]{1,0:T(8,128)(2,1)S(1)}, u32[]{:S(2)}, u32[]{:S(2)}) collective-permute-start(bf16[64,1024]{1,0:T(8,128)(2,1)S(1)} %slice.30), channel_id=1, source_target_pairs={{0,48},{64,112},{8,56},{72,120},{16,0},{80,64},{24,8},{88,72},{32,... | collective-permute-start | bytes 393224 | tf_op jit(solution)/shard_map/ppermute | solution.py:62
  48.4 1.7 %collective-permute-start.9 = (bf16[192,1024]{1,0:T(8,128)(2,1)S(1)}, bf16[192,1024]{1,0:T(8,128)(2,1)S(1)}, u32[]{:S(2)}, u32[]{:S(2)}) collective-permute-start(bf16[192,1024]{1,0:T(8,128)(2,1)S(1)} %get-tuple-element.54), channel_id=1, source_target_pairs={{0,64},{64,0},{8,72},{72,8},{16,80},{80,16},{24,88},{88,24},{32,96... | collective-permute-start | bytes 1179656 | tf_op jit(solution)/shard_map/ppermute | solution.py:62
  51.3 11.2 %collective-permute-start.11 = (bf16[192,1024]{1,0:T(8,128)(2,1)S(1)}, bf16[192,1024]{1,0:T(8,128)(2,1)S(1)}, u32[]{:S(2)}, u32[]{:S(2)}) collective-permute-start(bf16[192,1024]{1,0:T(8,128)(2,1)S(1)} %chip_sum.4.refs_2_), channel_id=1, source_target_pairs={{0,128},{64,192},{8,136},{72,200},{16,144},{80,208},{24,152},{88,2... | collective-permute-start | bytes 1179656 | tf_op jit(solution)/shard_map/ppermute | solution.py:62
  64.4 2.7 %collective-permute-start.12 = (bf16[512,1024]{1,0:T(8,128)(2,1)S(1)}, bf16[512,1024]{1,0:T(8,128)(2,1)S(1)}, u32[]{:S(2)}, u32[]{:S(2)}) collective-permute-start(bf16[512,1024]{1,0:T(8,128)(2,1)S(1)} %act.1.refs_0_), channel_id=1, source_target_pairs={{0,64},{64,0},{8,72},{72,8},{16,80},{80,16},{24,88},{88,24},{32,96... | collective-permute-start | bytes 3145736 | tf_op jit(solution)/shard_map/ppermute | solution.py:62
  66.3 4.4 %collective-permute-start.13 = (bf16[512,1024]{1,0:T(8,128)(2,1)S(1)}, bf16[512,1024]{1,0:T(8,128)(2,1)S(1)}, u32[]{:S(2)}, u32[]{:S(2)}) collective-permute-start(bf16[512,1024]{1,0:T(8,128)(2,1)S(1)} %grad_other.1), channel_id=1, source_target_pairs={{0,64},{64,0},{8,72},{72,8},{16,80},{80,16},{24,88},{88,24},{32,96... | collective-permute-start | bytes 3145736 | tf_op jit(solution)/shard_map/ppermute | solution.py:62
  69.0 31.4 %collective-permute-start.15 = (bf16[1024,1024]{1,0:T(8,128)(2,1)S(1)}, bf16[1024,1024]{1,0:T(8,128)(2,1)S(1)}, u32[]{:S(2)}, u32[]{:S(2)}) collective-permute-start(bf16[1024,1024]{1,0:T(8,128)(2,1)S(1)} %depth.7), channel_id=1, source_target_pairs={{0,2},{64,70},{8,10},{72,78},{16,18},{80,86},{24,26},{88,94},{32,3... | collective-permute-start | bytes 6291464 | tf_op jit(solution)/shard_map/ppermute | solution.py:62
  72.5 25.8 %collective-permute-start.14 = (bf16[512,1024]{1,0:T(8,128)(2,1)S(1)}, bf16[512,1024]{1,0:T(8,128)(2,1)S(1)}, u32[]{:S(2)}, u32[]{:S(2)}) collective-permute-start(bf16[512,1024]{1,0:T(8,128)(2,1)S(1)} %chip_sum.5.chip_ref), channel_id=1, source_target_pairs={{0,128},{64,192},{8,136},{72,200},{16,144},{80,208},{24,152},{88,2... | collective-permute-start | bytes 3145736 | tf_op jit(solution)/shard_map/ppermute | solution.py:62
  100.1 3.6 %collective-permute-start.16 = (bf16[528,1024]{1,0:T(8,128)(2,1)S(1)}, bf16[528,1024]{1,0:T(8,128)(2,1)S(1)}, u32[]{:S(2)}, u32[]{:S(2)}) collective-permute-start(bf16[528,1024]{1,0:T(8,128)(2,1)S(1)} %pre_grad.1.refs_5_.refs_2_.own_ref.refs_1_), channel_id=1, source_target_pairs={{0,64},{64,0},{8,72},{72,8},{16,80},{80,16},{24,88},{88,24},{32,96... | collective-permute-start | bytes 3244040 | tf_op jit(solution)/shard_map/ppermute | solution.py:62
  102.2 29.8 %collective-permute-start.18 = (bf16[1024,1024]{1,0:T(8,128)(2,1)S(1)}, bf16[1024,1024]{1,0:T(8,128)(2,1)S(1)}, u32[]{:S(2)}, u32[]{:S(2)}) collective-permute-start(bf16[1024,1024]{1,0:T(8,128)(2,1)S(1)} %depth.8), channel_id=1, source_target_pairs={{0,6},{64,66},{8,14},{72,74},{16,22},{80,82},{24,30},{88,90},{32,3... | collective-permute-start | bytes 6291464 | tf_op jit(solution)/shard_map/ppermute | solution.py:62
  105.0 27.0 %collective-permute-start.19 = (bf16[528,1024]{1,0:T(8,128)(2,1)S(1)}, bf16[528,1024]{1,0:T(8,128)(2,1)S(1)}, u32[]{:S(2)}, u32[]{:S(2)}) collective-permute-start(bf16[528,1024]{1,0:T(8,128)(2,1)S(1)} %depth.9.refs_6_), channel_id=1, source_target_pairs={{0,1},{64,65},{8,9},{72,73},{16,17},{80,81},{24,25},{88,89},{32,33... | collective-permute-start | bytes 3244040 | tf_op jit(solution)/shard_map/ppermute | solution.py:62
  111.1 9.3 %collective-permute-start.17 = (bf16[256,1024]{1,0:T(8,128)(2,1)S(1)}, bf16[256,1024]{1,0:T(8,128)(2,1)S(1)}, u32[]{:S(2)}, u32[]{:S(2)}) collective-permute-start(bf16[256,1024]{1,0:T(8,128)(2,1)S(1)} %get-tuple-element.72), channel_id=1, source_target_pairs={{0,8},{64,120},{8,0},{72,80},{16,24},{80,72},{24,16},{88,96},{32,4... | collective-permute-start | bytes 1572872 | tf_op jit(solution)/shard_map/ppermute | solution.py:62
  120.4 6.5 %collective-permute-start.20 = (bf16[128,1024]{1,0:T(8,128)(2,1)S(1)}, bf16[128,1024]{1,0:T(8,128)(2,1)S(1)}, u32[]{:S(2)}, u32[]{:S(2)}) collective-permute-start(bf16[128,1024]{1,0:T(8,128)(2,1)S(1)} %add_convert_fusion), channel_id=1, source_target_pairs={{0,56},{64,72},{8,16},{72,64},{16,8},{80,88},{24,32},{88,80},{32,2... | collective-permute-start | bytes 786440 | tf_op jit(solution)/shard_map/ppermute | solution.py:62
  133.3 15.6 %collective-permute-start.21 = (bf16[528,1024]{1,0:T(8,128)(2,1)S(1)}, bf16[528,1024]{1,0:T(8,128)(2,1)S(1)}, u32[]{:S(2)}, u32[]{:S(2)}) collective-permute-start(bf16[528,1024]{1,0:T(8,128)(2,1)S(1)} %depth.10.refs_4_), channel_id=1, source_target_pairs={{0,2},{64,70},{8,10},{72,78},{16,18},{80,86},{24,26},{88,94},{32,3... | collective-permute-start | bytes 3244040 | tf_op jit(solution)/shard_map/ppermute | solution.py:62
  135.8 13.1 %collective-permute-start.22 = (bf16[256,1024]{1,0:T(8,128)(2,1)S(1)}, bf16[256,1024]{1,0:T(8,128)(2,1)S(1)}, u32[]{:S(2)}, u32[]{:S(2)}) collective-permute-start(bf16[256,1024]{1,0:T(8,128)(2,1)S(1)} %depth.11), channel_id=1, source_target_pairs={{0,1},{64,65},{8,9},{72,73},{16,17},{80,81},{24,25},{88,89},{32,33... | collective-permute-start | bytes 1572872 | tf_op jit(solution)/shard_map/ppermute | solution.py:62
  138.9 9.3 %collective-permute-start.23 = (bf16[64,1024]{1,0:T(8,128)(2,1)S(1)}, bf16[64,1024]{1,0:T(8,128)(2,1)S(1)}, u32[]{:S(2)}, u32[]{:S(2)}) collective-permute-start(bf16[64,1024]{1,0:T(8,128)(2,1)S(1)} %add_convert_fusion.2), channel_id=1, source_target_pairs={{0,24},{64,104},{8,48},{72,96},{16,40},{80,120},{24,0},{88,112},{3... | collective-permute-start | bytes 393224 | tf_op jit(solution)/shard_map/ppermute | solution.py:62
  149.8 11.7 %collective-permute-start.25 = (bf16[160,1024]{1,0:T(8,128)(2,1)S(1)}, bf16[160,1024]{1,0:T(8,128)(2,1)S(1)}, u32[]{:S(2)}, u32[]{:S(2)}) collective-permute-start(bf16[160,1024]{1,0:T(8,128)(2,1)S(1)} %depth.13.sent_ref), channel_id=1, source_target_pairs={{0,6},{64,66},{8,14},{72,74},{16,22},{80,82},{24,30},{88,90},{32,3... | collective-permute-start | bytes 983048 | tf_op jit(solution)/shard_map/ppermute | solution.py:62
  153.5 8.0 %collective-permute-start.24 = (bf16[128,1024]{1,0:T(8,128)(2,1)S(1)}, bf16[128,1024]{1,0:T(8,128)(2,1)S(1)}, u32[]{:S(2)}, u32[]{:S(2)}) collective-permute-start(bf16[128,1024]{1,0:T(8,128)(2,1)S(1)} %depth.12), channel_id=1, source_target_pairs={{0,1},{64,65},{8,9},{72,73},{16,17},{80,81},{24,25},{88,89},{32,33... | collective-permute-start | bytes 786440 | tf_op jit(solution)/shard_map/ppermute | solution.py:62

commit v4 on v3

--- a/solution.py
+++ b/solution.py
@@ -400,11 +400,17 @@
         offsets = [offset for _, offset in got]
         return dict(sides=self.sides, level=level, got=offsets, riders=riders, base=base), given, size
 
-    def kept_rows(self, at, *earlier):
-        self.right = after(self.right, *earlier)
-        plan, given, size = self.plan(3, 0)
-        out = ((size, self.right.shape[1]), F32)
-        return local(functools.partial(depth_kernel, [plan]), "depth_kept", out, at, *given)
+
+def kept_rows(at, parts, *earlier):
+    plans, operands, base = [], [], 0
+    parts[0].right = after(parts[0].right, *earlier)
+    for part in parts:
+        plan, given, size = part.plan(3, base)
+        plans.append(plan)
+        operands += given
+        base += size
+    out = ((base, parts[0].right.shape[1]), F32)
+    return local(functools.partial(depth_kernel, plans), "depth_kept", out, at, *operands)
 
 
 def exchange(at, parts, pairs):
@@ -500,27 +506,29 @@
     chip_near = chip_sum(at, tok_near, w_in, send(terms, CORE), False)
     got_near = send(chip_near, NEAR)
     tok, cot, terms, cot_sum = arrange_far(at, tok_near, near + far, w_in)
-    terms, got_near = together(send(terms, CORE), got_near)
+    terms_two = grad_other(at, cot, w_out)
+    terms, got_near, terms_two = together(send(terms, CORE), got_near, terms_two)
     chip_far = chip_sum(at, tok, w_in, terms, False)
     got_far = send(chip_far, NEAR)
-    terms = grad_other(at, after(cot, got_far), w_out)
-    chip_two = chip_sum(at, cot, w_out, send(terms, CORE), True)
+    chip_two = chip_sum(at, cot, w_out, send(after(terms_two, chip_far), CORE), True)
     got_two = send(chip_two, NEAR)
+    got_far = after(got_far, chip_two)
     act = gelu(at, (chip_near, got_near), (chip_far, got_far), bias, 0)
     act_away = send(act, CORE)
 
-    out = DepthSum((OWN, AWAY), (act, act_away), cot)
-    _, got = exchange(at, [out], Y_ONE)
+    out = [DepthSum((OWN,), (act,), cot), DepthSum((AWAY,), (act_away,), cot)]
+    got = [exchange(at, [part], Y_ONE)[1] for part in out]
     bias = after(bias, act_away)
     slope = gelu(at, (chip_near, got_near), (chip_far, got_far), bias, 1)
     tok_one, tok_two = by_depth(at, after(tok, slope))
     pg = pre_grad(at, after(slope, tok_one), chip_two, got_two)
     pg_away = send(pg, CORE)
 
-    got, tok_one, tok_two, _ = together(got, tok_one, tok_two, pg)
-    arrived([out], got)
+    got[0], got[1], tok_one, tok_two, _ = together(*got, tok_one, tok_two, pg)
+    arrived(out[:1], got[0])
+    arrived(out[1:], got[1])
     one = DepthSum((OWN,), (tok_one,), pg)
-    sent_one, got_one = exchange(at, [out, one], Y_TWO)
+    sent_one, got_one = exchange(at, [*out, one], Y_TWO)
     two = DepthSum((OWN,), (after(tok_two, sent_one),), pg_away, (pg, pg_away, cot_sum))
     sent_two, got_two = exchange(at, [two], X_HI)
     gi, gi_sent = inputs_grad(at, after(pg, sent_two), pg_away, w_in_plain)
@@ -529,23 +537,23 @@
     gi_got.append(send(gi_sent, Z_STEPS[1]))
 
     got_one, got_two, gi_got[1] = together(got_one, got_two, gi_got[1])
-    arrived([out, one], got_one)
+    arrived([*out, one], got_one)
     arrived([two], got_two)
     sent_one, got_one = exchange(at, [one, two], Y_ONE)
-    sent_two, got_two = exchange(at, [out], X_HI)
+    sent_two, got_two = exchange(at, out, X_HI)
     gi_sent = gi[n : 2 * n] + gi_got[0][n : 2 * n].astype(F32) + gi_got[1][n:].astype(F32)
     gi_sent = gi_sent.astype(BF)
     gi_got.append(send(gi_sent, Z_STEPS[2]))
-    out_kept = out.kept_rows(at, sent_one, sent_two, gi_sent)
+    out_kept = kept_rows(at, out, sent_one, sent_two, gi_sent)
 
     got_one, got_two, gi_got[2], out_kept = together(got_one, got_two, gi_got[2], out_kept)
     arrived([one, two], got_one)
-    arrived([out], got_two)
+    got_out = got_two
     sent_one, got_one = exchange(at, [one], X_HI)
     sent_two, got_two = exchange(at, [two], Y_TWO)
     sent = sent_one, sent_two
-    one_kept, two_kept = one.kept_rows(at, *sent), two.kept_rows(at, *sent)
-    grad_w_out = place_rows(at, scale, after(out_kept, one_kept, two_kept), out.got[2][0])
+    one_kept, two_kept = kept_rows(at, [one], *sent), kept_rows(at, [two], *sent)
+    grad_w_out = place_rows(at, scale, after(out_kept, one_kept, two_kept), got_out)
     gi = gi[:n] + sum(got[:n].astype(F32) for got in gi_got)
     grad_inputs = gi.astype(BF)
     grad_w_in, db_in, db_out = place_columns(

time: 164 us -> 160 us (0.976)
  waiting for transfers between devices: 76.2 us -> 72 us
    ppermute x26 -> x27, waiting for transfers between devices: 76.2 us -> 72 us  [send(): return lax.ppermute(value, AXES, pairs)]
    pallas_call x24 -> x25, Pallas kernels: 35.6 us -> 36.3 us  [local(): pl.pallas_call(kernel, in_specs=[SCALARS] + [WHOLE] * len(arrays), out_sp...]
    ppermute x26 -> x27, starting transfers between devices: 39.5 us -> 38.8 us  [send(): return lax.ppermute(value, AXES, pairs)]
  transfers between devices with their start and end apart: 26 -> 27, of which waited for: 14 -> 14; matrix products, arithmetic and copies ran while one was open for 1% -> 1% of each run, Pallas kernels for 19% -> 20%
where the time goes in v4:
time: 160 us; the launch traced here: 159 us
  waiting for transfers between devices  72 us (45%)
  Pallas kernels  42.4 us (26%)
  starting transfers between devices  38.8 us (24%)
  local copies, waits for them, and re-layouts  4.01 us (3%)
    ppermute x27, waiting for transfers between devices, send(): return lax.ppermute(value, AXES, pairs)  72 us
    ppermute x27, starting transfers between devices, send(): return lax.ppermute(value, AXES, pairs)  38.8 us
    pallas_call x25, Pallas kernels, local(): pl.pallas_call(kernel, in_specs=[SCALARS] + [WHOLE] * len(arrays), out_sp...  36.3 us
    pallas_call x2, Pallas kernels, permute(): pl.pallas_call(functools.partial(permute_kernel, axis, orders), in_specs=...  4.46 us
    unnamed x6, local copies, waits for them, and re-layouts  3.3 us
  transfers between devices with their start and end apart: 27, of which 14 were waited for; matrix products, arithmetic and copies ran while one was open for 1% of the time, Pallas kernels for 20%

profile of v4, /device:TPU:32, one launch (start us, length us, event | category | flops | bytes accessed | tf_op | source)
XLA Modules:
  0.0 159.1 jit_solution(7826440949058310071)
XLA Ops:
  0.6 1.7 %pack.1.refs_0_ = bf16[128,1024]{1,0:T(8,128)(2,1)} custom-call(bf16[64,1024]{1,0:T(8,128)(2,1)} %a_ref.3, bf16[64,1024]{1,0:T(8,128)(2,1)} %b_ref.1), custom_call_target="tpu_custom_call" | custom-call | bytes 4096 | tf_op jit(solution)/shard_map/pack/pallas_call | solution.py:177
  2.3 2.0 %collective-permute-start.3 = (bf16[128,1024]{1,0:T(8,128)(2,1)}, bf16[128,1024]{1,0:T(8,128)(2,1)S(1)}, u32[]{:S(2)}, u32[]{:S(2)}) collective-permute-start(bf16[128,1024]{1,0:T(8,128)(2,1)} %pack.1.refs_0_), channel_id=1, source_target_pairs={{0,8},{64,72},{8,16},{72,80},{16,24},{80,88},{24,32},{88,96},{32,4... | collective-permute-start | bytes 786440 | tf_op jit(solution)/shard_map/ppermute | solution.py:62
  4.3 4.5 %collective-permute-start.2 = (bf16[128,1024]{1,0:T(8,128)(2,1)}, bf16[128,1024]{1,0:T(8,128)(2,1)S(1)}, u32[]{:S(2)}, u32[]{:S(2)}) collective-permute-start(bf16[128,1024]{1,0:T(8,128)(2,1)} %pack.1.refs_0_), channel_id=1, source_target_pairs={{0,16},{64,80},{8,24},{72,88},{16,32},{80,96},{24,40},{88,104},{32... | collective-permute-start | bytes 786440 | tf_op jit(solution)/shard_map/ppermute | solution.py:62
  11.2 2.2 %copy-done = bf16[2048,1024]{1,0:T(8,128)(2,1)S(1)} copy-done((bf16[2048,1024]{1,0:T(8,128)(2,1)S(1)}, bf16[2048,1024]{1,0:T(8,128)(2,1)}, u32[]{:S(2)}) %copy-start) | copy-done | bytes 4194328
  14.4 1.1 copy-done.1
  15.6 3.4 %permute_1.1 = (bf16[1024,2048]{1,0:T(8,128)(2,1)S(1)}, bf16[1024,2048]{1,0:T(8,128)(2,1)S(1)}) custom-call(s32[3]{0:T(128)S(1)} %pad_add_fusion.at_ref, bf16[1024,2048]{1,0:T(8,128)(2,1)S(1)} %copy-done.1), custom_call_target="tpu_custom_call" | custom-call | bytes 4096 | tf_op jit(solution)/shard_map/permute_1/pallas_call | solution.py:142
  19.0 6.6 %collective-permute-done.2.refs_3_ = bf16[128,1024]{1,0:T(8,128)(2,1)S(1)} collective-permute-done((bf16[128,1024]{1,0:T(8,128)(2,1)}, bf16[128,1024]{1,0:T(8,128)(2,1)S(1)}, u32[]{:S(2)}, u32[]{:S(2)}) %collective-permute-start.2) | collective-permute-done | bytes 262176 | tf_op jit(solution)/shard_map/ppermute | solution.py:62
  25.6 1.5 collective-permute-done.refs_1_
  27.1 1.4 arrange_near.1
  29.7 1.2 collective-permute-start.6
  30.9 1.4 chip_sum.3.refs_0_
  32.3 1.6 collective-permute-start.10
  33.9 4.8 %collective-permute-start.8 = (bf16[64,1024]{1,0:T(8,128)(2,1)S(1)}, bf16[64,1024]{1,0:T(8,128)(2,1)S(1)}, u32[]{:S(2)}, u32[]{:S(2)}) collective-permute-start(bf16[64,1024]{1,0:T(8,128)(2,1)S(1)} %slice.31), channel_id=1, source_target_pairs={{0,16},{64,80},{8,24},{72,88},{16,32},{80,96},{24,40},{88,104},{32... | collective-permute-start | bytes 393224 | tf_op jit(solution)/shard_map/ppermute | solution.py:62
  38.7 7.7 %collective-permute-done.8.refs_8_ = bf16[64,1024]{1,0:T(8,128)(2,1)S(1)} collective-permute-done((bf16[64,1024]{1,0:T(8,128)(2,1)S(1)}, bf16[64,1024]{1,0:T(8,128)(2,1)S(1)}, u32[]{:S(2)}, u32[]{:S(2)}) %collective-permute-start.8) | collective-permute-done | bytes 131104 | tf_op jit(solution)/shard_map/ppermute | solution.py:62
  46.5 1.9 %arrange_far.1 = (bf16[512,1024]{1,0:T(8,128)(2,1)S(1)}, bf16[512,1024]{1,0:T(8,128)(2,1)S(1)}, bf16[192,1024]{1,0:T(8,128)(2,1)S(1)}, f32[8,1024]{1,0:T(8,128)}, f32[1,1024]{1,0:T(1,128)S(1)}) custom-call(s32[3]{0:T(128)S(1)} %pad_add_fusion.at_ref, bf16[320,1024]{1,0:T(8,128)(2,1)S(1)} %get-tuple-element.55.a_ref.tok_ref, bf16[128,1024]{1,0:T(8,128)(2,1)S(1)} %copy-done.2, ...), custom_call_target="tpu_custom_call" | custom-call | bytes 4096 | tf_op jit(solution)/shard_map/arrange_far/pallas_call | solution.py:98
  48.4 1.8 %grad_other.1 = bf16[512,1024]{1,0:T(8,128)(2,1)S(1)} custom-call(s32[3]{0:T(128)S(1)} %pad_add_fusion.at_ref, bf16[512,1024]{1,0:T(8,128)(2,1)S(1)} %get-tuple-element.82.cot_ref.a_ref.refs_1_.refs_4_.refs_5_, bf16[2048,1024]{1,0:T(8,128)(2,1)S(1)} %permute_0.1.w_ref), custom_call_target="tpu_custom_call" | custom-call | bytes 4096 | tf_op jit(solution)/shard_map/grad_other/pallas_call | solution.py:98
  50.3 1.1 chip_sum.4.refs_2_
  52.0 1.4 collective-permute-start.11
  54.3 1.8 %chip_sum.5.chip_ref = bf16[512,1024]{1,0:T(8,128)(2,1)S(1)} custom-call(s32[3]{0:T(128)S(1)} %pad_add_fusion.at_ref, bf16[512,1024]{1,0:T(8,128)(2,1)S(1)} %get-tuple-element.82.cot_ref.a_ref.refs_1_.refs_4_.refs_5_, bf16[2048,1024]{1,0:T(8,128)(2,1)S(1)} %permute_0.1.w_ref, bf16[512,1024]{1,0:T(8,128)(2,1)S(1)} %collective-permute-done.12.got_ref), custom_call_target="tpu_custom_call" | custom-call | bytes 4096 | tf_op jit(solution)/shard_map/chip_sum/pallas_call | solution.py:98
  56.1 7.0 %collective-permute-done.11.refs_3_ = bf16[192,1024]{1,0:T(8,128)(2,1)S(1)} collective-permute-done((bf16[192,1024]{1,0:T(8,128)(2,1)S(1)}, bf16[192,1024]{1,0:T(8,128)(2,1)S(1)}, u32[]{:S(2)}, u32[]{:S(2)}) %collective-permute-start.11) | collective-permute-done | bytes 393248 | tf_op jit(solution)/shard_map/ppermute | solution.py:62
  63.1 1.8 %act.1.refs_0_ = bf16[512,1024]{1,0:T(8,128)(2,1)S(1)} custom-call(s32[3]{0:T(128)S(1)} %pad_add_fusion.at_ref, bf16[320,1024]{1,0:T(8,128)(2,1)S(1)} %chip_sum.3.refs_0_, bf16[320,1024]{1,0:T(8,128)(2,1)S(1)} %collective-permute-done.10.refs_1_, bf16[192,1024]{1,0:T(8,128)(2,1)S(1)} %chip_sum.4.refs_2_, ...), custom_call_target="tpu_custom_call" | custom-call | bytes 4096 | tf_op jit(solution)/shard_map/act/pallas_call | solution.py:98
  65.1 1.5 collective-permute-start.14
  66.6 1.3 depth.8
  67.9 1.7 %collective-permute-start.15 = (bf16[512,1024]{1,0:T(8,128)(2,1)S(1)}, bf16[512,1024]{1,0:T(8,128)(2,1)S(1)}, u32[]{:S(2)}, u32[]{:S(2)}) collective-permute-start(bf16[512,1024]{1,0:T(8,128)(2,1)S(1)} %depth.8), channel_id=1, source_target_pairs={{0,2},{64,70},{8,10},{72,78},{16,18},{80,86},{24,26},{88,94},{32,3... | collective-permute-start | bytes 3145736 | tf_op jit(solution)/shard_map/ppermute | solution.py:62
  69.6 1.3 depth.9
  71.4 2.4 %slope.1.slope_ref = f32[512,1024]{1,0:T(8,128)S(1)} custom-call(s32[3]{0:T(128)S(1)} %pad_add_fusion.at_ref, bf16[320,1024]{1,0:T(8,128)(2,1)S(1)} %chip_sum.3.refs_0_, bf16[320,1024]{1,0:T(8,128)(2,1)S(1)} %collective-permute-done.10.refs_1_, bf16[192,1024]{1,0:T(8,128)(2,1)S(1)} %chip_sum.4.refs_2_, ...), custom_call_target="tpu_custom_call" | custom-call | bytes 4096 | tf_op jit(solution)/shard_map/slope/pallas_call | solution.py:98
  75.0 15.7 %collective-permute-done.14.got_ref = bf16[512,1024]{1,0:T(8,128)(2,1)S(1)} collective-permute-done((bf16[512,1024]{1,0:T(8,128)(2,1)S(1)}, bf16[512,1024]{1,0:T(8,128)(2,1)S(1)}, u32[]{:S(2)}, u32[]{:S(2)}) %collective-permute-start.14) | collective-permute-done | bytes 1048608 | tf_op jit(solution)/shard_map/ppermute | solution.py:62
  90.7 1.8 %pre_grad.1.refs_7_.refs_2_.own_ref.refs_1_ = bf16[528,1024]{1,0:T(8,128)(2,1)S(1)} custom-call(s32[3]{0:T(128)S(1)} %pad_add_fusion.at_ref, f32[512,1024]{1,0:T(8,128)S(1)} %slope.1.slope_ref, bf16[512,1024]{1,0:T(8,128)(2,1)S(1)} %chip_sum.5.chip_ref, bf16[512,1024]{1,0:T(8,128)(2,1)S(1)} %collective-permute-done.14.got_ref), custom_call_target="tpu_custom_call" | custom-call | bytes 4096 | tf_op jit(solution)/shard_map/pre_grad/pallas_call | solution.py:98
  92.8 1.2 collective-permute-done.16.refs_5_.refs_6_
  94.1 1.8 %depth.10 = bf16[1024,1024]{1,0:T(8,128)(2,1)S(1)} custom-call(s32[3]{0:T(128)S(1)} %pad_add_fusion.at_ref, bf16[512,1024]{1,0:T(8,128)(2,1)S(1)} %act.1.refs_0_, bf16[512,1024]{1,0:T(8,128)(2,1)S(1)} %get-tuple-element.82.cot_ref.a_ref.refs_1_.refs_4_.refs_5_, bf16[512,1024]{1,0:T(8,128)(2,1)S(1)} %collective-permute-done.15.refs_2_, ...), custom_call_target="tpu_custom_call" | custom-call | bytes 4096 | tf_op jit(solution)/shard_map/depth/pallas_call | solution.py:98
  95.9 3.1 %collective-permute-start.19 = (bf16[1024,1024]{1,0:T(8,128)(2,1)S(1)}, bf16[1024,1024]{1,0:T(8,128)(2,1)S(1)}, u32[]{:S(2)}, u32[]{:S(2)}) collective-permute-start(bf16[1024,1024]{1,0:T(8,128)(2,1)S(1)} %depth.10), channel_id=1, source_target_pairs={{0,6},{64,66},{8,14},{72,74},{16,22},{80,82},{24,30},{88,90},{32,3... | collective-permute-start | bytes 6291464 | tf_op jit(solution)/shard_map/ppermute | solution.py:62
  99.0 1.3 depth.11.refs_6_
  100.3 2.8 %collective-permute-start.20 = (bf16[528,1024]{1,0:T(8,128)(2,1)S(1)}, bf16[528,1024]{1,0:T(8,128)(2,1)S(1)}, u32[]{:S(2)}, u32[]{:S(2)}) collective-permute-start(bf16[528,1024]{1,0:T(8,128)(2,1)S(1)} %depth.11.refs_6_), channel_id=1, source_target_pairs={{0,1},{64,65},{8,9},{72,73},{16,17},{80,81},{24,25},{88,89},{32,33... | collective-permute-start | bytes 3244040 | tf_op jit(solution)/shard_map/ppermute | solution.py:62
  103.1 3.0 %inputs_grad.1 = (f32[512,1024]{1,0:T(8,128)S(1)}, bf16[256,1024]{1,0:T(8,128)(2,1)S(1)}) custom-call(s32[3]{0:T(128)S(1)} %pad_add_fusion.at_ref, bf16[528,1024]{1,0:T(8,128)(2,1)S(1)} %pre_grad.1.refs_7_.refs_2_.own_ref.refs_1_, bf16[528,1024]{1,0:T(8,128)(2,1)S(1)} %collective-permute-done.17.refs_1_.refs_3_.away_ref.refs_4_, ...), custom_call_target="tpu_custom_call" | custom-call | bytes 4096 | tf_op jit(solution)/shard_map/inputs_grad/pallas_call | solution.py:98
  106.3 9.5 %collective-permute-done.18 = bf16[256,1024]{1,0:T(8,128)(2,1)S(1)} collective-permute-done((bf16[256,1024]{1,0:T(8,128)(2,1)S(1)}, bf16[256,1024]{1,0:T(8,128)(2,1)S(1)}, u32[]{:S(2)}, u32[]{:S(2)}) %collective-permute-start.18) | collective-permute-done | bytes 524320 | tf_op jit(solution)/shard_map/ppermute | solution.py:62
  115.9 1.6 %collective-permute-start.21 = (bf16[128,1024]{1,0:T(8,128)(2,1)S(1)}, bf16[128,1024]{1,0:T(8,128)(2,1)S(1)}, u32[]{:S(2)}, u32[]{:S(2)}) collective-permute-start(bf16[128,1024]{1,0:T(8,128)(2,1)S(1)} %add_convert_fusion), channel_id=1, source_target_pairs={{0,56},{64,72},{8,16},{72,64},{16,8},{80,88},{24,32},{88,80},{32,2... | collective-permute-start | bytes 786440 | tf_op jit(solution)/shard_map/ppermute | solution.py:62
  117.5 4.8 %collective-permute-done.21 = bf16[128,1024]{1,0:T(8,128)(2,1)S(1)} collective-permute-done((bf16[128,1024]{1,0:T(8,128)(2,1)S(1)}, bf16[128,1024]{1,0:T(8,128)(2,1)S(1)}, u32[]{:S(2)}, u32[]{:S(2)}) %collective-permute-start.21) | collective-permute-done | bytes 262176 | tf_op jit(solution)/shard_map/ppermute | solution.py:62
  122.3 2.9 %collective-permute-done.20.refs_5_.refs_2_ = bf16[528,1024]{1,0:T(8,128)(2,1)S(1)} collective-permute-done((bf16[528,1024]{1,0:T(8,128)(2,1)S(1)}, bf16[528,1024]{1,0:T(8,128)(2,1)S(1)}, u32[]{:S(2)}, u32[]{:S(2)}) %collective-permute-start.20) | collective-permute-done | bytes 1081376 | tf_op jit(solution)/shard_map/ppermute | solution.py:62
  125.3 1.3 depth.12.refs_4_
  126.6 1.5 collective-permute-start.22
  129.2 2.8 %collective-permute-start.23 = (bf16[256,1024]{1,0:T(8,128)(2,1)S(1)}, bf16[256,1024]{1,0:T(8,128)(2,1)S(1)}, u32[]{:S(2)}, u32[]{:S(2)}) collective-permute-start(bf16[256,1024]{1,0:T(8,128)(2,1)S(1)} %depth.13), channel_id=1, source_target_pairs={{0,1},{64,65},{8,9},{72,73},{16,17},{80,81},{24,25},{88,89},{32,33... | collective-permute-start | bytes 1572872 | tf_op jit(solution)/shard_map/ppermute | solution.py:62
  132.1 1.1 collective-permute-start.24
  134.3 6.4 %collective-permute-done.24 = bf16[64,1024]{1,0:T(8,128)(2,1)S(1)} collective-permute-done((bf16[64,1024]{1,0:T(8,128)(2,1)S(1)}, bf16[64,1024]{1,0:T(8,128)(2,1)S(1)}, u32[]{:S(2)}, u32[]{:S(2)}) %collective-permute-start.24) | collective-permute-done | bytes 131104 | tf_op jit(solution)/shard_map/ppermute | solution.py:62
  140.6 4.1 %collective-permute-done.23.got_ref = bf16[256,1024]{1,0:T(8,128)(2,1)S(1)} collective-permute-done((bf16[256,1024]{1,0:T(8,128)(2,1)S(1)}, bf16[256,1024]{1,0:T(8,128)(2,1)S(1)}, u32[]{:S(2)}, u32[]{:S(2)}) %collective-permute-start.23) | collective-permute-done | bytes 524320 | tf_op jit(solution)/shard_map/ppermute | solution.py:62
  146.9 2.8 %collective-permute-start.25 = (bf16[128,1024]{1,0:T(8,128)(2,1)S(1)}, bf16[128,1024]{1,0:T(8,128)(2,1)S(1)}, u32[]{:S(2)}, u32[]{:S(2)}) collective-permute-start(bf16[128,1024]{1,0:T(8,128)(2,1)S(1)} %depth.14), channel_id=1, source_target_pairs={{0,1},{64,65},{8,9},{72,73},{16,17},{80,81},{24,25},{88,89},{32,33... | collective-permute-start | bytes 786440 | tf_op jit(solution)/shard_map/ppermute | solution.py:62
  151.5 1.6 %place_rows.1 = f32[256,1024]{1,0:T(8,128)} custom-call(s32[3]{0:T(128)S(1)} %pad_add_fusion.at_ref, f32[256,1024]{1,0:T(8,128)S(1)} %depth_kept.3.keep_ref, bf16[256,1024]{1,0:T(8,128)(2,1)S(1)} %collective-permute-done.23.got_ref), custom_call_target="tpu_custom_call" | custom-call | bytes 4096 | tf_op jit(solution)/shard_map/place_rows/pallas_call | solution.py:98
  153.9 3.6 %collective-permute-done.25.got_ref = bf16[128,1024]{1,0:T(8,128)(2,1)S(1)} collective-permute-done((bf16[128,1024]{1,0:T(8,128)(2,1)S(1)}, bf16[128,1024]{1,0:T(8,128)(2,1)S(1)}, u32[]{:S(2)}, u32[]{:S(2)}) %collective-permute-start.25) | collective-permute-done | bytes 262176 | tf_op jit(solution)/shard_map/ppermute | solution.py:62
  157.4 1.7 %place_columns.1 = (f32[128,2048]{1,0:T(8,128)}, f32[16,128]{1,0:T(8,128)}, f32[8,128]{1,0:T(8,128)}) custom-call(s32[3]{0:T(128)S(1)} %pad_add_fusion.at_ref, f32[128,1024]{1,0:T(8,128)S(1)} %depth_kept.4.keep_ref, bf16[128,1024]{1,0:T(8,128)(2,1)S(1)} %collective-permute-done.25.got_ref, f32[128,1024]{1,0:T(8,128)S(1)} %depth_kept.5.keep2_ref, ...), custom_call_target="tpu_custom_call" | custom-call | bytes 4096 | tf_op jit(solution)/shard_map/place_columns/pallas_call | solution.py:98
  (47 shorter events, 15.3 us)
Async XLA Ops:
  2.3 16.6 %collective-permute-start.3 = (bf16[128,1024]{1,0:T(8,128)(2,1)}, bf16[128,1024]{1,0:T(8,128)(2,1)S(1)}, u32[]{:S(2)}, u32[]{:S(2)}) collective-permute-start(bf16[128,1024]{1,0:T(8,128)(2,1)} %pack.1.refs_0_), channel_id=1, source_target_pairs={{0,8},{64,72},{8,16},{72,80},{16,24},{80,88},{24,32},{88,96},{32,4... | collective-permute-start | bytes 786440 | tf_op jit(solution)/shard_map/ppermute | solution.py:62
  4.3 21.2 %collective-permute-start.2 = (bf16[128,1024]{1,0:T(8,128)(2,1)}, bf16[128,1024]{1,0:T(8,128)(2,1)S(1)}, u32[]{:S(2)}, u32[]{:S(2)}) collective-permute-start(bf16[128,1024]{1,0:T(8,128)(2,1)} %pack.1.refs_0_), channel_id=1, source_target_pairs={{0,16},{64,80},{8,24},{72,88},{16,32},{80,96},{24,40},{88,104},{32... | collective-permute-start | bytes 786440 | tf_op jit(solution)/shard_map/ppermute | solution.py:62
  8.8 16.8 %collective-permute-start.1 = (bf16[128,1024]{1,0:T(8,128)(2,1)}, bf16[128,1024]{1,0:T(8,128)(2,1)S(1)}, u32[]{:S(2)}, u32[]{:S(2)}) collective-permute-start(bf16[128,1024]{1,0:T(8,128)(2,1)} %pack.1.refs_0_), channel_id=1, source_target_pairs={{0,48},{64,112},{8,56},{72,120},{16,0},{80,64},{24,8},{88,72},{32,... | collective-permute-start | bytes 786440 | tf_op jit(solution)/shard_map/ppermute | solution.py:62
  8.8 18.3 %collective-permute-start = (bf16[128,1024]{1,0:T(8,128)(2,1)}, bf16[128,1024]{1,0:T(8,128)(2,1)S(1)}, u32[]{:S(2)}, u32[]{:S(2)}) collective-permute-start(bf16[128,1024]{1,0:T(8,128)(2,1)} %pack.1.refs_0_), channel_id=1, source_target_pairs={{0,56},{64,120},{8,0},{72,64},{16,8},{80,72},{24,16},{88,80},{32,2... | collective-permute-start | bytes 786440 | tf_op jit(solution)/shard_map/ppermute | solution.py:62
  11.2 2.2 %copy-start = (bf16[2048,1024]{1,0:T(8,128)(2,1)S(1)}, bf16[2048,1024]{1,0:T(8,128)(2,1)}, u32[]{:S(2)}) copy-start(bf16[2048,1024]{1,0:T(8,128)(2,1)} %a_ref.5) | copy-start | bytes 12582916
  13.4 2.2 %copy-start.1 = (bf16[1024,2048]{1,0:T(8,128)(2,1)S(1)}, bf16[1024,2048]{1,0:T(8,128)(2,1)}, u32[]{:S(2)}) copy-start(bf16[1024,2048]{1,0:T(8,128)(2,1)} %a_ref.4) | copy-start | bytes 12582916
  15.6 11.5 %copy-start.2 = (bf16[128,1024]{1,0:T(8,128)(2,1)S(1)}, bf16[128,1024]{1,0:T(8,128)(2,1)}, u32[]{:S(2)}) copy-start(bf16[128,1024]{1,0:T(8,128)(2,1)} %pack.1.refs_0_) | copy-start | bytes 786436
  28.5 2.4 %collective-permute-start.4 = (bf16[320,1024]{1,0:T(8,128)(2,1)S(1)}, bf16[320,1024]{1,0:T(8,128)(2,1)S(1)}, u32[]{:S(2)}, u32[]{:S(2)}) collective-permute-start(bf16[320,1024]{1,0:T(8,128)(2,1)S(1)} %get-tuple-element.56), channel_id=1, source_target_pairs={{0,64},{64,0},{8,72},{72,8},{16,80},{80,16},{24,88},{88,24},{32,96... | collective-permute-start | bytes 1966088 | tf_op jit(solution)/shard_map/ppermute | solution.py:62
  28.6 17.9 %collective-permute-start.5 = (bf16[128,1024]{1,0:T(8,128)(2,1)S(1)}, bf16[128,1024]{1,0:T(8,128)(2,1)S(1)}, u32[]{:S(2)}, u32[]{:S(2)}) collective-permute-start(bf16[128,1024]{1,0:T(8,128)(2,1)S(1)} %collective-permute-done.1.refs_2_), channel_id=1, source_target_pairs={{0,56},{64,120},{8,0},{72,64},{16,8},{80,72},{24,16},{88,80},{32,2... | collective-permute-start | bytes 786440 | tf_op jit(solution)/shard_map/ppermute | solution.py:62
  29.7 16.8 %collective-permute-start.6 = (bf16[128,1024]{1,0:T(8,128)(2,1)S(1)}, bf16[128,1024]{1,0:T(8,128)(2,1)S(1)}, u32[]{:S(2)}, u32[]{:S(2)}) collective-permute-start(bf16[128,1024]{1,0:T(8,128)(2,1)S(1)} %collective-permute-done.2.refs_3_), channel_id=1, source_target_pairs={{0,8},{64,72},{8,16},{72,80},{16,24},{80,88},{24,32},{88,96},{32,4... | collective-permute-start | bytes 786440 | tf_op jit(solution)/shard_map/ppermute | solution.py:62
  32.3 18.0 %collective-permute-start.10 = (bf16[320,1024]{1,0:T(8,128)(2,1)S(1)}, bf16[320,1024]{1,0:T(8,128)(2,1)S(1)}, u32[]{:S(2)}, u32[]{:S(2)}) collective-permute-start(bf16[320,1024]{1,0:T(8,128)(2,1)S(1)} %chip_sum.3.refs_0_), channel_id=1, source_target_pairs={{0,128},{64,192},{8,136},{72,200},{16,144},{80,208},{24,152},{88,2... | collective-permute-start | bytes 1966088 | tf_op jit(solution)/shard_map/ppermute | solution.py:62
  33.9 12.5 %collective-permute-start.8 = (bf16[64,1024]{1,0:T(8,128)(2,1)S(1)}, bf16[64,1024]{1,0:T(8,128)(2,1)S(1)}, u32[]{:S(2)}, u32[]{:S(2)}) collective-permute-start(bf16[64,1024]{1,0:T(8,128)(2,1)S(1)} %slice.31), channel_id=1, source_target_pairs={{0,16},{64,80},{8,24},{72,88},{16,32},{80,96},{24,40},{88,104},{32... | collective-permute-start | bytes 393224 | tf_op jit(solution)/shard_map/ppermute | solution.py:62
  38.7 7.8 %collective-permute-start.7 = (bf16[64,1024]{1,0:T(8,128)(2,1)S(1)}, bf16[64,1024]{1,0:T(8,128)(2,1)S(1)}, u32[]{:S(2)}, u32[]{:S(2)}) collective-permute-start(bf16[64,1024]{1,0:T(8,128)(2,1)S(1)} %slice.30), channel_id=1, source_target_pairs={{0,48},{64,112},{8,56},{72,120},{16,0},{80,64},{24,8},{88,72},{32,... | collective-permute-start | bytes 393224 | tf_op jit(solution)/shard_map/ppermute | solution.py:62
  48.4 1.8 %collective-permute-start.9 = (bf16[192,1024]{1,0:T(8,128)(2,1)S(1)}, bf16[192,1024]{1,0:T(8,128)(2,1)S(1)}, u32[]{:S(2)}, u32[]{:S(2)}) collective-permute-start(bf16[192,1024]{1,0:T(8,128)(2,1)S(1)} %get-tuple-element.57), channel_id=1, source_target_pairs={{0,64},{64,0},{8,72},{72,8},{16,80},{80,16},{24,88},{88,24},{32,96... | collective-permute-start | bytes 1179656 | tf_op jit(solution)/shard_map/ppermute | solution.py:62
  51.4 2.9 %collective-permute-start.12 = (bf16[512,1024]{1,0:T(8,128)(2,1)S(1)}, bf16[512,1024]{1,0:T(8,128)(2,1)S(1)}, u32[]{:S(2)}, u32[]{:S(2)}) collective-permute-start(bf16[512,1024]{1,0:T(8,128)(2,1)S(1)} %grad_other.1), channel_id=1, source_target_pairs={{0,64},{64,0},{8,72},{72,8},{16,80},{80,16},{24,88},{88,24},{32,96... | collective-permute-start | bytes 3145736 | tf_op jit(solution)/shard_map/ppermute | solution.py:62
  52.0 11.1 %collective-permute-start.11 = (bf16[192,1024]{1,0:T(8,128)(2,1)S(1)}, bf16[192,1024]{1,0:T(8,128)(2,1)S(1)}, u32[]{:S(2)}, u32[]{:S(2)}) collective-permute-start(bf16[192,1024]{1,0:T(8,128)(2,1)S(1)} %chip_sum.4.refs_2_), channel_id=1, source_target_pairs={{0,128},{64,192},{8,136},{72,200},{16,144},{80,208},{24,152},{88,2... | collective-permute-start | bytes 1179656 | tf_op jit(solution)/shard_map/ppermute | solution.py:62
  65.0 4.6 %collective-permute-start.13 = (bf16[512,1024]{1,0:T(8,128)(2,1)S(1)}, bf16[512,1024]{1,0:T(8,128)(2,1)S(1)}, u32[]{:S(2)}, u32[]{:S(2)}) collective-permute-start(bf16[512,1024]{1,0:T(8,128)(2,1)S(1)} %act.1.refs_0_), channel_id=1, source_target_pairs={{0,64},{64,0},{8,72},{72,8},{16,80},{80,16},{24,88},{88,24},{32,96... | collective-permute-start | bytes 3145736 | tf_op jit(solution)/shard_map/ppermute | solution.py:62
  65.1 25.6 %collective-permute-start.14 = (bf16[512,1024]{1,0:T(8,128)(2,1)S(1)}, bf16[512,1024]{1,0:T(8,128)(2,1)S(1)}, u32[]{:S(2)}, u32[]{:S(2)}) collective-permute-start(bf16[512,1024]{1,0:T(8,128)(2,1)S(1)} %chip_sum.5.chip_ref), channel_id=1, source_target_pairs={{0,128},{64,192},{8,136},{72,200},{16,144},{80,208},{24,152},{88,2... | collective-permute-start | bytes 3145736 | tf_op jit(solution)/shard_map/ppermute | solution.py:62
  67.9 24.9 %collective-permute-start.15 = (bf16[512,1024]{1,0:T(8,128)(2,1)S(1)}, bf16[512,1024]{1,0:T(8,128)(2,1)S(1)}, u32[]{:S(2)}, u32[]{:S(2)}) collective-permute-start(bf16[512,1024]{1,0:T(8,128)(2,1)S(1)} %depth.8), channel_id=1, source_target_pairs={{0,2},{64,70},{8,10},{72,78},{16,18},{80,86},{24,26},{88,94},{32,3... | collective-permute-start | bytes 3145736 | tf_op jit(solution)/shard_map/ppermute | solution.py:62
  70.9 23.2 %collective-permute-start.16 = (bf16[512,1024]{1,0:T(8,128)(2,1)S(1)}, bf16[512,1024]{1,0:T(8,128)(2,1)S(1)}, u32[]{:S(2)}, u32[]{:S(2)}) collective-permute-start(bf16[512,1024]{1,0:T(8,128)(2,1)S(1)} %depth.9), channel_id=1, source_target_pairs={{0,2},{64,70},{8,10},{72,78},{16,18},{80,86},{24,26},{88,94},{32,3... | collective-permute-start | bytes 3145736 | tf_op jit(solution)/shard_map/ppermute | solution.py:62
  92.5 6.5 %collective-permute-start.17 = (bf16[528,1024]{1,0:T(8,128)(2,1)S(1)}, bf16[528,1024]{1,0:T(8,128)(2,1)S(1)}, u32[]{:S(2)}, u32[]{:S(2)}) collective-permute-start(bf16[528,1024]{1,0:T(8,128)(2,1)S(1)} %pre_grad.1.refs_7_.refs_2_.own_ref.refs_1_), channel_id=1, source_target_pairs={{0,64},{64,0},{8,72},{72,8},{16,80},{80,16},{24,88},{88,24},{32,96... | collective-permute-start | bytes 3244040 | tf_op jit(solution)/shard_map/ppermute | solution.py:62
  95.9 29.3 %collective-permute-start.19 = (bf16[1024,1024]{1,0:T(8,128)(2,1)S(1)}, bf16[1024,1024]{1,0:T(8,128)(2,1)S(1)}, u32[]{:S(2)}, u32[]{:S(2)}) collective-permute-start(bf16[1024,1024]{1,0:T(8,128)(2,1)S(1)} %depth.10), channel_id=1, source_target_pairs={{0,6},{64,66},{8,14},{72,74},{16,22},{80,82},{24,30},{88,90},{32,3... | collective-permute-start | bytes 6291464 | tf_op jit(solution)/shard_map/ppermute | solution.py:62
  100.3 24.9 %collective-permute-start.20 = (bf16[528,1024]{1,0:T(8,128)(2,1)S(1)}, bf16[528,1024]{1,0:T(8,128)(2,1)S(1)}, u32[]{:S(2)}, u32[]{:S(2)}) collective-permute-start(bf16[528,1024]{1,0:T(8,128)(2,1)S(1)} %depth.11.refs_6_), channel_id=1, source_target_pairs={{0,1},{64,65},{8,9},{72,73},{16,17},{80,81},{24,25},{88,89},{32,33... | collective-permute-start | bytes 3244040 | tf_op jit(solution)/shard_map/ppermute | solution.py:62
  106.2 9.6 %collective-permute-start.18 = (bf16[256,1024]{1,0:T(8,128)(2,1)S(1)}, bf16[256,1024]{1,0:T(8,128)(2,1)S(1)}, u32[]{:S(2)}, u32[]{:S(2)}) collective-permute-start(bf16[256,1024]{1,0:T(8,128)(2,1)S(1)} %get-tuple-element.78), channel_id=1, source_target_pairs={{0,8},{64,120},{8,0},{72,80},{16,24},{80,72},{24,16},{88,96},{32,4... | collective-permute-start | bytes 1572872 | tf_op jit(solution)/shard_map/ppermute | solution.py:62
  115.9 6.5 %collective-permute-start.21 = (bf16[128,1024]{1,0:T(8,128)(2,1)S(1)}, bf16[128,1024]{1,0:T(8,128)(2,1)S(1)}, u32[]{:S(2)}, u32[]{:S(2)}) collective-permute-start(bf16[128,1024]{1,0:T(8,128)(2,1)S(1)} %add_convert_fusion), channel_id=1, source_target_pairs={{0,56},{64,72},{8,16},{72,64},{16,8},{80,88},{24,32},{88,80},{32,2... | collective-permute-start | bytes 786440 | tf_op jit(solution)/shard_map/ppermute | solution.py:62
  126.6 18.2 %collective-permute-start.22 = (bf16[528,1024]{1,0:T(8,128)(2,1)S(1)}, bf16[528,1024]{1,0:T(8,128)(2,1)S(1)}, u32[]{:S(2)}, u32[]{:S(2)}) collective-permute-start(bf16[528,1024]{1,0:T(8,128)(2,1)S(1)} %depth.12.refs_4_), channel_id=1, source_target_pairs={{0,2},{64,70},{8,10},{72,78},{16,18},{80,86},{24,26},{88,94},{32,3... | collective-permute-start | bytes 3244040 | tf_op jit(solution)/shard_map/ppermute | solution.py:62
  129.2 15.5 %collective-permute-start.23 = (bf16[256,1024]{1,0:T(8,128)(2,1)S(1)}, bf16[256,1024]{1,0:T(8,128)(2,1)S(1)}, u32[]{:S(2)}, u32[]{:S(2)}) collective-permute-start(bf16[256,1024]{1,0:T(8,128)(2,1)S(1)} %depth.13), channel_id=1, source_target_pairs={{0,1},{64,65},{8,9},{72,73},{16,17},{80,81},{24,25},{88,89},{32,33... | collective-permute-start | bytes 1572872 | tf_op jit(solution)/shard_map/ppermute | solution.py:62
  132.1 8.6 %collective-permute-start.24 = (bf16[64,1024]{1,0:T(8,128)(2,1)S(1)}, bf16[64,1024]{1,0:T(8,128)(2,1)S(1)}, u32[]{:S(2)}, u32[]{:S(2)}) collective-permute-start(bf16[64,1024]{1,0:T(8,128)(2,1)S(1)} %add_convert_fusion.2), channel_id=1, source_target_pairs={{0,24},{64,104},{8,48},{72,96},{16,40},{80,120},{24,0},{88,112},{3... | collective-permute-start | bytes 393224 | tf_op jit(solution)/shard_map/ppermute | solution.py:62
  145.6 11.8 %collective-permute-start.26 = (bf16[160,1024]{1,0:T(8,128)(2,1)S(1)}, bf16[160,1024]{1,0:T(8,128)(2,1)S(1)}, u32[]{:S(2)}, u32[]{:S(2)}) collective-permute-start(bf16[160,1024]{1,0:T(8,128)(2,1)S(1)} %depth.15.sent_ref), channel_id=1, source_target_pairs={{0,6},{64,66},{8,14},{72,74},{16,22},{80,82},{24,30},{88,90},{32,3... | collective-permute-start | bytes 983048 | tf_op jit(solution)/shard_map/ppermute | solution.py:62
  146.9 10.5 %collective-permute-start.25 = (bf16[128,1024]{1,0:T(8,128)(2,1)S(1)}, bf16[128,1024]{1,0:T(8,128)(2,1)S(1)}, u32[]{:S(2)}, u32[]{:S(2)}) collective-permute-start(bf16[128,1024]{1,0:T(8,128)(2,1)S(1)} %depth.14), channel_id=1, source_target_pairs={{0,1},{64,65},{8,9},{72,73},{16,17},{80,81},{24,25},{88,89},{32,33... | collective-permute-start | bytes 786440 | tf_op jit(solution)/shard_map/ppermute | solution.py:62

commit v5 on v4

--- a/solution.py
+++ b/solution.py
@@ -190,8 +190,9 @@
 
 
 def gather_near(block, *meanwhile):
-    near = [send(block, Z[-k]) for k in AWAY_Z[1:NEAR_BLOCKS]]
-    return [block, *together(*near, *meanwhile)[:4]]
+    found = {k: send(block, Z[-k]) for k in (-1, 1, -2, 2)}
+    found = dict(zip(found, together(*found.values(), *meanwhile)))
+    return [block] + [found[k] for k in AWAY_Z[1:NEAR_BLOCKS]]
 
 
 def gather_far(near):

time: 160 us -> 161 us (level)
  waiting for transfers between devices: 72 us -> 70.2 us
  starting transfers between devices: 38.8 us -> 40.5 us
    ppermute x27, waiting for transfers between devices: 72 us -> 70.2 us  [send(): return lax.ppermute(value, AXES, pairs)]
    ppermute x27, starting transfers between devices: 38.8 us -> 40.5 us  [send(): return lax.ppermute(value, AXES, pairs)]
  transfers between devices with their start and end apart: 27 -> 27, of which waited for: 14 -> 13; matrix products, arithmetic and copies ran while one was open for 1% -> 1% of each run, Pallas kernels for 20% -> 20%
where the time goes in v5:
time: 161 us; the launch traced here: 159 us
  waiting for transfers between devices  70.2 us (44%)
  Pallas kernels  42.5 us (26%)
  starting transfers between devices  40.5 us (25%)
  local copies, waits for them, and re-layouts  4.01 us (2%)
    ppermute x27, waiting for transfers between devices, send(): return lax.ppermute(value, AXES, pairs)  70.2 us
    ppermute x27, starting transfers between devices, send(): return lax.ppermute(value, AXES, pairs)  40.5 us
    pallas_call x25, Pallas kernels, local(): pl.pallas_call(kernel, in_specs=[SCALARS] + [WHOLE] * len(arrays), out_sp...  36.3 us
    pallas_call x2, Pallas kernels, permute(): pl.pallas_call(functools.partial(permute_kernel, axis, orders), in_specs=...  4.46 us
    unnamed x6, local copies, waits for them, and re-layouts  3.3 us
  transfers between devices with their start and end apart: 27, of which 13 were waited for; matrix products, arithmetic and copies ran while one was open for 1% of the time, Pallas kernels for 20%

profile of v5, /device:TPU:32, one launch (start us, length us, event | category | flops | bytes accessed | tf_op | source)
XLA Modules:
  0.0 159.0 jit_solution(8982903053953980647)
XLA Ops:
  0.6 1.7 %pack.1.refs_0_ = bf16[128,1024]{1,0:T(8,128)(2,1)} custom-call(bf16[64,1024]{1,0:T(8,128)(2,1)} %a_ref.3, bf16[64,1024]{1,0:T(8,128)(2,1)} %b_ref.1), custom_call_target="tpu_custom_call" | custom-call | bytes 4096 | tf_op jit(solution)/shard_map/pack/pallas_call | solution.py:177
  2.3 5.5 %collective-permute-start.3 = (bf16[128,1024]{1,0:T(8,128)(2,1)}, bf16[128,1024]{1,0:T(8,128)(2,1)S(1)}, u32[]{:S(2)}, u32[]{:S(2)}) collective-permute-start(bf16[128,1024]{1,0:T(8,128)(2,1)} %pack.1.refs_0_), channel_id=1, source_target_pairs={{0,48},{64,112},{8,56},{72,120},{16,0},{80,64},{24,8},{88,72},{32,... | collective-permute-start | bytes 786440 | tf_op jit(solution)/shard_map/ppermute | solution.py:62
  11.2 2.2 %copy-done = bf16[2048,1024]{1,0:T(8,128)(2,1)S(1)} copy-done((bf16[2048,1024]{1,0:T(8,128)(2,1)S(1)}, bf16[2048,1024]{1,0:T(8,128)(2,1)}, u32[]{:S(2)}) %copy-start) | copy-done | bytes 4194328
  14.4 1.1 copy-done.1
  15.6 3.4 %permute_1.1 = (bf16[1024,2048]{1,0:T(8,128)(2,1)S(1)}, bf16[1024,2048]{1,0:T(8,128)(2,1)S(1)}) custom-call(s32[3]{0:T(128)S(1)} %pad_add_fusion.at_ref, bf16[1024,2048]{1,0:T(8,128)(2,1)S(1)} %copy-done.1), custom_call_target="tpu_custom_call" | custom-call | bytes 4096 | tf_op jit(solution)/shard_map/permute_1/pallas_call | solution.py:142
  19.0 5.0 %collective-permute-done.2.refs_3_ = bf16[128,1024]{1,0:T(8,128)(2,1)S(1)} collective-permute-done((bf16[128,1024]{1,0:T(8,128)(2,1)}, bf16[128,1024]{1,0:T(8,128)(2,1)S(1)}, u32[]{:S(2)}, u32[]{:S(2)}) %collective-permute-start.2) | collective-permute-done | bytes 262176 | tf_op jit(solution)/shard_map/ppermute | solution.py:62
  24.0 2.4 %collective-permute-done.refs_4_ = bf16[128,1024]{1,0:T(8,128)(2,1)S(1)} collective-permute-done((bf16[128,1024]{1,0:T(8,128)(2,1)}, bf16[128,1024]{1,0:T(8,128)(2,1)S(1)}, u32[]{:S(2)}, u32[]{:S(2)}) %collective-permute-start) | collective-permute-done | bytes 262176 | tf_op jit(solution)/shard_map/ppermute | solution.py:62
  26.4 1.4 arrange_near.1
  27.9 3.4 %collective-permute-start.5 = (bf16[128,1024]{1,0:T(8,128)(2,1)S(1)}, bf16[128,1024]{1,0:T(8,128)(2,1)S(1)}, u32[]{:S(2)}, u32[]{:S(2)}) collective-permute-start(bf16[128,1024]{1,0:T(8,128)(2,1)S(1)} %collective-permute-done.3.refs_2_), channel_id=1, source_target_pairs={{0,56},{64,120},{8,0},{72,64},{16,8},{80,72},{24,16},{88,80},{32,2... | collective-permute-start | bytes 786440 | tf_op jit(solution)/shard_map/ppermute | solution.py:62
  31.3 1.4 chip_sum.3.refs_0_
  32.7 1.6 collective-permute-start.10
  34.3 1.4 collective-permute-start.8
  35.7 2.8 %collective-permute-start.7 = (bf16[64,1024]{1,0:T(8,128)(2,1)S(1)}, bf16[64,1024]{1,0:T(8,128)(2,1)S(1)}, u32[]{:S(2)}, u32[]{:S(2)}) collective-permute-start(bf16[64,1024]{1,0:T(8,128)(2,1)S(1)} %slice.30), channel_id=1, source_target_pairs={{0,48},{64,112},{8,56},{72,120},{16,0},{80,64},{24,8},{88,72},{32,... | collective-permute-start | bytes 393224 | tf_op jit(solution)/shard_map/ppermute | solution.py:62
  38.5 7.9 %collective-permute-done.8.refs_8_ = bf16[64,1024]{1,0:T(8,128)(2,1)S(1)} collective-permute-done((bf16[64,1024]{1,0:T(8,128)(2,1)S(1)}, bf16[64,1024]{1,0:T(8,128)(2,1)S(1)}, u32[]{:S(2)}, u32[]{:S(2)}) %collective-permute-start.8) | collective-permute-done | bytes 131104 | tf_op jit(solution)/shard_map/ppermute | solution.py:62
  46.4 1.9 %arrange_far.1 = (bf16[512,1024]{1,0:T(8,128)(2,1)S(1)}, bf16[512,1024]{1,0:T(8,128)(2,1)S(1)}, bf16[192,1024]{1,0:T(8,128)(2,1)S(1)}, f32[8,1024]{1,0:T(8,128)}, f32[1,1024]{1,0:T(1,128)S(1)}) custom-call(s32[3]{0:T(128)S(1)} %pad_add_fusion.at_ref, bf16[320,1024]{1,0:T(8,128)(2,1)S(1)} %get-tuple-element.55.a_ref.tok_ref, bf16[128,1024]{1,0:T(8,128)(2,1)S(1)} %copy-done.2, ...), custom_call_target="tpu_custom_call" | custom-call | bytes 4096 | tf_op jit(solution)/shard_map/arrange_far/pallas_call | solution.py:98
  48.3 1.8 %grad_other.1 = bf16[512,1024]{1,0:T(8,128)(2,1)S(1)} custom-call(s32[3]{0:T(128)S(1)} %pad_add_fusion.at_ref, bf16[512,1024]{1,0:T(8,128)(2,1)S(1)} %get-tuple-element.82.cot_ref.a_ref.refs_1_.refs_4_.refs_5_, bf16[2048,1024]{1,0:T(8,128)(2,1)S(1)} %permute_0.1.w_ref), custom_call_target="tpu_custom_call" | custom-call | bytes 4096 | tf_op jit(solution)/shard_map/grad_other/pallas_call | solution.py:98
  50.1 1.1 chip_sum.4.refs_2_
  51.9 1.5 collective-permute-start.11
  54.1 1.8 %chip_sum.5.chip_ref = bf16[512,1024]{1,0:T(8,128)(2,1)S(1)} custom-call(s32[3]{0:T(128)S(1)} %pad_add_fusion.at_ref, bf16[512,1024]{1,0:T(8,128)(2,1)S(1)} %get-tuple-element.82.cot_ref.a_ref.refs_1_.refs_4_.refs_5_, bf16[2048,1024]{1,0:T(8,128)(2,1)S(1)} %permute_0.1.w_ref, bf16[512,1024]{1,0:T(8,128)(2,1)S(1)} %collective-permute-done.12.got_ref), custom_call_target="tpu_custom_call" | custom-call | bytes 4096 | tf_op jit(solution)/shard_map/chip_sum/pallas_call | solution.py:98
  56.0 7.0 %collective-permute-done.11.refs_3_ = bf16[192,1024]{1,0:T(8,128)(2,1)S(1)} collective-permute-done((bf16[192,1024]{1,0:T(8,128)(2,1)S(1)}, bf16[192,1024]{1,0:T(8,128)(2,1)S(1)}, u32[]{:S(2)}, u32[]{:S(2)}) %collective-permute-start.11) | collective-permute-done | bytes 393248 | tf_op jit(solution)/shard_map/ppermute | solution.py:62
  63.0 1.8 %act.1.refs_0_ = bf16[512,1024]{1,0:T(8,128)(2,1)S(1)} custom-call(s32[3]{0:T(128)S(1)} %pad_add_fusion.at_ref, bf16[320,1024]{1,0:T(8,128)(2,1)S(1)} %chip_sum.3.refs_0_, bf16[320,1024]{1,0:T(8,128)(2,1)S(1)} %collective-permute-done.10.refs_1_, bf16[192,1024]{1,0:T(8,128)(2,1)S(1)} %chip_sum.4.refs_2_, ...), custom_call_target="tpu_custom_call" | custom-call | bytes 4096 | tf_op jit(solution)/shard_map/act/pallas_call | solution.py:98
  64.9 1.6 collective-permute-start.14
  66.5 1.3 depth.8
  67.8 1.7 %collective-permute-start.15 = (bf16[512,1024]{1,0:T(8,128)(2,1)S(1)}, bf16[512,1024]{1,0:T(8,128)(2,1)S(1)}, u32[]{:S(2)}, u32[]{:S(2)}) collective-permute-start(bf16[512,1024]{1,0:T(8,128)(2,1)S(1)} %depth.8), channel_id=1, source_target_pairs={{0,2},{64,70},{8,10},{72,78},{16,18},{80,86},{24,26},{88,94},{32,3... | collective-permute-start | bytes 3145736 | tf_op jit(solution)/shard_map/ppermute | solution.py:62
  69.5 1.3 depth.9
  71.3 2.4 %slope.1.slope_ref = f32[512,1024]{1,0:T(8,128)S(1)} custom-call(s32[3]{0:T(128)S(1)} %pad_add_fusion.at_ref, bf16[320,1024]{1,0:T(8,128)(2,1)S(1)} %chip_sum.3.refs_0_, bf16[320,1024]{1,0:T(8,128)(2,1)S(1)} %collective-permute-done.10.refs_1_, bf16[192,1024]{1,0:T(8,128)(2,1)S(1)} %chip_sum.4.refs_2_, ...), custom_call_target="tpu_custom_call" | custom-call | bytes 4096 | tf_op jit(solution)/shard_map/slope/pallas_call | solution.py:98
  74.9 15.6 %collective-permute-done.14.got_ref = bf16[512,1024]{1,0:T(8,128)(2,1)S(1)} collective-permute-done((bf16[512,1024]{1,0:T(8,128)(2,1)S(1)}, bf16[512,1024]{1,0:T(8,128)(2,1)S(1)}, u32[]{:S(2)}, u32[]{:S(2)}) %collective-permute-start.14) | collective-permute-done | bytes 1048608 | tf_op jit(solution)/shard_map/ppermute | solution.py:62
  90.5 1.8 %pre_grad.1.refs_7_.refs_2_.own_ref.refs_1_ = bf16[528,1024]{1,0:T(8,128)(2,1)S(1)} custom-call(s32[3]{0:T(128)S(1)} %pad_add_fusion.at_ref, f32[512,1024]{1,0:T(8,128)S(1)} %slope.1.slope_ref, bf16[512,1024]{1,0:T(8,128)(2,1)S(1)} %chip_sum.5.chip_ref, bf16[512,1024]{1,0:T(8,128)(2,1)S(1)} %collective-permute-done.14.got_ref), custom_call_target="tpu_custom_call" | custom-call | bytes 4096 | tf_op jit(solution)/shard_map/pre_grad/pallas_call | solution.py:98
  92.7 1.3 collective-permute-done.16.refs_5_.refs_6_
  93.9 1.9 %depth.10 = bf16[1024,1024]{1,0:T(8,128)(2,1)S(1)} custom-call(s32[3]{0:T(128)S(1)} %pad_add_fusion.at_ref, bf16[512,1024]{1,0:T(8,128)(2,1)S(1)} %act.1.refs_0_, bf16[512,1024]{1,0:T(8,128)(2,1)S(1)} %get-tuple-element.82.cot_ref.a_ref.refs_1_.refs_4_.refs_5_, bf16[512,1024]{1,0:T(8,128)(2,1)S(1)} %collective-permute-done.15.refs_2_, ...), custom_call_target="tpu_custom_call" | custom-call | bytes 4096 | tf_op jit(solution)/shard_map/depth/pallas_call | solution.py:98
  95.8 3.1 %collective-permute-start.19 = (bf16[1024,1024]{1,0:T(8,128)(2,1)S(1)}, bf16[1024,1024]{1,0:T(8,128)(2,1)S(1)}, u32[]{:S(2)}, u32[]{:S(2)}) collective-permute-start(bf16[1024,1024]{1,0:T(8,128)(2,1)S(1)} %depth.10), channel_id=1, source_target_pairs={{0,6},{64,66},{8,14},{72,74},{16,22},{80,82},{24,30},{88,90},{32,3... | collective-permute-start | bytes 6291464 | tf_op jit(solution)/shard_map/ppermute | solution.py:62
  98.9 1.3 depth.11.refs_6_
  100.2 2.8 %collective-permute-start.20 = (bf16[528,1024]{1,0:T(8,128)(2,1)S(1)}, bf16[528,1024]{1,0:T(8,128)(2,1)S(1)}, u32[]{:S(2)}, u32[]{:S(2)}) collective-permute-start(bf16[528,1024]{1,0:T(8,128)(2,1)S(1)} %depth.11.refs_6_), channel_id=1, source_target_pairs={{0,1},{64,65},{8,9},{72,73},{16,17},{80,81},{24,25},{88,89},{32,33... | collective-permute-start | bytes 3244040 | tf_op jit(solution)/shard_map/ppermute | solution.py:62
  103.0 3.0 %inputs_grad.1 = (f32[512,1024]{1,0:T(8,128)S(1)}, bf16[256,1024]{1,0:T(8,128)(2,1)S(1)}) custom-call(s32[3]{0:T(128)S(1)} %pad_add_fusion.at_ref, bf16[528,1024]{1,0:T(8,128)(2,1)S(1)} %pre_grad.1.refs_7_.refs_2_.own_ref.refs_1_, bf16[528,1024]{1,0:T(8,128)(2,1)S(1)} %collective-permute-done.17.refs_1_.refs_3_.away_ref.refs_4_, ...), custom_call_target="tpu_custom_call" | custom-call | bytes 4096 | tf_op jit(solution)/shard_map/inputs_grad/pallas_call | solution.py:98
  106.1 1.4 collective-permute-start.18
  107.5 7.9 %collective-permute-done.18 = bf16[256,1024]{1,0:T(8,128)(2,1)S(1)} collective-permute-done((bf16[256,1024]{1,0:T(8,128)(2,1)S(1)}, bf16[256,1024]{1,0:T(8,128)(2,1)S(1)}, u32[]{:S(2)}, u32[]{:S(2)}) %collective-permute-start.18) | collective-permute-done | bytes 524320 | tf_op jit(solution)/shard_map/ppermute | solution.py:62
  115.5 6.4 %collective-permute-done.21 = bf16[128,1024]{1,0:T(8,128)(2,1)S(1)} collective-permute-done((bf16[128,1024]{1,0:T(8,128)(2,1)S(1)}, bf16[128,1024]{1,0:T(8,128)(2,1)S(1)}, u32[]{:S(2)}, u32[]{:S(2)}) %collective-permute-start.21) | collective-permute-done | bytes 262176 | tf_op jit(solution)/shard_map/ppermute | solution.py:62
  121.9 3.3 %collective-permute-done.20.refs_5_.refs_2_ = bf16[528,1024]{1,0:T(8,128)(2,1)S(1)} collective-permute-done((bf16[528,1024]{1,0:T(8,128)(2,1)S(1)}, bf16[528,1024]{1,0:T(8,128)(2,1)S(1)}, u32[]{:S(2)}, u32[]{:S(2)}) %collective-permute-start.20) | collective-permute-done | bytes 1081376 | tf_op jit(solution)/shard_map/ppermute | solution.py:62
  125.2 1.3 depth.12.refs_4_
  126.5 1.5 collective-permute-start.22
  129.1 2.8 %collective-permute-start.23 = (bf16[256,1024]{1,0:T(8,128)(2,1)S(1)}, bf16[256,1024]{1,0:T(8,128)(2,1)S(1)}, u32[]{:S(2)}, u32[]{:S(2)}) collective-permute-start(bf16[256,1024]{1,0:T(8,128)(2,1)S(1)} %depth.13), channel_id=1, source_target_pairs={{0,1},{64,65},{8,9},{72,73},{16,17},{80,81},{24,25},{88,89},{32,33... | collective-permute-start | bytes 1572872 | tf_op jit(solution)/shard_map/ppermute | solution.py:62
  132.0 2.4 %collective-permute-start.24 = (bf16[64,1024]{1,0:T(8,128)(2,1)S(1)}, bf16[64,1024]{1,0:T(8,128)(2,1)S(1)}, u32[]{:S(2)}, u32[]{:S(2)}) collective-permute-start(bf16[64,1024]{1,0:T(8,128)(2,1)S(1)} %add_convert_fusion.2), channel_id=1, source_target_pairs={{0,24},{64,104},{8,48},{72,96},{16,40},{80,120},{24,0},{88,112},{3... | collective-permute-start | bytes 393224 | tf_op jit(solution)/shard_map/ppermute | solution.py:62
  135.4 7.0 %collective-permute-done.24 = bf16[64,1024]{1,0:T(8,128)(2,1)S(1)} collective-permute-done((bf16[64,1024]{1,0:T(8,128)(2,1)S(1)}, bf16[64,1024]{1,0:T(8,128)(2,1)S(1)}, u32[]{:S(2)}, u32[]{:S(2)}) %collective-permute-start.24) | collective-permute-done | bytes 131104 | tf_op jit(solution)/shard_map/ppermute | solution.py:62
  142.4 2.2 %collective-permute-done.23.got_ref = bf16[256,1024]{1,0:T(8,128)(2,1)S(1)} collective-permute-done((bf16[256,1024]{1,0:T(8,128)(2,1)S(1)}, bf16[256,1024]{1,0:T(8,128)(2,1)S(1)}, u32[]{:S(2)}, u32[]{:S(2)}) %collective-permute-start.23) | collective-permute-done | bytes 524320 | tf_op jit(solution)/shard_map/ppermute | solution.py:62
  146.8 2.9 %collective-permute-start.25 = (bf16[128,1024]{1,0:T(8,128)(2,1)S(1)}, bf16[128,1024]{1,0:T(8,128)(2,1)S(1)}, u32[]{:S(2)}, u32[]{:S(2)}) collective-permute-start(bf16[128,1024]{1,0:T(8,128)(2,1)S(1)} %depth.14), channel_id=1, source_target_pairs={{0,1},{64,65},{8,9},{72,73},{16,17},{80,81},{24,25},{88,89},{32,33... | collective-permute-start | bytes 786440 | tf_op jit(solution)/shard_map/ppermute | solution.py:62
  151.5 1.6 %place_rows.1 = f32[256,1024]{1,0:T(8,128)} custom-call(s32[3]{0:T(128)S(1)} %pad_add_fusion.at_ref, f32[256,1024]{1,0:T(8,128)S(1)} %depth_kept.3.keep_ref, bf16[256,1024]{1,0:T(8,128)(2,1)S(1)} %collective-permute-done.23.got_ref), custom_call_target="tpu_custom_call" | custom-call | bytes 4096 | tf_op jit(solution)/shard_map/place_rows/pallas_call | solution.py:98
  153.8 3.5 %collective-permute-done.25.got_ref = bf16[128,1024]{1,0:T(8,128)(2,1)S(1)} collective-permute-done((bf16[128,1024]{1,0:T(8,128)(2,1)S(1)}, bf16[128,1024]{1,0:T(8,128)(2,1)S(1)}, u32[]{:S(2)}, u32[]{:S(2)}) %collective-permute-start.25) | collective-permute-done | bytes 262176 | tf_op jit(solution)/shard_map/ppermute | solution.py:62
  157.3 1.7 %place_columns.1 = (f32[128,2048]{1,0:T(8,128)}, f32[16,128]{1,0:T(8,128)}, f32[8,128]{1,0:T(8,128)}) custom-call(s32[3]{0:T(128)S(1)} %pad_add_fusion.at_ref, f32[128,1024]{1,0:T(8,128)S(1)} %depth_kept.4.keep_ref, bf16[128,1024]{1,0:T(8,128)(2,1)S(1)} %collective-permute-done.25.got_ref, f32[128,1024]{1,0:T(8,128)S(1)} %depth_kept.5.keep2_ref, ...), custom_call_target="tpu_custom_call" | custom-call | bytes 4096 | tf_op jit(solution)/shard_map/place_columns/pallas_call | solution.py:98
  (47 shorter events, 15.1 us)
Async XLA Ops:
  2.3 16.6 %collective-permute-start.3 = (bf16[128,1024]{1,0:T(8,128)(2,1)}, bf16[128,1024]{1,0:T(8,128)(2,1)S(1)}, u32[]{:S(2)}, u32[]{:S(2)}) collective-permute-start(bf16[128,1024]{1,0:T(8,128)(2,1)} %pack.1.refs_0_), channel_id=1, source_target_pairs={{0,48},{64,112},{8,56},{72,120},{16,0},{80,64},{24,8},{88,72},{32,... | collective-permute-start | bytes 786440 | tf_op jit(solution)/shard_map/ppermute | solution.py:62
  7.8 16.1 %collective-permute-start.2 = (bf16[128,1024]{1,0:T(8,128)(2,1)}, bf16[128,1024]{1,0:T(8,128)(2,1)S(1)}, u32[]{:S(2)}, u32[]{:S(2)}) collective-permute-start(bf16[128,1024]{1,0:T(8,128)(2,1)} %pack.1.refs_0_), channel_id=1, source_target_pairs={{0,16},{64,80},{8,24},{72,88},{16,32},{80,96},{24,40},{88,104},{32... | collective-permute-start | bytes 786440 | tf_op jit(solution)/shard_map/ppermute | solution.py:62
  7.8 16.1 %collective-permute-start.1 = (bf16[128,1024]{1,0:T(8,128)(2,1)}, bf16[128,1024]{1,0:T(8,128)(2,1)S(1)}, u32[]{:S(2)}, u32[]{:S(2)}) collective-permute-start(bf16[128,1024]{1,0:T(8,128)(2,1)} %pack.1.refs_0_), channel_id=1, source_target_pairs={{0,56},{64,120},{8,0},{72,64},{16,8},{80,72},{24,16},{88,80},{32,2... | collective-permute-start | bytes 786440 | tf_op jit(solution)/shard_map/ppermute | solution.py:62
  8.8 17.5 %collective-permute-start = (bf16[128,1024]{1,0:T(8,128)(2,1)}, bf16[128,1024]{1,0:T(8,128)(2,1)S(1)}, u32[]{:S(2)}, u32[]{:S(2)}) collective-permute-start(bf16[128,1024]{1,0:T(8,128)(2,1)} %pack.1.refs_0_), channel_id=1, source_target_pairs={{0,8},{64,72},{8,16},{72,80},{16,24},{80,88},{24,32},{88,96},{32,4... | collective-permute-start | bytes 786440 | tf_op jit(solution)/shard_map/ppermute | solution.py:62
  11.2 2.2 %copy-start = (bf16[2048,1024]{1,0:T(8,128)(2,1)S(1)}, bf16[2048,1024]{1,0:T(8,128)(2,1)}, u32[]{:S(2)}) copy-start(bf16[2048,1024]{1,0:T(8,128)(2,1)} %a_ref.5) | copy-start | bytes 12582916
  13.4 2.2 %copy-start.1 = (bf16[1024,2048]{1,0:T(8,128)(2,1)S(1)}, bf16[1024,2048]{1,0:T(8,128)(2,1)}, u32[]{:S(2)}) copy-start(bf16[1024,2048]{1,0:T(8,128)(2,1)} %a_ref.4) | copy-start | bytes 12582916
  15.6 10.8 %copy-start.2 = (bf16[128,1024]{1,0:T(8,128)(2,1)S(1)}, bf16[128,1024]{1,0:T(8,128)(2,1)}, u32[]{:S(2)}) copy-start(bf16[128,1024]{1,0:T(8,128)(2,1)} %pack.1.refs_0_) | copy-start | bytes 786436
  27.8 3.5 %collective-permute-start.4 = (bf16[320,1024]{1,0:T(8,128)(2,1)S(1)}, bf16[320,1024]{1,0:T(8,128)(2,1)S(1)}, u32[]{:S(2)}, u32[]{:S(2)}) collective-permute-start(bf16[320,1024]{1,0:T(8,128)(2,1)S(1)} %get-tuple-element.56), channel_id=1, source_target_pairs={{0,64},{64,0},{8,72},{72,8},{16,80},{80,16},{24,88},{88,24},{32,96... | collective-permute-start | bytes 1966088 | tf_op jit(solution)/shard_map/ppermute | solution.py:62
  27.9 18.5 %collective-permute-start.5 = (bf16[128,1024]{1,0:T(8,128)(2,1)S(1)}, bf16[128,1024]{1,0:T(8,128)(2,1)S(1)}, u32[]{:S(2)}, u32[]{:S(2)}) collective-permute-start(bf16[128,1024]{1,0:T(8,128)(2,1)S(1)} %collective-permute-done.3.refs_2_), channel_id=1, source_target_pairs={{0,56},{64,120},{8,0},{72,64},{16,8},{80,72},{24,16},{88,80},{32,2... | collective-permute-start | bytes 786440 | tf_op jit(solution)/shard_map/ppermute | solution.py:62
  31.3 15.1 %collective-permute-start.6 = (bf16[128,1024]{1,0:T(8,128)(2,1)S(1)}, bf16[128,1024]{1,0:T(8,128)(2,1)S(1)}, u32[]{:S(2)}, u32[]{:S(2)}) collective-permute-start(bf16[128,1024]{1,0:T(8,128)(2,1)S(1)} %collective-permute-done.2.refs_3_), channel_id=1, source_target_pairs={{0,8},{64,72},{8,16},{72,80},{16,24},{80,88},{24,32},{88,96},{32,4... | collective-permute-start | bytes 786440 | tf_op jit(solution)/shard_map/ppermute | solution.py:62
  32.7 17.5 %collective-permute-start.10 = (bf16[320,1024]{1,0:T(8,128)(2,1)S(1)}, bf16[320,1024]{1,0:T(8,128)(2,1)S(1)}, u32[]{:S(2)}, u32[]{:S(2)}) collective-permute-start(bf16[320,1024]{1,0:T(8,128)(2,1)S(1)} %chip_sum.3.refs_0_), channel_id=1, source_target_pairs={{0,128},{64,192},{8,136},{72,200},{16,144},{80,208},{24,152},{88,2... | collective-permute-start | bytes 1966088 | tf_op jit(solution)/shard_map/ppermute | solution.py:62
  34.3 12.1 %collective-permute-start.8 = (bf16[64,1024]{1,0:T(8,128)(2,1)S(1)}, bf16[64,1024]{1,0:T(8,128)(2,1)S(1)}, u32[]{:S(2)}, u32[]{:S(2)}) collective-permute-start(bf16[64,1024]{1,0:T(8,128)(2,1)S(1)} %slice.31), channel_id=1, source_target_pairs={{0,16},{64,80},{8,24},{72,88},{16,32},{80,96},{24,40},{88,104},{32... | collective-permute-start | bytes 393224 | tf_op jit(solution)/shard_map/ppermute | solution.py:62
  35.7 10.6 %collective-permute-start.7 = (bf16[64,1024]{1,0:T(8,128)(2,1)S(1)}, bf16[64,1024]{1,0:T(8,128)(2,1)S(1)}, u32[]{:S(2)}, u32[]{:S(2)}) collective-permute-start(bf16[64,1024]{1,0:T(8,128)(2,1)S(1)} %slice.30), channel_id=1, source_target_pairs={{0,48},{64,112},{8,56},{72,120},{16,0},{80,64},{24,8},{88,72},{32,... | collective-permute-start | bytes 393224 | tf_op jit(solution)/shard_map/ppermute | solution.py:62
  48.3 1.8 %collective-permute-start.9 = (bf16[192,1024]{1,0:T(8,128)(2,1)S(1)}, bf16[192,1024]{1,0:T(8,128)(2,1)S(1)}, u32[]{:S(2)}, u32[]{:S(2)}) collective-permute-start(bf16[192,1024]{1,0:T(8,128)(2,1)S(1)} %get-tuple-element.57), channel_id=1, source_target_pairs={{0,64},{64,0},{8,72},{72,8},{16,80},{80,16},{24,88},{88,24},{32,96... | collective-permute-start | bytes 1179656 | tf_op jit(solution)/shard_map/ppermute | solution.py:62
  51.3 2.9 %collective-permute-start.12 = (bf16[512,1024]{1,0:T(8,128)(2,1)S(1)}, bf16[512,1024]{1,0:T(8,128)(2,1)S(1)}, u32[]{:S(2)}, u32[]{:S(2)}) collective-permute-start(bf16[512,1024]{1,0:T(8,128)(2,1)S(1)} %grad_other.1), channel_id=1, source_target_pairs={{0,64},{64,0},{8,72},{72,8},{16,80},{80,16},{24,88},{88,24},{32,96... | collective-permute-start | bytes 3145736 | tf_op jit(solution)/shard_map/ppermute | solution.py:62
  51.9 11.1 %collective-permute-start.11 = (bf16[192,1024]{1,0:T(8,128)(2,1)S(1)}, bf16[192,1024]{1,0:T(8,128)(2,1)S(1)}, u32[]{:S(2)}, u32[]{:S(2)}) collective-permute-start(bf16[192,1024]{1,0:T(8,128)(2,1)S(1)} %chip_sum.4.refs_2_), channel_id=1, source_target_pairs={{0,128},{64,192},{8,136},{72,200},{16,144},{80,208},{24,152},{88,2... | collective-permute-start | bytes 1179656 | tf_op jit(solution)/shard_map/ppermute | solution.py:62
  64.8 4.7 %collective-permute-start.13 = (bf16[512,1024]{1,0:T(8,128)(2,1)S(1)}, bf16[512,1024]{1,0:T(8,128)(2,1)S(1)}, u32[]{:S(2)}, u32[]{:S(2)}) collective-permute-start(bf16[512,1024]{1,0:T(8,128)(2,1)S(1)} %act.1.refs_0_), channel_id=1, source_target_pairs={{0,64},{64,0},{8,72},{72,8},{16,80},{80,16},{24,88},{88,24},{32,96... | collective-permute-start | bytes 3145736 | tf_op jit(solution)/shard_map/ppermute | solution.py:62
  64.9 25.6 %collective-permute-start.14 = (bf16[512,1024]{1,0:T(8,128)(2,1)S(1)}, bf16[512,1024]{1,0:T(8,128)(2,1)S(1)}, u32[]{:S(2)}, u32[]{:S(2)}) collective-permute-start(bf16[512,1024]{1,0:T(8,128)(2,1)S(1)} %chip_sum.5.chip_ref), channel_id=1, source_target_pairs={{0,128},{64,192},{8,136},{72,200},{16,144},{80,208},{24,152},{88,2... | collective-permute-start | bytes 3145736 | tf_op jit(solution)/shard_map/ppermute | solution.py:62
  67.8 24.8 %collective-permute-start.15 = (bf16[512,1024]{1,0:T(8,128)(2,1)S(1)}, bf16[512,1024]{1,0:T(8,128)(2,1)S(1)}, u32[]{:S(2)}, u32[]{:S(2)}) collective-permute-start(bf16[512,1024]{1,0:T(8,128)(2,1)S(1)} %depth.8), channel_id=1, source_target_pairs={{0,2},{64,70},{8,10},{72,78},{16,18},{80,86},{24,26},{88,94},{32,3... | collective-permute-start | bytes 3145736 | tf_op jit(solution)/shard_map/ppermute | solution.py:62
  70.8 23.1 %collective-permute-start.16 = (bf16[512,1024]{1,0:T(8,128)(2,1)S(1)}, bf16[512,1024]{1,0:T(8,128)(2,1)S(1)}, u32[]{:S(2)}, u32[]{:S(2)}) collective-permute-start(bf16[512,1024]{1,0:T(8,128)(2,1)S(1)} %depth.9), channel_id=1, source_target_pairs={{0,2},{64,70},{8,10},{72,78},{16,18},{80,86},{24,26},{88,94},{32,3... | collective-permute-start | bytes 3145736 | tf_op jit(solution)/shard_map/ppermute | solution.py:62
  92.3 6.6 %collective-permute-start.17 = (bf16[528,1024]{1,0:T(8,128)(2,1)S(1)}, bf16[528,1024]{1,0:T(8,128)(2,1)S(1)}, u32[]{:S(2)}, u32[]{:S(2)}) collective-permute-start(bf16[528,1024]{1,0:T(8,128)(2,1)S(1)} %pre_grad.1.refs_7_.refs_2_.own_ref.refs_1_), channel_id=1, source_target_pairs={{0,64},{64,0},{8,72},{72,8},{16,80},{80,16},{24,88},{88,24},{32,96... | collective-permute-start | bytes 3244040 | tf_op jit(solution)/shard_map/ppermute | solution.py:62
  95.8 29.4 %collective-permute-start.19 = (bf16[1024,1024]{1,0:T(8,128)(2,1)S(1)}, bf16[1024,1024]{1,0:T(8,128)(2,1)S(1)}, u32[]{:S(2)}, u32[]{:S(2)}) collective-permute-start(bf16[1024,1024]{1,0:T(8,128)(2,1)S(1)} %depth.10), channel_id=1, source_target_pairs={{0,6},{64,66},{8,14},{72,74},{16,22},{80,82},{24,30},{88,90},{32,3... | collective-permute-start | bytes 6291464 | tf_op jit(solution)/shard_map/ppermute | solution.py:62
  100.2 24.9 %collective-permute-start.20 = (bf16[528,1024]{1,0:T(8,128)(2,1)S(1)}, bf16[528,1024]{1,0:T(8,128)(2,1)S(1)}, u32[]{:S(2)}, u32[]{:S(2)}) collective-permute-start(bf16[528,1024]{1,0:T(8,128)(2,1)S(1)} %depth.11.refs_6_), channel_id=1, source_target_pairs={{0,1},{64,65},{8,9},{72,73},{16,17},{80,81},{24,25},{88,89},{32,33... | collective-permute-start | bytes 3244040 | tf_op jit(solution)/shard_map/ppermute | solution.py:62
  106.1 9.3 %collective-permute-start.18 = (bf16[256,1024]{1,0:T(8,128)(2,1)S(1)}, bf16[256,1024]{1,0:T(8,128)(2,1)S(1)}, u32[]{:S(2)}, u32[]{:S(2)}) collective-permute-start(bf16[256,1024]{1,0:T(8,128)(2,1)S(1)} %get-tuple-element.78), channel_id=1, source_target_pairs={{0,8},{64,120},{8,0},{72,80},{16,24},{80,72},{24,16},{88,96},{32,4... | collective-permute-start | bytes 1572872 | tf_op jit(solution)/shard_map/ppermute | solution.py:62
  115.4 6.5 %collective-permute-start.21 = (bf16[128,1024]{1,0:T(8,128)(2,1)S(1)}, bf16[128,1024]{1,0:T(8,128)(2,1)S(1)}, u32[]{:S(2)}, u32[]{:S(2)}) collective-permute-start(bf16[128,1024]{1,0:T(8,128)(2,1)S(1)} %add_convert_fusion), channel_id=1, source_target_pairs={{0,56},{64,72},{8,16},{72,64},{16,8},{80,88},{24,32},{88,80},{32,2... | collective-permute-start | bytes 786440 | tf_op jit(solution)/shard_map/ppermute | solution.py:62
  126.5 18.1 %collective-permute-start.22 = (bf16[528,1024]{1,0:T(8,128)(2,1)S(1)}, bf16[528,1024]{1,0:T(8,128)(2,1)S(1)}, u32[]{:S(2)}, u32[]{:S(2)}) collective-permute-start(bf16[528,1024]{1,0:T(8,128)(2,1)S(1)} %depth.12.refs_4_), channel_id=1, source_target_pairs={{0,2},{64,70},{8,10},{72,78},{16,18},{80,86},{24,26},{88,94},{32,3... | collective-permute-start | bytes 3244040 | tf_op jit(solution)/shard_map/ppermute | solution.py:62
  129.1 15.5 %collective-permute-start.23 = (bf16[256,1024]{1,0:T(8,128)(2,1)S(1)}, bf16[256,1024]{1,0:T(8,128)(2,1)S(1)}, u32[]{:S(2)}, u32[]{:S(2)}) collective-permute-start(bf16[256,1024]{1,0:T(8,128)(2,1)S(1)} %depth.13), channel_id=1, source_target_pairs={{0,1},{64,65},{8,9},{72,73},{16,17},{80,81},{24,25},{88,89},{32,33... | collective-permute-start | bytes 1572872 | tf_op jit(solution)/shard_map/ppermute | solution.py:62
  132.0 10.4 %collective-permute-start.24 = (bf16[64,1024]{1,0:T(8,128)(2,1)S(1)}, bf16[64,1024]{1,0:T(8,128)(2,1)S(1)}, u32[]{:S(2)}, u32[]{:S(2)}) collective-permute-start(bf16[64,1024]{1,0:T(8,128)(2,1)S(1)} %add_convert_fusion.2), channel_id=1, source_target_pairs={{0,24},{64,104},{8,48},{72,96},{16,40},{80,120},{24,0},{88,112},{3... | collective-permute-start | bytes 393224 | tf_op jit(solution)/shard_map/ppermute | solution.py:62
  145.5 11.8 %collective-permute-start.26 = (bf16[160,1024]{1,0:T(8,128)(2,1)S(1)}, bf16[160,1024]{1,0:T(8,128)(2,1)S(1)}, u32[]{:S(2)}, u32[]{:S(2)}) collective-permute-start(bf16[160,1024]{1,0:T(8,128)(2,1)S(1)} %depth.15.sent_ref), channel_id=1, source_target_pairs={{0,6},{64,66},{8,14},{72,74},{16,22},{80,82},{24,30},{88,90},{32,3... | collective-permute-start | bytes 983048 | tf_op jit(solution)/shard_map/ppermute | solution.py:62
  146.8 10.6 %collective-permute-start.25 = (bf16[128,1024]{1,0:T(8,128)(2,1)S(1)}, bf16[128,1024]{1,0:T(8,128)(2,1)S(1)}, u32[]{:S(2)}, u32[]{:S(2)}) collective-permute-start(bf16[128,1024]{1,0:T(8,128)(2,1)S(1)} %depth.14), channel_id=1, source_target_pairs={{0,1},{64,65},{8,9},{72,73},{16,17},{80,81},{24,25},{88,89},{32,33... | collective-permute-start | bytes 786440 | tf_op jit(solution)/shard_map/ppermute | solution.py:62

commit v6 on v5

--- a/solution.py
+++ b/solution.py
@@ -190,7 +190,7 @@
 
 
 def gather_near(block, *meanwhile):
-    found = {k: send(block, Z[-k]) for k in (-1, 1, -2, 2)}
+    found = {k: send(block, Z[-k]) for k in (2, -2, 1, -1)}
     found = dict(zip(found, together(*found.values(), *meanwhile)))
     return [block] + [found[k] for k in AWAY_Z[1:NEAR_BLOCKS]]
 

time: 161 us -> 158 us (0.981); the launches traced: 159 us -> 158 us
  waiting for transfers between devices: 70.2 us -> 68.2 us
    ppermute x27, waiting for transfers between devices: 70.2 us -> 68.2 us  [send(): return lax.ppermute(value, AXES, pairs)]
  transfers between devices with their start and end apart: 27 -> 27, of which waited for: 13 -> 13; matrix products, arithmetic and copies ran while one was open for 1% -> 1% of each run, Pallas kernels for 20% -> 21%
where the time goes in v6:
time: 158 us
  waiting for transfers between devices  68.2 us (43%)
  Pallas kernels  42.4 us (27%)
  starting transfers between devices  41.3 us (26%)
  local copies, waits for them, and re-layouts  4.01 us (3%)
    ppermute x27, waiting for transfers between devices, send(): return lax.ppermute(value, AXES, pairs)  68.2 us
    ppermute x27, starting transfers between devices, send(): return lax.ppermute(value, AXES, pairs)  41.3 us
    pallas_call x25, Pallas kernels, local(): pl.pallas_call(kernel, in_specs=[SCALARS] + [WHOLE] * len(arrays), out_sp...  36.3 us
    pallas_call x2, Pallas kernels, permute(): pl.pallas_call(functools.partial(permute_kernel, axis, orders), in_specs=...  4.46 us
    unnamed x6, local copies, waits for them, and re-layouts  3.3 us
  transfers between devices with their start and end apart: 27, of which 13 were waited for; matrix products, arithmetic and copies ran while one was open for 1% of the time, Pallas kernels for 21%

profile of v6, /device:TPU:32, one launch (start us, length us, event | category | flops | bytes accessed | tf_op | source)
XLA Modules:
  0.0 157.8 jit_solution(2181449133230258401)
XLA Ops:
  0.6 1.7 %pack.1.refs_0_ = bf16[128,1024]{1,0:T(8,128)(2,1)} custom-call(bf16[64,1024]{1,0:T(8,128)(2,1)} %a_ref.3, bf16[64,1024]{1,0:T(8,128)(2,1)} %b_ref.1), custom_call_target="tpu_custom_call" | custom-call | bytes 4096 | tf_op jit(solution)/shard_map/pack/pallas_call | solution.py:177
  2.3 2.0 %collective-permute-start.3 = (bf16[128,1024]{1,0:T(8,128)(2,1)}, bf16[128,1024]{1,0:T(8,128)(2,1)S(1)}, u32[]{:S(2)}, u32[]{:S(2)}) collective-permute-start(bf16[128,1024]{1,0:T(8,128)(2,1)} %pack.1.refs_0_), channel_id=1, source_target_pairs={{0,8},{64,72},{8,16},{72,80},{16,24},{80,88},{24,32},{88,96},{32,4... | collective-permute-start | bytes 786440 | tf_op jit(solution)/shard_map/ppermute | solution.py:62
  4.4 4.4 %collective-permute-start.1 = (bf16[128,1024]{1,0:T(8,128)(2,1)}, bf16[128,1024]{1,0:T(8,128)(2,1)S(1)}, u32[]{:S(2)}, u32[]{:S(2)}) collective-permute-start(bf16[128,1024]{1,0:T(8,128)(2,1)} %pack.1.refs_0_), channel_id=1, source_target_pairs={{0,16},{64,80},{8,24},{72,88},{16,32},{80,96},{24,40},{88,104},{32... | collective-permute-start | bytes 786440 | tf_op jit(solution)/shard_map/ppermute | solution.py:62
  11.2 2.2 %copy-done = bf16[2048,1024]{1,0:T(8,128)(2,1)S(1)} copy-done((bf16[2048,1024]{1,0:T(8,128)(2,1)S(1)}, bf16[2048,1024]{1,0:T(8,128)(2,1)}, u32[]{:S(2)}) %copy-start) | copy-done | bytes 4194328
  14.4 1.1 copy-done.1
  15.6 3.4 %permute_1.1 = (bf16[1024,2048]{1,0:T(8,128)(2,1)S(1)}, bf16[1024,2048]{1,0:T(8,128)(2,1)S(1)}) custom-call(s32[3]{0:T(128)S(1)} %pad_add_fusion.at_ref, bf16[1024,2048]{1,0:T(8,128)(2,1)S(1)} %copy-done.1), custom_call_target="tpu_custom_call" | custom-call | bytes 4096 | tf_op jit(solution)/shard_map/permute_1/pallas_call | solution.py:142
  19.0 6.6 %collective-permute-done.1.refs_3_ = bf16[128,1024]{1,0:T(8,128)(2,1)S(1)} collective-permute-done((bf16[128,1024]{1,0:T(8,128)(2,1)}, bf16[128,1024]{1,0:T(8,128)(2,1)S(1)}, u32[]{:S(2)}, u32[]{:S(2)}) %collective-permute-start.1) | collective-permute-done | bytes 262176 | tf_op jit(solution)/shard_map/ppermute | solution.py:62
  25.6 1.4 arrange_near.1
  27.1 3.7 %collective-permute-start.6 = (bf16[128,1024]{1,0:T(8,128)(2,1)S(1)}, bf16[128,1024]{1,0:T(8,128)(2,1)S(1)}, u32[]{:S(2)}, u32[]{:S(2)}) collective-permute-start(bf16[128,1024]{1,0:T(8,128)(2,1)S(1)} %collective-permute-done.1.refs_3_), channel_id=1, source_target_pairs={{0,8},{64,72},{8,16},{72,80},{16,24},{80,88},{24,32},{88,96},{32,4... | collective-permute-start | bytes 786440 | tf_op jit(solution)/shard_map/ppermute | solution.py:62
  30.9 1.4 chip_sum.3.refs_0_
  32.3 1.6 collective-permute-start.10
  33.9 1.4 collective-permute-start.8
  35.3 2.8 %collective-permute-start.7 = (bf16[64,1024]{1,0:T(8,128)(2,1)S(1)}, bf16[64,1024]{1,0:T(8,128)(2,1)S(1)}, u32[]{:S(2)}, u32[]{:S(2)}) collective-permute-start(bf16[64,1024]{1,0:T(8,128)(2,1)S(1)} %slice.30), channel_id=1, source_target_pairs={{0,48},{64,112},{8,56},{72,120},{16,0},{80,64},{24,8},{88,72},{32,... | collective-permute-start | bytes 393224 | tf_op jit(solution)/shard_map/ppermute | solution.py:62
  38.1 6.4 %collective-permute-done.8.refs_8_ = bf16[64,1024]{1,0:T(8,128)(2,1)S(1)} collective-permute-done((bf16[64,1024]{1,0:T(8,128)(2,1)S(1)}, bf16[64,1024]{1,0:T(8,128)(2,1)S(1)}, u32[]{:S(2)}, u32[]{:S(2)}) %collective-permute-start.8) | collective-permute-done | bytes 131104 | tf_op jit(solution)/shard_map/ppermute | solution.py:62
  44.5 1.9 %arrange_far.1 = (bf16[512,1024]{1,0:T(8,128)(2,1)S(1)}, bf16[512,1024]{1,0:T(8,128)(2,1)S(1)}, bf16[192,1024]{1,0:T(8,128)(2,1)S(1)}, f32[8,1024]{1,0:T(8,128)}, f32[1,1024]{1,0:T(1,128)S(1)}) custom-call(s32[3]{0:T(128)S(1)} %pad_add_fusion.at_ref, bf16[320,1024]{1,0:T(8,128)(2,1)S(1)} %get-tuple-element.55.a_ref.tok_ref, bf16[128,1024]{1,0:T(8,128)(2,1)S(1)} %copy-done.2, ...), custom_call_target="tpu_custom_call" | custom-call | bytes 4096 | tf_op jit(solution)/shard_map/arrange_far/pallas_call | solution.py:98
  46.4 1.8 %grad_other.1 = bf16[512,1024]{1,0:T(8,128)(2,1)S(1)} custom-call(s32[3]{0:T(128)S(1)} %pad_add_fusion.at_ref, bf16[512,1024]{1,0:T(8,128)(2,1)S(1)} %get-tuple-element.82.cot_ref.a_ref.refs_1_.refs_4_.refs_5_, bf16[2048,1024]{1,0:T(8,128)(2,1)S(1)} %permute_0.1.w_ref), custom_call_target="tpu_custom_call" | custom-call | bytes 4096 | tf_op jit(solution)/shard_map/grad_other/pallas_call | solution.py:98
  49.1 1.1 chip_sum.4.refs_2_
  50.3 1.6 collective-permute-start.11
  52.9 1.8 %chip_sum.5.chip_ref = bf16[512,1024]{1,0:T(8,128)(2,1)S(1)} custom-call(s32[3]{0:T(128)S(1)} %pad_add_fusion.at_ref, bf16[512,1024]{1,0:T(8,128)(2,1)S(1)} %get-tuple-element.82.cot_ref.a_ref.refs_1_.refs_4_.refs_5_, bf16[2048,1024]{1,0:T(8,128)(2,1)S(1)} %permute_0.1.w_ref, bf16[512,1024]{1,0:T(8,128)(2,1)S(1)} %collective-permute-done.12.got_ref), custom_call_target="tpu_custom_call" | custom-call | bytes 4096 | tf_op jit(solution)/shard_map/chip_sum/pallas_call | solution.py:98
  54.8 7.1 %collective-permute-done.11.refs_3_ = bf16[192,1024]{1,0:T(8,128)(2,1)S(1)} collective-permute-done((bf16[192,1024]{1,0:T(8,128)(2,1)S(1)}, bf16[192,1024]{1,0:T(8,128)(2,1)S(1)}, u32[]{:S(2)}, u32[]{:S(2)}) %collective-permute-start.11) | collective-permute-done | bytes 393248 | tf_op jit(solution)/shard_map/ppermute | solution.py:62
  61.8 1.8 %act.1.refs_0_ = bf16[512,1024]{1,0:T(8,128)(2,1)S(1)} custom-call(s32[3]{0:T(128)S(1)} %pad_add_fusion.at_ref, bf16[320,1024]{1,0:T(8,128)(2,1)S(1)} %chip_sum.3.refs_0_, bf16[320,1024]{1,0:T(8,128)(2,1)S(1)} %collective-permute-done.10.refs_1_, bf16[192,1024]{1,0:T(8,128)(2,1)S(1)} %chip_sum.4.refs_2_, ...), custom_call_target="tpu_custom_call" | custom-call | bytes 4096 | tf_op jit(solution)/shard_map/act/pallas_call | solution.py:98
  63.8 1.6 collective-permute-start.14
  65.4 1.3 depth.8
  66.7 1.7 %collective-permute-start.15 = (bf16[512,1024]{1,0:T(8,128)(2,1)S(1)}, bf16[512,1024]{1,0:T(8,128)(2,1)S(1)}, u32[]{:S(2)}, u32[]{:S(2)}) collective-permute-start(bf16[512,1024]{1,0:T(8,128)(2,1)S(1)} %depth.8), channel_id=1, source_target_pairs={{0,2},{64,70},{8,10},{72,78},{16,18},{80,86},{24,26},{88,94},{32,3... | collective-permute-start | bytes 3145736 | tf_op jit(solution)/shard_map/ppermute | solution.py:62
  68.3 1.3 depth.9
  70.2 2.4 %slope.1.slope_ref = f32[512,1024]{1,0:T(8,128)S(1)} custom-call(s32[3]{0:T(128)S(1)} %pad_add_fusion.at_ref, bf16[320,1024]{1,0:T(8,128)(2,1)S(1)} %chip_sum.3.refs_0_, bf16[320,1024]{1,0:T(8,128)(2,1)S(1)} %collective-permute-done.10.refs_1_, bf16[192,1024]{1,0:T(8,128)(2,1)S(1)} %chip_sum.4.refs_2_, ...), custom_call_target="tpu_custom_call" | custom-call | bytes 4096 | tf_op jit(solution)/shard_map/slope/pallas_call | solution.py:98
  73.7 15.7 %collective-permute-done.14.got_ref = bf16[512,1024]{1,0:T(8,128)(2,1)S(1)} collective-permute-done((bf16[512,1024]{1,0:T(8,128)(2,1)S(1)}, bf16[512,1024]{1,0:T(8,128)(2,1)S(1)}, u32[]{:S(2)}, u32[]{:S(2)}) %collective-permute-start.14) | collective-permute-done | bytes 1048608 | tf_op jit(solution)/shard_map/ppermute | solution.py:62
  89.4 1.8 %pre_grad.1.refs_7_.refs_2_.own_ref.refs_1_ = bf16[528,1024]{1,0:T(8,128)(2,1)S(1)} custom-call(s32[3]{0:T(128)S(1)} %pad_add_fusion.at_ref, f32[512,1024]{1,0:T(8,128)S(1)} %slope.1.slope_ref, bf16[512,1024]{1,0:T(8,128)(2,1)S(1)} %chip_sum.5.chip_ref, bf16[512,1024]{1,0:T(8,128)(2,1)S(1)} %collective-permute-done.14.got_ref), custom_call_target="tpu_custom_call" | custom-call | bytes 4096 | tf_op jit(solution)/shard_map/pre_grad/pallas_call | solution.py:98
  91.5 1.3 collective-permute-done.16.refs_5_.refs_6_
  92.8 1.8 %depth.10 = bf16[1024,1024]{1,0:T(8,128)(2,1)S(1)} custom-call(s32[3]{0:T(128)S(1)} %pad_add_fusion.at_ref, bf16[512,1024]{1,0:T(8,128)(2,1)S(1)} %act.1.refs_0_, bf16[512,1024]{1,0:T(8,128)(2,1)S(1)} %get-tuple-element.82.cot_ref.a_ref.refs_1_.refs_4_.refs_5_, bf16[512,1024]{1,0:T(8,128)(2,1)S(1)} %collective-permute-done.15.refs_2_, ...), custom_call_target="tpu_custom_call" | custom-call | bytes 4096 | tf_op jit(solution)/shard_map/depth/pallas_call | solution.py:98
  94.6 3.1 %collective-permute-start.19 = (bf16[1024,1024]{1,0:T(8,128)(2,1)S(1)}, bf16[1024,1024]{1,0:T(8,128)(2,1)S(1)}, u32[]{:S(2)}, u32[]{:S(2)}) collective-permute-start(bf16[1024,1024]{1,0:T(8,128)(2,1)S(1)} %depth.10), channel_id=1, source_target_pairs={{0,6},{64,66},{8,14},{72,74},{16,22},{80,82},{24,30},{88,90},{32,3... | collective-permute-start | bytes 6291464 | tf_op jit(solution)/shard_map/ppermute | solution.py:62
  97.8 1.3 depth.11.refs_6_
  99.1 2.8 %collective-permute-start.20 = (bf16[528,1024]{1,0:T(8,128)(2,1)S(1)}, bf16[528,1024]{1,0:T(8,128)(2,1)S(1)}, u32[]{:S(2)}, u32[]{:S(2)}) collective-permute-start(bf16[528,1024]{1,0:T(8,128)(2,1)S(1)} %depth.11.refs_6_), channel_id=1, source_target_pairs={{0,1},{64,65},{8,9},{72,73},{16,17},{80,81},{24,25},{88,89},{32,33... | collective-permute-start | bytes 3244040 | tf_op jit(solution)/shard_map/ppermute | solution.py:62
  101.9 3.0 %inputs_grad.1 = (f32[512,1024]{1,0:T(8,128)S(1)}, bf16[256,1024]{1,0:T(8,128)(2,1)S(1)}) custom-call(s32[3]{0:T(128)S(1)} %pad_add_fusion.at_ref, bf16[528,1024]{1,0:T(8,128)(2,1)S(1)} %pre_grad.1.refs_7_.refs_2_.own_ref.refs_1_, bf16[528,1024]{1,0:T(8,128)(2,1)S(1)} %collective-permute-done.17.refs_1_.refs_3_.away_ref.refs_4_, ...), custom_call_target="tpu_custom_call" | custom-call | bytes 4096 | tf_op jit(solution)/shard_map/inputs_grad/pallas_call | solution.py:98
  105.0 9.4 %collective-permute-done.18 = bf16[256,1024]{1,0:T(8,128)(2,1)S(1)} collective-permute-done((bf16[256,1024]{1,0:T(8,128)(2,1)S(1)}, bf16[256,1024]{1,0:T(8,128)(2,1)S(1)}, u32[]{:S(2)}, u32[]{:S(2)}) %collective-permute-start.18) | collective-permute-done | bytes 524320 | tf_op jit(solution)/shard_map/ppermute | solution.py:62
  114.5 2.4 %collective-permute-start.21 = (bf16[128,1024]{1,0:T(8,128)(2,1)S(1)}, bf16[128,1024]{1,0:T(8,128)(2,1)S(1)}, u32[]{:S(2)}, u32[]{:S(2)}) collective-permute-start(bf16[128,1024]{1,0:T(8,128)(2,1)S(1)} %add_convert_fusion), channel_id=1, source_target_pairs={{0,56},{64,72},{8,16},{72,64},{16,8},{80,88},{24,32},{88,80},{32,2... | collective-permute-start | bytes 786440 | tf_op jit(solution)/shard_map/ppermute | solution.py:62
  116.9 4.4 %collective-permute-done.21 = bf16[128,1024]{1,0:T(8,128)(2,1)S(1)} collective-permute-done((bf16[128,1024]{1,0:T(8,128)(2,1)S(1)}, bf16[128,1024]{1,0:T(8,128)(2,1)S(1)}, u32[]{:S(2)}, u32[]{:S(2)}) %collective-permute-start.21) | collective-permute-done | bytes 262176 | tf_op jit(solution)/shard_map/ppermute | solution.py:62
  121.2 2.8 %collective-permute-done.20.refs_5_.refs_2_ = bf16[528,1024]{1,0:T(8,128)(2,1)S(1)} collective-permute-done((bf16[528,1024]{1,0:T(8,128)(2,1)S(1)}, bf16[528,1024]{1,0:T(8,128)(2,1)S(1)}, u32[]{:S(2)}, u32[]{:S(2)}) %collective-permute-start.20) | collective-permute-done | bytes 1081376 | tf_op jit(solution)/shard_map/ppermute | solution.py:62
  124.0 1.3 depth.12.refs_4_
  125.3 1.5 collective-permute-start.22
  127.9 2.8 %collective-permute-start.23 = (bf16[256,1024]{1,0:T(8,128)(2,1)S(1)}, bf16[256,1024]{1,0:T(8,128)(2,1)S(1)}, u32[]{:S(2)}, u32[]{:S(2)}) collective-permute-start(bf16[256,1024]{1,0:T(8,128)(2,1)S(1)} %depth.13), channel_id=1, source_target_pairs={{0,1},{64,65},{8,9},{72,73},{16,17},{80,81},{24,25},{88,89},{32,33... | collective-permute-start | bytes 1572872 | tf_op jit(solution)/shard_map/ppermute | solution.py:62
  130.8 2.4 %collective-permute-start.24 = (bf16[64,1024]{1,0:T(8,128)(2,1)S(1)}, bf16[64,1024]{1,0:T(8,128)(2,1)S(1)}, u32[]{:S(2)}, u32[]{:S(2)}) collective-permute-start(bf16[64,1024]{1,0:T(8,128)(2,1)S(1)} %add_convert_fusion.2), channel_id=1, source_target_pairs={{0,24},{64,104},{8,48},{72,96},{16,40},{80,120},{24,0},{88,112},{3... | collective-permute-start | bytes 393224 | tf_op jit(solution)/shard_map/ppermute | solution.py:62
  134.2 5.0 %collective-permute-done.24 = bf16[64,1024]{1,0:T(8,128)(2,1)S(1)} collective-permute-done((bf16[64,1024]{1,0:T(8,128)(2,1)S(1)}, bf16[64,1024]{1,0:T(8,128)(2,1)S(1)}, u32[]{:S(2)}, u32[]{:S(2)}) %collective-permute-start.24) | collective-permute-done | bytes 131104 | tf_op jit(solution)/shard_map/ppermute | solution.py:62
  139.3 4.2 %collective-permute-done.23.got_ref = bf16[256,1024]{1,0:T(8,128)(2,1)S(1)} collective-permute-done((bf16[256,1024]{1,0:T(8,128)(2,1)S(1)}, bf16[256,1024]{1,0:T(8,128)(2,1)S(1)}, u32[]{:S(2)}, u32[]{:S(2)}) %collective-permute-start.23) | collective-permute-done | bytes 524320 | tf_op jit(solution)/shard_map/ppermute | solution.py:62
  145.7 2.8 %collective-permute-start.25 = (bf16[128,1024]{1,0:T(8,128)(2,1)S(1)}, bf16[128,1024]{1,0:T(8,128)(2,1)S(1)}, u32[]{:S(2)}, u32[]{:S(2)}) collective-permute-start(bf16[128,1024]{1,0:T(8,128)(2,1)S(1)} %depth.14), channel_id=1, source_target_pairs={{0,1},{64,65},{8,9},{72,73},{16,17},{80,81},{24,25},{88,89},{32,33... | collective-permute-start | bytes 786440 | tf_op jit(solution)/shard_map/ppermute | solution.py:62
  150.2 1.6 %place_rows.1 = f32[256,1024]{1,0:T(8,128)} custom-call(s32[3]{0:T(128)S(1)} %pad_add_fusion.at_ref, f32[256,1024]{1,0:T(8,128)S(1)} %depth_kept.3.keep_ref, bf16[256,1024]{1,0:T(8,128)(2,1)S(1)} %collective-permute-done.23.got_ref), custom_call_target="tpu_custom_call" | custom-call | bytes 4096 | tf_op jit(solution)/shard_map/place_rows/pallas_call | solution.py:98
  152.6 3.6 %collective-permute-done.25.got_ref = bf16[128,1024]{1,0:T(8,128)(2,1)S(1)} collective-permute-done((bf16[128,1024]{1,0:T(8,128)(2,1)S(1)}, bf16[128,1024]{1,0:T(8,128)(2,1)S(1)}, u32[]{:S(2)}, u32[]{:S(2)}) %collective-permute-start.25) | collective-permute-done | bytes 262176 | tf_op jit(solution)/shard_map/ppermute | solution.py:62
  156.2 1.7 %place_columns.1 = (f32[128,2048]{1,0:T(8,128)}, f32[16,128]{1,0:T(8,128)}, f32[8,128]{1,0:T(8,128)}) custom-call(s32[3]{0:T(128)S(1)} %pad_add_fusion.at_ref, f32[128,1024]{1,0:T(8,128)S(1)} %depth_kept.4.keep_ref, bf16[128,1024]{1,0:T(8,128)(2,1)S(1)} %collective-permute-done.25.got_ref, f32[128,1024]{1,0:T(8,128)S(1)} %depth_kept.5.keep2_ref, ...), custom_call_target="tpu_custom_call" | custom-call | bytes 4096 | tf_op jit(solution)/shard_map/place_columns/pallas_call | solution.py:98
  (47 shorter events, 14.8 us)
Async XLA Ops:
  2.3 16.6 %collective-permute-start.3 = (bf16[128,1024]{1,0:T(8,128)(2,1)}, bf16[128,1024]{1,0:T(8,128)(2,1)S(1)}, u32[]{:S(2)}, u32[]{:S(2)}) collective-permute-start(bf16[128,1024]{1,0:T(8,128)(2,1)} %pack.1.refs_0_), channel_id=1, source_target_pairs={{0,8},{64,72},{8,16},{72,80},{16,24},{80,88},{24,32},{88,96},{32,4... | collective-permute-start | bytes 786440 | tf_op jit(solution)/shard_map/ppermute | solution.py:62
  4.3 14.6 %collective-permute-start.2 = (bf16[128,1024]{1,0:T(8,128)(2,1)}, bf16[128,1024]{1,0:T(8,128)(2,1)S(1)}, u32[]{:S(2)}, u32[]{:S(2)}) collective-permute-start(bf16[128,1024]{1,0:T(8,128)(2,1)} %pack.1.refs_0_), channel_id=1, source_target_pairs={{0,56},{64,120},{8,0},{72,64},{16,8},{80,72},{24,16},{88,80},{32,2... | collective-permute-start | bytes 786440 | tf_op jit(solution)/shard_map/ppermute | solution.py:62
  4.4 21.1 %collective-permute-start.1 = (bf16[128,1024]{1,0:T(8,128)(2,1)}, bf16[128,1024]{1,0:T(8,128)(2,1)S(1)}, u32[]{:S(2)}, u32[]{:S(2)}) collective-permute-start(bf16[128,1024]{1,0:T(8,128)(2,1)} %pack.1.refs_0_), channel_id=1, source_target_pairs={{0,16},{64,80},{8,24},{72,88},{16,32},{80,96},{24,40},{88,104},{32... | collective-permute-start | bytes 786440 | tf_op jit(solution)/shard_map/ppermute | solution.py:62
  8.8 16.8 %collective-permute-start = (bf16[128,1024]{1,0:T(8,128)(2,1)}, bf16[128,1024]{1,0:T(8,128)(2,1)S(1)}, u32[]{:S(2)}, u32[]{:S(2)}) collective-permute-start(bf16[128,1024]{1,0:T(8,128)(2,1)} %pack.1.refs_0_), channel_id=1, source_target_pairs={{0,48},{64,112},{8,56},{72,120},{16,0},{80,64},{24,8},{88,72},{32,... | collective-permute-start | bytes 786440 | tf_op jit(solution)/shard_map/ppermute | solution.py:62
  11.2 2.2 %copy-start = (bf16[2048,1024]{1,0:T(8,128)(2,1)S(1)}, bf16[2048,1024]{1,0:T(8,128)(2,1)}, u32[]{:S(2)}) copy-start(bf16[2048,1024]{1,0:T(8,128)(2,1)} %a_ref.5) | copy-start | bytes 12582916
  13.4 2.2 %copy-start.1 = (bf16[1024,2048]{1,0:T(8,128)(2,1)S(1)}, bf16[1024,2048]{1,0:T(8,128)(2,1)}, u32[]{:S(2)}) copy-start(bf16[1024,2048]{1,0:T(8,128)(2,1)} %a_ref.4) | copy-start | bytes 12582916
  15.6 10.0 %copy-start.2 = (bf16[128,1024]{1,0:T(8,128)(2,1)S(1)}, bf16[128,1024]{1,0:T(8,128)(2,1)}, u32[]{:S(2)}) copy-start(bf16[128,1024]{1,0:T(8,128)(2,1)} %pack.1.refs_0_) | copy-start | bytes 786436
  27.0 3.9 %collective-permute-start.4 = (bf16[320,1024]{1,0:T(8,128)(2,1)S(1)}, bf16[320,1024]{1,0:T(8,128)(2,1)S(1)}, u32[]{:S(2)}, u32[]{:S(2)}) collective-permute-start(bf16[320,1024]{1,0:T(8,128)(2,1)S(1)} %get-tuple-element.56), channel_id=1, source_target_pairs={{0,64},{64,0},{8,72},{72,8},{16,80},{80,16},{24,88},{88,24},{32,96... | collective-permute-start | bytes 1966088 | tf_op jit(solution)/shard_map/ppermute | solution.py:62
  27.1 17.5 %collective-permute-start.5 = (bf16[128,1024]{1,0:T(8,128)(2,1)S(1)}, bf16[128,1024]{1,0:T(8,128)(2,1)S(1)}, u32[]{:S(2)}, u32[]{:S(2)}) collective-permute-start(bf16[128,1024]{1,0:T(8,128)(2,1)S(1)} %collective-permute-done.refs_2_), channel_id=1, source_target_pairs={{0,56},{64,120},{8,0},{72,64},{16,8},{80,72},{24,16},{88,80},{32,2... | collective-permute-start | bytes 786440 | tf_op jit(solution)/shard_map/ppermute | solution.py:62
  27.1 17.4 %collective-permute-start.6 = (bf16[128,1024]{1,0:T(8,128)(2,1)S(1)}, bf16[128,1024]{1,0:T(8,128)(2,1)S(1)}, u32[]{:S(2)}, u32[]{:S(2)}) collective-permute-start(bf16[128,1024]{1,0:T(8,128)(2,1)S(1)} %collective-permute-done.1.refs_3_), channel_id=1, source_target_pairs={{0,8},{64,72},{8,16},{72,80},{16,24},{80,88},{24,32},{88,96},{32,4... | collective-permute-start | bytes 786440 | tf_op jit(solution)/shard_map/ppermute | solution.py:62
  32.3 16.8 %collective-permute-start.10 = (bf16[320,1024]{1,0:T(8,128)(2,1)S(1)}, bf16[320,1024]{1,0:T(8,128)(2,1)S(1)}, u32[]{:S(2)}, u32[]{:S(2)}) collective-permute-start(bf16[320,1024]{1,0:T(8,128)(2,1)S(1)} %chip_sum.3.refs_0_), channel_id=1, source_target_pairs={{0,128},{64,192},{8,136},{72,200},{16,144},{80,208},{24,152},{88,2... | collective-permute-start | bytes 1966088 | tf_op jit(solution)/shard_map/ppermute | solution.py:62
  33.9 10.6 %collective-permute-start.8 = (bf16[64,1024]{1,0:T(8,128)(2,1)S(1)}, bf16[64,1024]{1,0:T(8,128)(2,1)S(1)}, u32[]{:S(2)}, u32[]{:S(2)}) collective-permute-start(bf16[64,1024]{1,0:T(8,128)(2,1)S(1)} %slice.31), channel_id=1, source_target_pairs={{0,16},{64,80},{8,24},{72,88},{16,32},{80,96},{24,40},{88,104},{32... | collective-permute-start | bytes 393224 | tf_op jit(solution)/shard_map/ppermute | solution.py:62
  35.3 9.2 %collective-permute-start.7 = (bf16[64,1024]{1,0:T(8,128)(2,1)S(1)}, bf16[64,1024]{1,0:T(8,128)(2,1)S(1)}, u32[]{:S(2)}, u32[]{:S(2)}) collective-permute-start(bf16[64,1024]{1,0:T(8,128)(2,1)S(1)} %slice.30), channel_id=1, source_target_pairs={{0,48},{64,112},{8,56},{72,120},{16,0},{80,64},{24,8},{88,72},{32,... | collective-permute-start | bytes 393224 | tf_op jit(solution)/shard_map/ppermute | solution.py:62
  46.4 1.8 %collective-permute-start.9 = (bf16[192,1024]{1,0:T(8,128)(2,1)S(1)}, bf16[192,1024]{1,0:T(8,128)(2,1)S(1)}, u32[]{:S(2)}, u32[]{:S(2)}) collective-permute-start(bf16[192,1024]{1,0:T(8,128)(2,1)S(1)} %get-tuple-element.57), channel_id=1, source_target_pairs={{0,64},{64,0},{8,72},{72,8},{16,80},{80,16},{24,88},{88,24},{32,96... | collective-permute-start | bytes 1179656 | tf_op jit(solution)/shard_map/ppermute | solution.py:62
  50.2 2.7 %collective-permute-start.12 = (bf16[512,1024]{1,0:T(8,128)(2,1)S(1)}, bf16[512,1024]{1,0:T(8,128)(2,1)S(1)}, u32[]{:S(2)}, u32[]{:S(2)}) collective-permute-start(bf16[512,1024]{1,0:T(8,128)(2,1)S(1)} %grad_other.1), channel_id=1, source_target_pairs={{0,64},{64,0},{8,72},{72,8},{16,80},{80,16},{24,88},{88,24},{32,96... | collective-permute-start | bytes 3145736 | tf_op jit(solution)/shard_map/ppermute | solution.py:62
  50.3 11.5 %collective-permute-start.11 = (bf16[192,1024]{1,0:T(8,128)(2,1)S(1)}, bf16[192,1024]{1,0:T(8,128)(2,1)S(1)}, u32[]{:S(2)}, u32[]{:S(2)}) collective-permute-start(bf16[192,1024]{1,0:T(8,128)(2,1)S(1)} %chip_sum.4.refs_2_), channel_id=1, source_target_pairs={{0,128},{64,192},{8,136},{72,200},{16,144},{80,208},{24,152},{88,2... | collective-permute-start | bytes 1179656 | tf_op jit(solution)/shard_map/ppermute | solution.py:62
  63.7 4.7 %collective-permute-start.13 = (bf16[512,1024]{1,0:T(8,128)(2,1)S(1)}, bf16[512,1024]{1,0:T(8,128)(2,1)S(1)}, u32[]{:S(2)}, u32[]{:S(2)}) collective-permute-start(bf16[512,1024]{1,0:T(8,128)(2,1)S(1)} %act.1.refs_0_), channel_id=1, source_target_pairs={{0,64},{64,0},{8,72},{72,8},{16,80},{80,16},{24,88},{88,24},{32,96... | collective-permute-start | bytes 3145736 | tf_op jit(solution)/shard_map/ppermute | solution.py:62
  63.8 25.6 %collective-permute-start.14 = (bf16[512,1024]{1,0:T(8,128)(2,1)S(1)}, bf16[512,1024]{1,0:T(8,128)(2,1)S(1)}, u32[]{:S(2)}, u32[]{:S(2)}) collective-permute-start(bf16[512,1024]{1,0:T(8,128)(2,1)S(1)} %chip_sum.5.chip_ref), channel_id=1, source_target_pairs={{0,128},{64,192},{8,136},{72,200},{16,144},{80,208},{24,152},{88,2... | collective-permute-start | bytes 3145736 | tf_op jit(solution)/shard_map/ppermute | solution.py:62
  66.7 24.8 %collective-permute-start.15 = (bf16[512,1024]{1,0:T(8,128)(2,1)S(1)}, bf16[512,1024]{1,0:T(8,128)(2,1)S(1)}, u32[]{:S(2)}, u32[]{:S(2)}) collective-permute-start(bf16[512,1024]{1,0:T(8,128)(2,1)S(1)} %depth.8), channel_id=1, source_target_pairs={{0,2},{64,70},{8,10},{72,78},{16,18},{80,86},{24,26},{88,94},{32,3... | collective-permute-start | bytes 3145736 | tf_op jit(solution)/shard_map/ppermute | solution.py:62
  69.7 23.1 %collective-permute-start.16 = (bf16[512,1024]{1,0:T(8,128)(2,1)S(1)}, bf16[512,1024]{1,0:T(8,128)(2,1)S(1)}, u32[]{:S(2)}, u32[]{:S(2)}) collective-permute-start(bf16[512,1024]{1,0:T(8,128)(2,1)S(1)} %depth.9), channel_id=1, source_target_pairs={{0,2},{64,70},{8,10},{72,78},{16,18},{80,86},{24,26},{88,94},{32,3... | collective-permute-start | bytes 3145736 | tf_op jit(solution)/shard_map/ppermute | solution.py:62
  91.2 6.6 %collective-permute-start.17 = (bf16[528,1024]{1,0:T(8,128)(2,1)S(1)}, bf16[528,1024]{1,0:T(8,128)(2,1)S(1)}, u32[]{:S(2)}, u32[]{:S(2)}) collective-permute-start(bf16[528,1024]{1,0:T(8,128)(2,1)S(1)} %pre_grad.1.refs_7_.refs_2_.own_ref.refs_1_), channel_id=1, source_target_pairs={{0,64},{64,0},{8,72},{72,8},{16,80},{80,16},{24,88},{88,24},{32,96... | collective-permute-start | bytes 3244040 | tf_op jit(solution)/shard_map/ppermute | solution.py:62
  94.6 29.4 %collective-permute-start.19 = (bf16[1024,1024]{1,0:T(8,128)(2,1)S(1)}, bf16[1024,1024]{1,0:T(8,128)(2,1)S(1)}, u32[]{:S(2)}, u32[]{:S(2)}) collective-permute-start(bf16[1024,1024]{1,0:T(8,128)(2,1)S(1)} %depth.10), channel_id=1, source_target_pairs={{0,6},{64,66},{8,14},{72,74},{16,22},{80,82},{24,30},{88,90},{32,3... | collective-permute-start | bytes 6291464 | tf_op jit(solution)/shard_map/ppermute | solution.py:62
  99.1 24.9 %collective-permute-start.20 = (bf16[528,1024]{1,0:T(8,128)(2,1)S(1)}, bf16[528,1024]{1,0:T(8,128)(2,1)S(1)}, u32[]{:S(2)}, u32[]{:S(2)}) collective-permute-start(bf16[528,1024]{1,0:T(8,128)(2,1)S(1)} %depth.11.refs_6_), channel_id=1, source_target_pairs={{0,1},{64,65},{8,9},{72,73},{16,17},{80,81},{24,25},{88,89},{32,33... | collective-permute-start | bytes 3244040 | tf_op jit(solution)/shard_map/ppermute | solution.py:62
  104.9 9.5 %collective-permute-start.18 = (bf16[256,1024]{1,0:T(8,128)(2,1)S(1)}, bf16[256,1024]{1,0:T(8,128)(2,1)S(1)}, u32[]{:S(2)}, u32[]{:S(2)}) collective-permute-start(bf16[256,1024]{1,0:T(8,128)(2,1)S(1)} %get-tuple-element.78), channel_id=1, source_target_pairs={{0,8},{64,120},{8,0},{72,80},{16,24},{80,72},{24,16},{88,96},{32,4... | collective-permute-start | bytes 1572872 | tf_op jit(solution)/shard_map/ppermute | solution.py:62
  114.5 6.7 %collective-permute-start.21 = (bf16[128,1024]{1,0:T(8,128)(2,1)S(1)}, bf16[128,1024]{1,0:T(8,128)(2,1)S(1)}, u32[]{:S(2)}, u32[]{:S(2)}) collective-permute-start(bf16[128,1024]{1,0:T(8,128)(2,1)S(1)} %add_convert_fusion), channel_id=1, source_target_pairs={{0,56},{64,72},{8,16},{72,64},{16,8},{80,88},{24,32},{88,80},{32,2... | collective-permute-start | bytes 786440 | tf_op jit(solution)/shard_map/ppermute | solution.py:62
  125.3 18.2 %collective-permute-start.22 = (bf16[528,1024]{1,0:T(8,128)(2,1)S(1)}, bf16[528,1024]{1,0:T(8,128)(2,1)S(1)}, u32[]{:S(2)}, u32[]{:S(2)}) collective-permute-start(bf16[528,1024]{1,0:T(8,128)(2,1)S(1)} %depth.12.refs_4_), channel_id=1, source_target_pairs={{0,2},{64,70},{8,10},{72,78},{16,18},{80,86},{24,26},{88,94},{32,3... | collective-permute-start | bytes 3244040 | tf_op jit(solution)/shard_map/ppermute | solution.py:62
  127.9 15.5 %collective-permute-start.23 = (bf16[256,1024]{1,0:T(8,128)(2,1)S(1)}, bf16[256,1024]{1,0:T(8,128)(2,1)S(1)}, u32[]{:S(2)}, u32[]{:S(2)}) collective-permute-start(bf16[256,1024]{1,0:T(8,128)(2,1)S(1)} %depth.13), channel_id=1, source_target_pairs={{0,1},{64,65},{8,9},{72,73},{16,17},{80,81},{24,25},{88,89},{32,33... | collective-permute-start | bytes 1572872 | tf_op jit(solution)/shard_map/ppermute | solution.py:62
  130.8 8.5 %collective-permute-start.24 = (bf16[64,1024]{1,0:T(8,128)(2,1)S(1)}, bf16[64,1024]{1,0:T(8,128)(2,1)S(1)}, u32[]{:S(2)}, u32[]{:S(2)}) collective-permute-start(bf16[64,1024]{1,0:T(8,128)(2,1)S(1)} %add_convert_fusion.2), channel_id=1, source_target_pairs={{0,24},{64,104},{8,48},{72,96},{16,40},{80,120},{24,0},{88,112},{3... | collective-permute-start | bytes 393224 | tf_op jit(solution)/shard_map/ppermute | solution.py:62
  144.4 11.8 %collective-permute-start.26 = (bf16[160,1024]{1,0:T(8,128)(2,1)S(1)}, bf16[160,1024]{1,0:T(8,128)(2,1)S(1)}, u32[]{:S(2)}, u32[]{:S(2)}) collective-permute-start(bf16[160,1024]{1,0:T(8,128)(2,1)S(1)} %depth.15.sent_ref), channel_id=1, source_target_pairs={{0,6},{64,66},{8,14},{72,74},{16,22},{80,82},{24,30},{88,90},{32,3... | collective-permute-start | bytes 983048 | tf_op jit(solution)/shard_map/ppermute | solution.py:62
  145.7 10.5 %collective-permute-start.25 = (bf16[128,1024]{1,0:T(8,128)(2,1)S(1)}, bf16[128,1024]{1,0:T(8,128)(2,1)S(1)}, u32[]{:S(2)}, u32[]{:S(2)}) collective-permute-start(bf16[128,1024]{1,0:T(8,128)(2,1)S(1)} %depth.14), channel_id=1, source_target_pairs={{0,1},{64,65},{8,9},{72,73},{16,17},{80,81},{24,25},{88,89},{32,33... | collective-permute-start | bytes 786440 | tf_op jit(solution)/shard_map/ppermute | solution.py:62
